TPU v7x, 32 devices: a whole 2x2x4 slice. The times are simulated.
32 devices in a mesh: blk: 4 (over y, x), head: 8 (over z, core).
Axes of the slice: x: 2, y: 2, z: 4, core: 2. Of those that a mesh axis runs over, the one named last changes fastest.
Arguments:
- tokens: bfloat16 [4, 1024, 2048], P('blk', 'head'), may hold values from -6 to 6
- lengths: int32 [1], replicated, may hold values from 1024 to 4096, as said below
- query_weight: bfloat16 [2048, 2048], P(('blk', 'head')), may hold values from -0.125 to 0.125
- key_weight: bfloat16 [2048, 2048], P(('blk', 'head')), may hold values from -0.125 to 0.125
- value_weight: bfloat16 [2048, 2048], P(('blk', 'head')), may hold values from -0.125 to 0.125
- output_weight: bfloat16 [2048, 2048], P(('blk', 'head')), may hold values from -4 to 4
- gate_weight: bfloat16 [2048, 8192], P(('blk', 'head')), may hold values from -0.125 to 0.125
- up_weight: bfloat16 [2048, 8192], P(('blk', 'head')), may hold values from -0.125 to 0.125
- down_weight: bfloat16 [8192, 2048], P(('blk', 'head')), may hold values from -0.0625 to 0.0625
- cotangent: bfloat16 [4, 1024, 2048], P('blk', 'head'), may hold values from -6 to 6
Outputs:
- layer_output: bfloat16 [4, 1024, 2048], P('blk', 'head')
- tokens_grad: bfloat16 [4, 1024, 2048], P('blk', 'head')
- query_grad: float32 [2048, 2048], P(('blk', 'head'))
- key_grad: float32 [2048, 2048], P(('blk', 'head'))
- value_grad: float32 [2048, 2048], P(('blk', 'head'))
- output_grad: float32 [2048, 2048], P(('blk', 'head'))
- gate_grad: float32 [2048, 8192], P(('blk', 'head'))
- up_grad: float32 [2048, 8192], P(('blk', 'head'))
- down_grad: float32 [8192, 2048], P(('blk', 'head'))
Inputs may be any that keep to these rules, and one draw needn't show every extreme that they name: Each slot holds valid tokens at its first lengths positions; in every draw some slot is full.
All inputs are finite; a program needn't handle non-finite values.
Results may differ from a plain program's by a relative error of at most 0.018.
Values may be sent and summed in bfloat16 or wider, within the bound.
No kernel may reach another device: no remote copies, remote signals or barrier semaphores. Data moves between devices by JAX's collectives and lax.ppermute only.
A program may use at most 640 MiB of HBM per device.

v0:
```python
import math

import jax
import jax.numpy as jnp
from jax import lax
from jax.sharding import PartitionSpec as P

HEADS = 16
HDIM = 128
SEQ = 4096


EPSILON = 1e-05
NEGATIVE = -1e30


def from_behind(value, axis, by):
    peers = lax.axis_size(axis)
    pairs = [(i, i + by) for i in range(peers) if 0 <= i + by < peers]
    return lax.ppermute(value, axis, pairs)


def shifted(value, axis, by):
    peers = lax.axis_size(axis)
    return lax.ppermute(value, axis, [(i, (i + by) % peers) for i in range(peers)])


def normalize_rows(values):
    centered = values - jnp.mean(values, axis=-1, keepdims=True)
    variance = jnp.mean(centered * centered, axis=-1, keepdims=True)
    inverse = lax.rsqrt(variance + EPSILON)
    return (centered * inverse, inverse)


def normalize_back(normed, inverse, upstream):
    mean_grad = jnp.mean(upstream, axis=-1, keepdims=True)
    mean_proj = jnp.mean(upstream * normed, axis=-1, keepdims=True)
    return inverse * (upstream - mean_grad - normed * mean_proj)


def rotary_tables(positions, head_dim):
    half_dim = head_dim // 2
    frequency = jnp.exp(
        jnp.arange(half_dim).astype(jnp.float32) * (-2.0 * math.log(10000.0) / head_dim)
    )
    angles = positions.astype(jnp.float32)[:, None] * frequency[None, :]
    return (jnp.cos(angles)[None, :, None, :], jnp.sin(angles)[None, :, None, :])


def rotate(values, cosine_table, sine_table):
    half_dim = values.shape[-1] // 2
    first_half = values[..., :half_dim]
    second_half = values[..., half_dim:]
    return jnp.concatenate(
        [
            first_half * cosine_table - second_half * sine_table,
            second_half * cosine_table + first_half * sine_table,
        ],
        axis=-1,
    )


def dot_transposed(left, right):
    return lax.dot_general(
        left, right, (((1,), (1,)), ((), ())), preferred_element_type=jnp.float32
    )


def outer_sum(left, right):
    return lax.dot_general(
        left, right, (((0,), (0,)), ((), ())), preferred_element_type=jnp.float32
    )


def block_visible(query_pos, key_pos, slot_lengths):
    causal = key_pos[None, :] <= query_pos[:, None]
    live_keys = key_pos[None, :] < slot_lengths[:, None]
    return causal[None, None, :, :] & live_keys[:, None, None, :]


def local(
    tokens,
    lengths,
    query_weight,
    key_weight,
    value_weight,
    output_weight,
    gate_weight,
    up_weight,
    down_weight,
    cotangent,
):
    loop_size = lax.axis_size("blk")
    head_size = lax.axis_size("head")
    loop_index = lax.axis_index("blk")
    head_index = lax.axis_index("head")
    inputs = tokens[0].astype(jnp.float32)
    token_count = inputs.shape[0]
    model_width = inputs.shape[1]
    hidden_width = gate_weight.shape[1]
    local_heads = HEADS // head_size
    block_rows = SEQ // loop_size
    group_rows = token_count * head_size
    slot_count = group_rows // block_rows
    score_scale = 1.0 / math.sqrt(HDIM)
    slot_ids = jnp.arange(slot_count)
    row_ids = head_index * token_count + jnp.arange(token_count)
    my_slot = row_ids // block_rows
    my_pos = loop_index * block_rows + row_ids % block_rows
    my_length = jnp.sum(
        jnp.where(my_slot[:, None] == slot_ids[None, :], lengths[None, :], 0), axis=1
    )
    valid_rows = (my_pos < my_length).astype(jnp.float32)[:, None]
    normed_one, inverse_one = normalize_rows(inputs)
    normed_low = normed_one.astype(jnp.bfloat16)
    pieces = (
        lax.all_gather(query_weight, ("blk", "head"), axis=0, tiled=True),
        lax.all_gather(key_weight, ("blk", "head"), axis=0, tiled=True),
        lax.all_gather(value_weight, ("blk", "head"), axis=0, tiled=True),
        lax.all_gather(output_weight, ("blk", "head"), axis=0, tiled=True),
    )
    columns = normed_low
    new_sums = tuple(
        (
            jnp.dot(columns, pieces[number], preferred_element_type=jnp.float32)
            for number in range(3)
        )
    )
    placed = pieces[3]
    query_lin, key_lin, value_lin, output_full = new_sums + (placed,)

    def heads_layout(values):
        return values.astype(jnp.bfloat16).reshape(token_count, HEADS, HDIM)

    def slot_layout(values):
        return values.reshape(slot_count, block_rows, local_heads, HDIM)

    query_heads, key_heads, value_heads = (
        lax.all_to_all(heads_layout(query_lin), "head", split_axis=1, concat_axis=0, tiled=True),
        lax.all_to_all(heads_layout(key_lin), "head", split_axis=1, concat_axis=0, tiled=True),
        lax.all_to_all(heads_layout(value_lin), "head", split_axis=1, concat_axis=0, tiled=True),
    )
    own_pos = loop_index * block_rows + jnp.arange(block_rows)
    cosine_table, sine_table = rotary_tables(own_pos, HDIM)
    query_rot = rotate(
        slot_layout(query_heads).astype(jnp.float32), cosine_table, sine_table
    ).astype(jnp.bfloat16)
    key_rot = rotate(slot_layout(key_heads).astype(jnp.float32), cosine_table, sine_table).astype(
        jnp.bfloat16
    )
    value_own = slot_layout(value_heads)

    def block_scores(query_part, key_part, source, length_part):
        key_pos = source * block_rows + jnp.arange(block_rows)
        raw_scores = (
            jnp.einsum("aqhd,akhd->ahqk", query_part, key_part, preferred_element_type=jnp.float32)
            * score_scale
        )
        return jnp.where(block_visible(own_pos, key_pos, length_part), raw_scores, NEGATIVE)

    def forward_block(softmax_state, query_part, key_part, value_part, source, length_part):
        peak_old, total_old, accum_old = softmax_state
        scores = block_scores(query_part, key_part, source, length_part)
        peak_new = jnp.maximum(peak_old, jnp.max(scores, axis=-1))
        shrink = jnp.exp(peak_old - peak_new)
        weights = jnp.exp(scores - peak_new[..., None])
        total_new = total_old * shrink + jnp.sum(weights, axis=-1)
        mixed_block = jnp.einsum(
            "ahqk,akhd->aqhd",
            weights.astype(jnp.bfloat16),
            value_part,
            preferred_element_type=jnp.float32,
        )
        accum_new = accum_old * jnp.transpose(shrink, (0, 2, 1))[..., None] + mixed_block
        return (peak_new, total_new, accum_new)

    def forward_step(softmax_state, key_block, value_block, source):
        return forward_block(softmax_state, query_rot, key_block, value_block, source, lengths)

    row_shape = (slot_count, local_heads, block_rows)
    block_shape = (slot_count, block_rows, local_heads, HDIM)
    softmax_state = (
        jnp.full(row_shape, NEGATIVE, jnp.float32),
        jnp.zeros(row_shape, jnp.float32),
        jnp.zeros(block_shape, jnp.float32),
    )
    key_block = key_rot
    value_block = value_own
    kept_blocks = []
    for loop_step in range(loop_size):
        source = (loop_index - loop_step) % loop_size
        kept_blocks.append((key_block, value_block))
        softmax_state = lax.cond(
            loop_step <= loop_index,
            lambda current: forward_step(current, key_block, value_block, source),
            lambda current: current,
            softmax_state,
        )
        if loop_step + 1 < loop_size:
            key_block, value_block = from_behind((key_block, value_block), "blk", 1)
    peak_final, total_final, accum_final = softmax_state
    has_total = total_final > 0.0
    safe_total = jnp.where(has_total, total_final, 1.0)
    attended = jnp.where(
        jnp.transpose(has_total, (0, 2, 1))[..., None],
        accum_final / jnp.transpose(safe_total, (0, 2, 1))[..., None],
        0.0,
    )
    log_total = peak_final + jnp.log(safe_total)
    joined_heads = lax.all_to_all(
        attended.astype(jnp.bfloat16).reshape(group_rows, local_heads, HDIM),
        "head",
        split_axis=0,
        concat_axis=1,
        tiled=True,
    )
    joined_low = joined_heads.reshape(token_count, model_width)
    residual = inputs + jnp.dot(joined_low, output_full, preferred_element_type=jnp.float32)
    normed_two, inverse_two = normalize_rows(residual)
    normed_two_low = normed_two.astype(jnp.bfloat16)
    pieces = (
        lax.all_gather(gate_weight, ("blk", "head"), axis=0, tiled=True),
        lax.all_gather(up_weight, ("blk", "head"), axis=0, tiled=True),
    )
    columns = normed_two_low
    gate_act = jnp.dot(columns, pieces[0], preferred_element_type=jnp.float32)
    up_act = jnp.dot(columns, pieces[1], preferred_element_type=jnp.float32)
    sigmoid_gate = jax.nn.sigmoid(gate_act)
    silu_gate = gate_act * sigmoid_gate
    product_low = (silu_gate * up_act).astype(jnp.bfloat16)
    columns = product_low
    down_act = jnp.dot(
        columns,
        lax.all_gather(down_weight, ("blk", "head"), axis=0, tiled=True),
        preferred_element_type=jnp.float32,
    )
    layer_output = ((residual + down_act) * valid_rows).astype(jnp.bfloat16)[None]
    upstream = cotangent[0].astype(jnp.float32) * valid_rows
    upstream_low = upstream.astype(jnp.bfloat16)
    product_grad = dot_transposed(
        upstream_low, lax.all_gather(down_weight, ("blk", "head"), axis=0, tiled=True)
    )
    gate_grad_act = (
        product_grad * up_act * sigmoid_gate * (1.0 + gate_act * (1.0 - sigmoid_gate))
    ).astype(jnp.bfloat16)
    up_grad_act = (product_grad * silu_gate).astype(jnp.bfloat16)
    pieces = lax.all_gather((gate_weight, up_weight), ("blk", "head"), axis=0, tiled=True)
    normed_two_grad = dot_transposed(gate_grad_act, pieces[0]) + dot_transposed(
        up_grad_act, pieces[1]
    )
    residual_grad = upstream + normalize_back(normed_two, inverse_two, normed_two_grad)
    residual_low = residual_grad.astype(jnp.bfloat16)
    joined_grad = dot_transposed(residual_low, output_full).astype(jnp.bfloat16)
    attended_grad = slot_layout(
        lax.all_to_all(
            joined_grad.reshape(token_count, HEADS, HDIM),
            "head",
            split_axis=1,
            concat_axis=0,
            tiled=True,
        )
    )
    row_delta = jnp.transpose(
        jnp.sum(attended_grad.astype(jnp.float32) * attended, axis=-1), (0, 2, 1)
    )

    def backward_block(
        grad_state,
        query_part,
        key_part,
        value_part,
        grad_part,
        delta_part,
        total_part,
        source,
        length_part,
    ):
        query_acc, key_acc, value_acc = grad_state
        scores = block_scores(query_part, key_part, source, length_part)
        probabilities = jnp.exp(scores - total_part[..., None])
        value_acc = value_acc + jnp.einsum(
            "ahqk,aqhd->akhd",
            probabilities.astype(jnp.bfloat16),
            grad_part,
            preferred_element_type=jnp.float32,
        )
        prob_grad = jnp.einsum(
            "aqhd,akhd->ahqk", grad_part, value_part, preferred_element_type=jnp.float32
        )
        score_grad = (probabilities * (prob_grad - delta_part[..., None])).astype(jnp.bfloat16)
        query_acc = (
            query_acc
            + jnp.einsum(
                "ahqk,akhd->aqhd", score_grad, key_part, preferred_element_type=jnp.float32
            )
            * score_scale
        )
        key_acc = (
            key_acc
            + jnp.einsum(
                "ahqk,aqhd->akhd", score_grad, query_part, preferred_element_type=jnp.float32
            )
            * score_scale
        )
        return (query_acc, key_acc, value_acc)

    def backward_step(grad_state, key_block, value_block, source):
        return backward_block(
            grad_state,
            query_rot,
            key_block,
            value_block,
            attended_grad,
            row_delta,
            log_total,
            source,
            lengths,
        )

    query_acc = jnp.zeros(block_shape, jnp.float32)
    key_acc = jnp.zeros(block_shape, jnp.float32)
    value_acc = jnp.zeros(block_shape, jnp.float32)
    key_block = key_rot
    value_block = value_own
    for loop_step in range(loop_size):
        source = (loop_index - loop_step) % loop_size
        if loop_step > 0:
            key_block, value_block = from_behind((key_block, value_block), "blk", 1)
        query_acc, key_acc, value_acc = lax.cond(
            loop_step <= loop_index,
            lambda current: backward_step(current, key_block, value_block, source),
            lambda current: current,
            (query_acc, key_acc, value_acc),
        )
        key_acc, value_acc = (
            shifted(key_acc.astype(jnp.bfloat16), "blk", 1).astype(key_acc.dtype),
            shifted(value_acc.astype(jnp.bfloat16), "blk", 1).astype(value_acc.dtype),
        )
    query_grad_low = rotate(query_acc, cosine_table, -sine_table).astype(jnp.bfloat16)
    key_grad_low = rotate(key_acc, cosine_table, -sine_table).astype(jnp.bfloat16)
    value_grad_low = value_acc.astype(jnp.bfloat16)

    def tokens_layout(values):
        return values.reshape(group_rows, local_heads, HDIM)

    query_back, key_back, value_back = (
        lax.all_to_all(
            tokens_layout(query_grad_low), "head", split_axis=0, concat_axis=1, tiled=True
        ),
        lax.all_to_all(
            tokens_layout(key_grad_low), "head", split_axis=0, concat_axis=1, tiled=True
        ),
        lax.all_to_all(
            tokens_layout(value_grad_low), "head", split_axis=0, concat_axis=1, tiled=True
        ),
    )
    query_back = query_back.reshape(token_count, model_width)
    key_back = key_back.reshape(token_count, model_width)
    value_back = value_back.reshape(token_count, model_width)
    pieces = lax.all_gather(
        (query_weight, key_weight, value_weight), ("blk", "head"), axis=0, tiled=True
    )
    normed_one_grad = (
        dot_transposed(query_back, pieces[0])
        + dot_transposed(key_back, pieces[1])
        + dot_transposed(value_back, pieces[2])
    )
    tokens_grad = (residual_grad + normalize_back(normed_one, inverse_one, normed_one_grad)).astype(
        jnp.bfloat16
    )[None]
    width_ratio = hidden_width // model_width
    shard_rows = model_width // (loop_size * head_size)
    down_term = outer_sum(product_low, upstream_low).reshape(
        shard_rows * lax.axis_size(("blk", "head")), width_ratio * model_width
    )
    summed = lax.psum_scatter(
        jnp.concatenate(
            [
                outer_sum(normed_low, query_back),
                outer_sum(normed_low, key_back),
                outer_sum(normed_low, value_back),
                outer_sum(joined_low, residual_low),
                outer_sum(normed_two_low, gate_grad_act),
                outer_sum(normed_two_low, up_grad_act),
                down_term,
            ],
            axis=1,
        ),
        ("blk", "head"),
        scatter_dimension=0,
        tiled=True,
    )
    gate_start = 4 * model_width
    up_start = gate_start + hidden_width
    down_start = up_start + hidden_width
    return (
        layer_output,
        tokens_grad,
        summed[:, :model_width],
        summed[:, model_width : 2 * model_width],
        summed[:, 2 * model_width : 3 * model_width],
        summed[:, 3 * model_width : gate_start],
        summed[:, gate_start:up_start],
        summed[:, up_start:down_start],
        summed[:, down_start:].reshape(shard_rows * width_ratio, model_width),
    )


def solution(mesh):
    in_specs = (
        P("blk", "head", None),
        P(),
        P(("blk", "head"), None),
        P(("blk", "head"), None),
        P(("blk", "head"), None),
        P(("blk", "head"), None),
        P(("blk", "head"), None),
        P(("blk", "head"), None),
        P(("blk", "head"), None),
        P("blk", "head", None),
    )
    out_specs = (
        P("blk", "head", None),
        P("blk", "head", None),
        P(("blk", "head"), None),
        P(("blk", "head"), None),
        P(("blk", "head"), None),
        P(("blk", "head"), None),
        P(("blk", "head"), None),
        P(("blk", "head"), None),
        P(("blk", "head"), None),
    )
    return jax.shard_map(local, mesh=mesh, in_specs=in_specs, out_specs=out_specs, check_vma=False)
```

profile of v0, /device:TPU:5, one launch (start us, length us, event | category | flops | bytes accessed | tf_op | source)
XLA Modules:
  0.0 4324.9 jit_solution(9102774538559989726)
XLA Ops:
  14.5 75.6 %all-gather.10.cloned.1.call-done = bf16[2048,2048]{1,0:T(8,128)(2,1)} async-done(((bf16[64,2048]{1,0:T(8,128)(2,1)}), bf16[2048,2048]{1,0:T(8,128)(2,1)}) %all-gather.10.cloned.1.call-update) | async-done | bytes 8388624 | tf_op jit(solution)/shard_map/all_gather | solution.py:118
  99.5 73.7 %all-gather.8.cloned.1.call-done = bf16[2048,2048]{1,0:T(8,128)(2,1)} async-done(((bf16[64,2048]{1,0:T(8,128)(2,1)}), bf16[2048,2048]{1,0:T(8,128)(2,1)}) %all-gather.8.cloned.1.call-update) | async-done | bytes 8388624 | tf_op jit(solution)/shard_map/all_gather | solution.py:117
  182.5 73.6 %all-gather.12.cloned.1.call-done = bf16[2048,2048]{1,0:T(8,128)(2,1)} async-done(((bf16[64,2048]{1,0:T(8,128)(2,1)}), bf16[2048,2048]{1,0:T(8,128)(2,1)}) %all-gather.12.cloned.1.call-update) | async-done | bytes 8388624 | tf_op jit(solution)/shard_map/all_gather | solution.py:119
  270.9 15.7 all-to-all-done.2
  293.8 14.9 collective-permute-done
  311.0 11.8 collective-permute-done.1
  324.8 20.4 collective-permute-done.2
  347.3 10.2 collective-permute-done.3
  361.1 11.0 conditional.8
  372.1 12.7 conditional.9
  384.9 14.1 conditional.10
  413.5 29.1 all-to-all-done.3
  448.5 120.5 %all-gather.16.cloned.1.call-done = bf16[2048,8192]{1,0:T(8,128)(2,1)} async-done(((bf16[64,8192]{1,0:T(8,128)(2,1)}), bf16[2048,8192]{1,0:T(8,128)(2,1)}) %all-gather.16.cloned.1.call-update) | async-done | bytes 33554448 | tf_op jit(solution)/shard_map/all_gather | solution.py:222
  568.9 17.9 fusion.230
  586.8 178.0 %all-gather.18.cloned.1.call-done = bf16[2048,8192]{1,0:T(8,128)(2,1)} async-done(((bf16[64,8192]{1,0:T(8,128)(2,1)}), bf16[2048,8192]{1,0:T(8,128)(2,1)}) %all-gather.18.cloned.1.call-update) | async-done | bytes 33554448 | tf_op jit(solution)/shard_map/all_gather | solution.py:223
  764.8 17.7 fusion.231
  782.5 178.3 %all-gather.20.cloned.1.call-done = bf16[8192,2048]{1,0:T(8,128)(2,1)} async-done(((bf16[256,2048]{1,0:T(8,128)(2,1)}), bf16[8192,2048]{1,0:T(8,128)(2,1)}) %all-gather.20.cloned.1.call-update) | async-done | bytes 33554448 | tf_op jit(solution)/shard_map/all_gather | solution.py:234
  960.8 21.3 multiply_convert_fusion.4
  982.1 17.4 fusion.232
  999.5 17.4 fusion.224
  1019.5 6.4 fusion.189
  1030.7 14.5 all-to-all-done.4
  1048.7 21.4 conditional.12
  1074.3 10.7 collective-permute-done.6
  1085.0 11.2 collective-permute-done.7
  1097.2 22.5 conditional.13
  1121.3 11.2 collective-permute-done.8
  1132.5 11.2 collective-permute-done.9
  1144.7 23.2 conditional.14
  1169.4 10.2 collective-permute-done.10
  1179.7 11.2 collective-permute-done.11
  1193.1 21.9 collective-permute-start.12
  1229.5 8.9 all-to-all-start.5
  1242.4 10.7 all-to-all-done.5
  1261.0 12.2 collective-permute-done.13
  1278.9 24.3 fusion.209
  1303.2 79.4 %reshape.1258 = f32[2048,8192]{1,0:T(8,128)} reshape(f32[8192,2048]{1,0:T(8,128)} %fusion.209) | data formatting | bytes 134217728 | tf_op jit(solution)/shard_map/reshape | solution.py:373
  1386.0 8.3 convolution_dynamic-update-slice_fusion.5
  1394.4 8.8 convolution_dynamic-update-slice_fusion.4
  1403.1 8.3 convolution_dynamic-update-slice_fusion.3
  1411.5 8.2 convolution_dynamic-update-slice_fusion.2
  1419.7 24.2 convolution_dynamic-update-slice_fusion.1
  1443.9 23.7 convolution_dynamic-update-slice_fusion
  1467.5 44.3 %constant_dynamic-update-slice_fusion = f32[2048,32768]{1,0:T(8,128)} fusion(f32[2048,32768]{1,0:T(8,128)} %convolution_dynamic-update-slice_fusion, f32[2048,8192]{1,0:T(8,128)} %reshape.1258), kind=kLoop, calls=%fused_computation.284 | loop fusion | bytes 134217728 | tf_op jit(solution)/shard_map/concatenate | solution.py:377
  1513.7 14.9 fusion.179
  1528.7 6.6 fusion.233
  1535.3 6.5 convolution_add_fusion.3
  1546.3 2761.8 %reduce-scatter.2.cloned.1.call-done = f32[64,32768]{1,0:T(8,128)} async-done(((f32[2048,32768]{1,0:T(8,128)}), f32[64,32768]{1,0:T(8,128)}) %reduce-scatter.2.cloned.1.call-update) | async-done | bytes 8388624 | tf_op jit(solution)/shard_map/reduce_scatter | solution.py:376
  (291 shorter events, 257.5 us)
Async XLA Ops:
  7.2 82.9 %all-gather.10.cloned.1.call-start = ((), (), s32[]{:S(2)}) async-start(), calls=%async_computation.10 | async-start | bytes 8650752 | tf_op jit(solution)/shard_map/all_gather | solution.py:118
  7.9 165.3 %all-gather.8.cloned.1.call-start = ((), (), s32[]{:S(2)}) async-start(), calls=%async_computation.9 | async-start | bytes 8650752 | tf_op jit(solution)/shard_map/all_gather | solution.py:117
  8.7 247.5 %all-gather.12.cloned.1.call-start = ((), (), s32[]{:S(2)}) async-start(), calls=%async_computation.11 | async-start | bytes 8650752 | tf_op jit(solution)/shard_map/all_gather | solution.py:119
  9.4 433.6 %all-gather.14.cloned.1.call-start = ((), (), s32[]{:S(2)}) async-start(), calls=%async_computation.12 | async-start | bytes 8650752 | tf_op jit(solution)/shard_map/all_gather | solution.py:120
  10.0 559.0 %all-gather.16.cloned.1.call-start = ((), (), s32[]{:S(2)}) async-start(), calls=%async_computation.13 | async-start | bytes 34603008 | tf_op jit(solution)/shard_map/all_gather | solution.py:222
  10.6 754.2 %all-gather.18.cloned.1.call-start = ((), (), s32[]{:S(2)}) async-start(), calls=%async_computation.14 | async-start | bytes 34603008 | tf_op jit(solution)/shard_map/all_gather | solution.py:223
  11.1 949.6 %all-gather.20.cloned.1.call-start = ((), (), s32[]{:S(2)}) async-start(), calls=%async_computation.15 | async-start | bytes 34603008 | tf_op jit(solution)/shard_map/all_gather | solution.py:234
  13.1 243.1 %copy-start.39 = (f32[128]{0:T(128)}, f32[128]{0:T(128)S(1)}, u32[]{:S(2)}) copy-start(f32[128]{0:T(128)S(1)} %broadcast_multiply_fusion.5) | copy-start | bytes 1540
  14.4 241.7 %copy-start.42 = (f32[128]{0:T(128)}, f32[128]{0:T(128)S(1)}, u32[]{:S(2)}) copy-start(f32[128]{0:T(128)S(1)} %add_rsqrt_fusion.1) | copy-start | bytes 1540
  14.4 158.8 %copy-start = (bf16[1,128,2048]{2,1,0:T(8,128)(2,1)S(1)}, bf16[1,128,2048]{2,1,0:T(8,128)(2,1)}, u32[]{:S(2)}) copy-start(bf16[1,128,2048]{2,1,0:T(8,128)(2,1)} %param.26) | copy-start | bytes 1572868
  95.9 83.0 %all-to-all-start.1 = ((bf16[128,16,128]{2,0,1:T(8,128)(2,1)}), bf16[128,16,128]{2,0,1:T(8,128)(2,1)S(1)}, u32[]{:S(2)}, u32[]{:S(2)}) async-start(bf16[128,16,128]{2,0,1:T(8,128)(2,1)} %bitcast.492), calls=%async_computation.1 | async-start | bytes 1048576 | tf_op jit(solution)/shard_map/all_to_all | solution.py:140
  178.9 82.9 %all-to-all-start = ((bf16[128,16,128]{2,0,1:T(8,128)(2,1)}), bf16[128,16,128]{2,0,1:T(8,128)(2,1)S(1)}, u32[]{:S(2)}, u32[]{:S(2)}) async-start(bf16[128,16,128]{2,0,1:T(8,128)(2,1)} %bitcast.493), calls=%async_computation | async-start | bytes 1048576 | tf_op jit(solution)/shard_map/all_to_all | solution.py:139
  261.8 24.9 all-to-all-start.2
  287.7 57.5 %copy-start.36 = (bf16[8,128,2,128]{3,1,0,2:T(8,128)(2,1)}, bf16[8,128,2,128]{3,1,0,2:T(8,128)(2,1)S(1)}, u32[]{:S(2)}) copy-start(bf16[8,128,2,128]{3,1,0,2:T(8,128)(2,1)S(1)} %copy.241) | copy-start | bytes 1572868
  290.0 18.8 collective-permute-start
  291.9 30.9 collective-permute-start.1
  308.7 63.4 %copy-start.34 = (bf16[1,1024,2,128]{1,3,2,0:T(8,128)(2,1)}, bf16[1,1024,2,128]{1,3,2,0:T(8,128)(2,1)S(1)}, u32[]{:S(2)}) copy-start(bf16[1,1024,2,128]{1,3,2,0:T(8,128)(2,1)S(1)} %collective-permute-done) | copy-start | bytes 1572868
  308.7 36.5 collective-permute-start.2
  322.8 37.3 copy-start.47
  322.8 34.7 collective-permute-start.3
  345.3 53.7 %collective-permute-start.4 = (bf16[1,1024,2,128]{1,3,2,0:T(8,128)(2,1)}, bf16[1,1024,2,128]{1,3,2,0:T(8,128)(2,1)}, u32[]{:S(2)}, u32[]{:S(2)}) collective-permute-start(bf16[1,1024,2,128]{1,3,2,0:T(8,128)(2,1)} %collective-permute-done.2), channel_id=1, source_target_pairs={{0,8},{8,16},{16,24},{1,9},{9,17},{17,25},{2,10},{10,18},{18,26},{... | collective-permute-start | bytes 1572872 | tf_op jit(solution)/shard_map/ppermute | solution.py:20
  357.5 41.5 collective-permute-start.5
  406.9 35.7 all-to-all-start.3
  413.5 865.4 %copy-start.45 = (f32[128]{0:T(128)}, f32[128]{0:T(128)S(1)}, u32[]{:S(2)}) copy-start(f32[128]{0:T(128)S(1)} %compare_convert_fusion) | copy-start | bytes 1540
  448.0 568.8 %copy-start.3 = (f32[128,2048]{1,0:T(8,128)}, f32[128,2048]{1,0:T(8,128)S(1)}, u32[]{:S(2)}) copy-start(f32[128,2048]{1,0:T(8,128)S(1)} %get-tuple-element.715) | copy-start | bytes 3145732
  448.5 316.3 %copy-start.8 = (bf16[128,2048]{1,0:T(8,128)(2,1)}, bf16[128,2048]{1,0:T(8,128)(2,1)S(1)}, u32[]{:S(2)}) copy-start(bf16[128,2048]{1,0:T(8,128)(2,1)S(1)} %fusion.200) | copy-start | bytes 1572868
  586.8 374.0 %copy-start.33 = (bf16[1,128,2048]{2,1,0:T(8,128)(2,1)S(1)}, bf16[1,128,2048]{2,1,0:T(8,128)(2,1)}, u32[]{:S(2)}) copy-start(bf16[1,128,2048]{2,1,0:T(8,128)(2,1)} %param.35) | copy-start | bytes 1572868
  1019.5 27.0 copy-start.23
  1026.8 18.3 all-to-all-start.4
  1071.4 13.5 collective-permute-start.6
  1073.0 23.1 collective-permute-start.7
  1119.8 12.6 collective-permute-start.8
  1121.2 22.5 collective-permute-start.9
  1167.9 11.7 collective-permute-start.10
  1169.3 21.5 collective-permute-start.11
  1192.0 32.2 copy-start.32
  1193.1 30.1 collective-permute-start.12
  1216.6 41.3 copy-start.30
  1216.6 62.3 %copy-start.10 = (bf16[128,8192]{1,0:T(8,128)(2,1)S(1)}, bf16[128,8192]{1,0:T(8,128)(2,1)}, u32[]{:S(2)}) copy-start(bf16[128,8192]{1,0:T(8,128)(2,1)} %get-tuple-element.694) | copy-start | bytes 6291460
  1229.5 23.5 all-to-all-start.5
  1253.0 20.1 all-to-all-start.6
  1258.7 14.4 collective-permute-start.13
  1273.2 112.5 %all-to-all-start.7 = ((bf16[1024,2,128]{2,1,0:T(2,128)(2,1)}), bf16[1024,2,128]{2,1,0:T(2,128)(2,1)S(1)}, u32[]{:S(2)}, u32[]{:S(2)}) async-start(bf16[1024,2,128]{2,1,0:T(2,128)(2,1)} %bitcast.131), calls=%async_computation.7 | async-start | bytes 1048576 | tf_op jit(solution)/shard_map/all_to_all | solution.py:353
  1278.9 3029.1 %reduce-scatter.2.cloned.1.call-start = ((), (), s32[]{:S(2)}) async-start(), calls=%async_computation.16 | async-start | bytes 276824064 | tf_op jit(solution)/shard_map/reduce_scatter | solution.py:376
  1303.2 82.8 %copy-start.1 = (bf16[1,128,2048]{2,1,0:T(8,128)(2,1)S(1)}, bf16[1,128,2048]{2,1,0:T(8,128)(2,1)}, u32[]{:S(2)}) copy-start(bf16[1,128,2048]{2,1,0:T(8,128)(2,1)} %param.26) | copy-start | bytes 1572868
  1303.2 82.9 %copy-start.40 = (f32[128]{0:T(128)S(1)}, f32[128]{0:T(128)}, u32[]{:S(2)}) copy-start(f32[128]{0:T(128)} %copy-done.39) | copy-start | bytes 1540
  1303.2 82.9 %copy-start.43 = (f32[128]{0:T(128)S(1)}, f32[128]{0:T(128)}, u32[]{:S(2)}) copy-start(f32[128]{0:T(128)} %copy-done.42) | copy-start | bytes 1540
  1419.7 24.2 copy-start.13
  (37 other events, 312.4 us)
Sparse Core Ops, SparseCore 0:
  11.0 79.0 all-gather.9
  93.0 80.1 all-gather.7
  176.2 79.8 all-gather.11
  259.0 101.3 all-gather.13
  363.2 205.6 all-gather.15
  571.8 192.9 all-gather.17
  767.8 192.9 all-gather.19
  1512.0 2796.0 reduce-scatter.1
where the time goes:
time: 4340 us; the launch traced here: 4320 us
  waiting for transfers between devices  3670 us (85%)
  matrix products  335 us (8%)
  local copies, waits for them, and re-layouts  168 us (4%)
  starting transfers between devices  79.8 us (2%)
  other arithmetic  52.6 us (1%)
    reduce_scatter x1, waiting for transfers between devices, local(): lax.psum_scatter(jnp.concatenate([outer_sum(normed_low, query_back), oute...  2760 us
    all_gather x1, waiting for transfers between devices, local(): lax.all_gather(down_weight, ('blk', 'head'), axis=0, tiled=True)  178 us
    all_gather x1, waiting for transfers between devices, local(): lax.all_gather(up_weight, ('blk', 'head'), axis=0, tiled=True)  178 us
    all_gather x1, waiting for transfers between devices, local(): lax.all_gather(gate_weight, ('blk', 'head'), axis=0, tiled=True)  120 us
    dot_general x7, matrix products, outer_sum(): lax.dot_general(left, right, (((0,), (0,)), ((), ())), preferred_element_...  106 us
  transfers between devices with their start and end apart: 30, of which 23 were waited for; matrix products, arithmetic and copies ran while one was open for 6% of the time, Pallas kernels for 0%

commit v1 on v0

v1 whole, which is shorter than its diff:
```python
import functools
import math

import jax
import jax.numpy as jnp
from jax import lax
from jax.experimental import pallas as pl
from jax.experimental.pallas import tpu as pltpu
from jax.sharding import PartitionSpec as P

HEADS = 16
HDIM = 128
SEQ = 4096

EPSILON = 1e-05
NEGATIVE = -1e30
SCALE = 1.0 / math.sqrt(HDIM)
VMEM_LIMIT = 48 * 1024 * 1024
BF16 = jnp.bfloat16
F32 = jnp.float32


def normalize_rows(values):
    centered = values - jnp.mean(values, axis=-1, keepdims=True)
    variance = jnp.mean(centered * centered, axis=-1, keepdims=True)
    inverse = lax.rsqrt(variance + EPSILON)
    return (centered * inverse, inverse)


def normalize_back(normed, inverse, upstream):
    mean_grad = jnp.mean(upstream, axis=-1, keepdims=True)
    mean_proj = jnp.mean(upstream * normed, axis=-1, keepdims=True)
    return inverse * (upstream - mean_grad - normed * mean_proj)


def rotary_tables(positions):
    half_dim = HDIM // 2
    frequency = jnp.exp(
        jnp.arange(half_dim).astype(F32) * (-2.0 * math.log(10000.0) / HDIM)
    )
    angles = positions.astype(F32)[:, None] * frequency[None, :]
    cosine, sine = jnp.cos(angles), jnp.sin(angles)
    return (
        jnp.concatenate([cosine, cosine], axis=1),
        jnp.concatenate([-sine, sine], axis=1),
    )


def dot(left, right):
    return jnp.dot(left, right, preferred_element_type=F32)


def dot_transposed(left, right):
    return lax.dot_general(left, right, (((1,), (1,)), ((), ())), preferred_element_type=F32)


def outer_sum(left, right):
    return lax.dot_general(left, right, (((0,), (0,)), ((), ())), preferred_element_type=F32)


def swapped(value, mask, keep=None):
    peers = lax.axis_size("blk")
    pairs = [(i, i ^ mask) for i in range(peers) if keep is None or keep(i, i ^ mask)]
    return lax.ppermute(value, "blk", pairs)


def gather_blk(value):
    peers = lax.axis_size("blk")
    me = lax.axis_index("blk")
    whole = jnp.zeros((peers,) + value.shape, value.dtype)
    whole = lax.dynamic_update_index_in_dim(whole, value, me, 0)
    for mask in range(1, peers):
        whole = lax.dynamic_update_index_in_dim(whole, swapped(value, mask), me ^ mask, 0)
    return whole


def sum_to_owner(part_for):
    peers = lax.axis_size("blk")
    me = lax.axis_index("blk")
    arrived = [
        swapped(part_for(me ^ mask).astype(BF16), mask) for mask in range(1, peers)
    ]
    total = part_for(me)
    for part in arrived:
        total = total + part.astype(F32)
    return total


def rope_kernel(lin_ref, cos_ref, sin_ref, q_ref, kv_ref, *, heads):
    width = heads * HDIM
    cosine, sine = cos_ref[...], sin_ref[...]
    for part in range(2 * heads):
        columns = slice(part * HDIM, (part + 1) * HDIM)
        value = lin_ref[:, columns].astype(F32)
        turned = (value * cosine + pltpu.roll(value, HDIM // 2, 1) * sine).astype(BF16)
        if part < heads:
            q_ref[:, columns] = turned
        else:
            kv_ref[:, slice((part - heads) * HDIM, (part - heads + 1) * HDIM)] = turned
    kv_ref[:, width:] = lin_ref[:, 2 * width :]


def rope(linear, cosine, sine, heads, block_rows):
    rows = linear.shape[0]
    width = heads * HDIM
    tile = min(256, block_rows)
    per_block = block_rows // tile
    return pl.pallas_call(
        functools.partial(rope_kernel, heads=heads),
        grid=(rows // tile,),
        in_specs=[
            pl.BlockSpec((tile, 3 * width), lambda i: (i, 0)),
            pl.BlockSpec((tile, HDIM), lambda i: (i % per_block, 0)),
            pl.BlockSpec((tile, HDIM), lambda i: (i % per_block, 0)),
        ],
        out_specs=[
            pl.BlockSpec((tile, width), lambda i: (i, 0)),
            pl.BlockSpec((tile, 2 * width), lambda i: (i, 0)),
        ],
        out_shape=[
            jax.ShapeDtypeStruct((rows, width), BF16),
            jax.ShapeDtypeStruct((rows, 2 * width), BF16),
        ],
        name="rope",
    )(linear, cosine, sine)


def unrope_kernel(place_ref, dq_ref, cos_ref, sin_ref, *refs, heads, masks):
    parts, out_ref = refs[:-1], refs[-1]
    width = heads * HDIM
    me = place_ref[0]
    cosine, sine = cos_ref[...], sin_ref[...]

    def back(value):
        return (value * cosine - pltpu.roll(value, HDIM // 2, 1) * sine).astype(BF16)

    for head in range(heads):
        columns = slice(head * HDIM, (head + 1) * HDIM)
        out_ref[:, columns] = back(dq_ref[:, columns])
    for part in range(2 * heads):
        columns = slice(part * HDIM, (part + 1) * HDIM)
        total = parts[0][:, columns].astype(F32)
        for mask, ref in zip(masks[1:], parts[1:]):
            total = total + jnp.where((me ^ mask) > me, ref[:, columns].astype(F32), 0.0)
        target = slice(width + part * HDIM, width + (part + 1) * HDIM)
        out_ref[:, target] = back(total) if part < heads else total.astype(BF16)


def unrope(place, dq, cosine, sine, parts, masks, heads, block_rows):
    rows = dq.shape[0]
    width = heads * HDIM
    tile = min(256, block_rows)
    per_block = block_rows // tile
    return pl.pallas_call(
        functools.partial(unrope_kernel, heads=heads, masks=masks),
        grid_spec=pltpu.PrefetchScalarGridSpec(
            num_scalar_prefetch=1,
            grid=(rows // tile,),
            in_specs=[
                pl.BlockSpec((tile, width), lambda i, *_: (i, 0)),
                pl.BlockSpec((tile, HDIM), lambda i, *_: (i % per_block, 0)),
                pl.BlockSpec((tile, HDIM), lambda i, *_: (i % per_block, 0)),
            ]
            + [pl.BlockSpec((tile, 2 * width), lambda i, *_: (i, 0))] * len(parts),
            out_specs=pl.BlockSpec((tile, 3 * width), lambda i, *_: (i, 0)),
        ),
        out_shape=jax.ShapeDtypeStruct((rows, 3 * width), BF16),
        name="unrope",
    )(place, dq, cosine, sine, *parts)


def visible(first_row, rows, first_key, keys, length):
    row = first_row + lax.broadcasted_iota(jnp.int32, (rows, keys), 0)
    key = first_key + lax.broadcasted_iota(jnp.int32, (rows, keys), 1)
    return (key <= row) & (key < length)


def block_cases(place_ref, mask, block_rows, body):
    me = place_ref[0]
    length = place_ref[1 + pl.program_id(0)]
    if mask == 0:
        body(True, True, me, length)
        return
    source = me ^ mask
    whole = (source + 1) * block_rows <= length

    @pl.when((source < me) & whole)
    def _():
        body(False, False, source, length)

    @pl.when((source < me) & jnp.logical_not(whole))
    def _():
        body(False, True, source, length)


def forward_kernel(place_ref, q_ref, *refs, masks, started, final, tile, block_rows):
    kv_refs, refs = refs[: 2 * len(masks)], refs[2 * len(masks) :]
    if started:
        (m_in, l_in, acc_in), refs = refs[:3], refs[3:]
    outs, (m_ref, l_ref, acc_ref) = refs[:-3], refs[-3:]
    if started:
        m_ref[...] = m_in[...]
        l_ref[...] = l_in[...]
        acc_ref[...] = acc_in[...]
    else:
        m_ref[...] = jnp.full(m_ref.shape, NEGATIVE, F32)
        l_ref[...] = jnp.zeros(l_ref.shape, F32)
        acc_ref[...] = jnp.zeros(acc_ref.shape, F32)
    me = place_ref[0]
    for number, mask in enumerate(masks):
        k_ref, v_ref = kv_refs[2 * number], kv_refs[2 * number + 1]

        def body(diagonal, masked, source, length, k_ref=k_ref, v_ref=v_ref):
            for first in range(0, block_rows, tile):
                rows = slice(first, first + tile)
                keys = first + tile if diagonal else block_rows
                scores = dot_transposed(q_ref[rows, :], k_ref[:keys, :]) * SCALE
                if masked:
                    seen = visible(
                        me * block_rows + first, tile, source * block_rows, keys, length
                    )
                    scores = jnp.where(seen, scores, NEGATIVE)
                peak_old = m_ref[rows, :1]
                peak = jnp.maximum(peak_old, jnp.max(scores, axis=1, keepdims=True))
                shrink = jnp.exp(peak_old - peak)
                weights = jnp.exp(scores - peak)
                total = l_ref[rows, :1] * shrink + jnp.sum(weights, axis=1, keepdims=True)
                acc_ref[rows, :] = acc_ref[rows, :] * shrink + dot(
                    weights.astype(BF16), v_ref[:keys, :]
                )
                m_ref[rows, :] = jnp.broadcast_to(peak, (tile, HDIM))
                l_ref[rows, :] = jnp.broadcast_to(total, (tile, HDIM))

        block_cases(place_ref, mask, block_rows, body)
    if final:
        o_ref, lse_ref = outs
        total = l_ref[...]
        o_ref[...] = (acc_ref[...] / total).astype(BF16)
        lse_ref[...] = m_ref[...] + jnp.log(total)
    else:
        for out, ref in zip(outs, (m_ref, l_ref, acc_ref)):
            out[...] = ref[...]


def forward_attention(place, query, blocks, masks, state, final, heads, block_rows):
    rows, width = query.shape
    head_block = pl.BlockSpec((block_rows, HDIM), lambda s, n, *_: (s, n))
    key_block = pl.BlockSpec((block_rows, HDIM), lambda s, n, *_: (s, n))
    value_block = pl.BlockSpec((block_rows, HDIM), lambda s, n, *_: (s, heads + n))
    wide = jax.ShapeDtypeStruct((rows, width), F32)
    outs = [jax.ShapeDtypeStruct((rows, width), BF16), wide] if final else [wide] * 3
    started = state is not None
    operands = [query]
    for block in blocks:
        operands += [block, block]
    operands += list(state) if started else []
    return pl.pallas_call(
        functools.partial(
            forward_kernel,
            masks=masks,
            started=started,
            final=final,
            tile=min(256, block_rows),
            block_rows=block_rows,
        ),
        grid_spec=pltpu.PrefetchScalarGridSpec(
            num_scalar_prefetch=1,
            grid=(rows // block_rows, heads),
            in_specs=[head_block]
            + [key_block, value_block] * len(blocks)
            + ([head_block] * 3 if started else []),
            out_specs=[head_block] * len(outs),
            scratch_shapes=[pltpu.VMEM((block_rows, HDIM), F32)] * 3,
        ),
        out_shape=outs,
        compiler_params=pltpu.CompilerParams(vmem_limit_bytes=VMEM_LIMIT),
        cost_estimate=pl.CostEstimate(
            flops=4 * rows * block_rows * width * len(masks),
            bytes_accessed=4 * rows * width * 8,
            transcendentals=rows * block_rows * heads * len(masks),
        ),
        name="attention_forward",
    )(place, *operands)


def backward_kernel(
    place_ref, q_ref, k_ref, v_ref, o_ref, do_ref, lse_ref, *refs, mask, started, tile, block_rows
):
    if started:
        dq_in, dq_ref, dk_ref, dv_ref, dk_acc, dv_acc = refs
        dq_ref[...] = dq_in[...]
    else:
        dq_ref, dk_ref, dv_ref, dk_acc, dv_acc = refs
        dq_ref[...] = jnp.zeros(dq_ref.shape, F32)
    me = place_ref[0]

    def body(diagonal, masked, source, length):
        dk_acc[...] = jnp.zeros(dk_acc.shape, F32)
        dv_acc[...] = jnp.zeros(dv_acc.shape, F32)
        for first in range(0, block_rows, tile):
            rows = slice(first, first + tile)
            keys = first + tile if diagonal else block_rows
            query, grad = q_ref[rows, :], do_ref[rows, :]
            key, value = k_ref[:keys, :], v_ref[:keys, :]
            delta = jnp.sum(
                grad.astype(F32) * o_ref[rows, :].astype(F32), axis=1, keepdims=True
            )
            scores = dot_transposed(query, key) * SCALE
            if masked:
                seen = visible(me * block_rows + first, tile, source * block_rows, keys, length)
                scores = jnp.where(seen, scores, NEGATIVE)
            probs = jnp.exp(scores - lse_ref[rows, :1])
            dv_acc[:keys, :] += outer_sum(probs.astype(BF16), grad)
            prob_grad = dot_transposed(grad, value)
            score_grad = (probs * (prob_grad - delta)).astype(BF16)
            dk_acc[:keys, :] += outer_sum(score_grad, query)
            dq_ref[rows, :] += dot(score_grad, key) * SCALE
        dk_ref[...] = (dk_acc[...] * SCALE).astype(BF16)
        dv_ref[...] = dv_acc[...].astype(BF16)

    block_cases(place_ref, mask, block_rows, body)


def backward_attention(place, query, block, mask, out, grad, lse, dq, heads, block_rows):
    rows, width = query.shape
    head_block = pl.BlockSpec((block_rows, HDIM), lambda s, n, *_: (s, n))
    value_block = pl.BlockSpec((block_rows, HDIM), lambda s, n, *_: (s, heads + n))
    started = dq is not None
    return pl.pallas_call(
        functools.partial(
            backward_kernel,
            mask=mask,
            started=started,
            tile=min(256, block_rows),
            block_rows=block_rows,
        ),
        grid_spec=pltpu.PrefetchScalarGridSpec(
            num_scalar_prefetch=1,
            grid=(rows // block_rows, heads),
            in_specs=[head_block, head_block, value_block, head_block, head_block, head_block]
            + ([head_block] if started else []),
            out_specs=[head_block] * 3,
            scratch_shapes=[pltpu.VMEM((block_rows, HDIM), F32)] * 2,
        ),
        out_shape=[
            jax.ShapeDtypeStruct((rows, width), F32),
            jax.ShapeDtypeStruct((rows, width), BF16),
            jax.ShapeDtypeStruct((rows, width), BF16),
        ],
        compiler_params=pltpu.CompilerParams(vmem_limit_bytes=VMEM_LIMIT),
        cost_estimate=pl.CostEstimate(
            flops=10 * rows * block_rows * width,
            bytes_accessed=4 * rows * width * 8,
            transcendentals=rows * block_rows * heads,
        ),
        name="attention_backward",
    )(place, query, block, block, out, grad, lse, *([dq] if started else []))


def local(
    tokens,
    lengths,
    query_weight,
    key_weight,
    value_weight,
    output_weight,
    gate_weight,
    up_weight,
    down_weight,
    cotangent,
):
    blocks = lax.axis_size("blk")
    parts = lax.axis_size("head")
    me = lax.axis_index("blk")
    part = lax.axis_index("head")
    inputs = tokens[0].astype(F32)
    token_count, model_width = inputs.shape
    hidden_width = gate_weight.shape[1]
    heads = HEADS // parts
    width = heads * HDIM
    block_rows = SEQ // blocks
    group_rows = token_count * parts
    slots = group_rows // block_rows
    shard_rows = query_weight.shape[0]
    band_rows = shard_rows * parts
    chunk = hidden_width // (blocks * parts)
    masks = list(range(blocks))
    place = jnp.concatenate([me[None].astype(jnp.int32), lengths.astype(jnp.int32)])

    row_ids = part * token_count + jnp.arange(token_count)
    my_length = jnp.sum(
        jnp.where((row_ids // block_rows)[:, None] == jnp.arange(slots)[None, :], lengths[None, :], 0),
        axis=1,
    )
    valid = (me * block_rows + row_ids % block_rows < my_length).astype(F32)[:, None]

    with jax.named_scope("projection_weights"):
        stacked = jnp.stack([query_weight, key_weight, value_weight])
        stacked = stacked.reshape(3, shard_rows, parts, width).transpose(2, 1, 0, 3)
        stacked = lax.all_to_all(stacked, "head", split_axis=0, concat_axis=0, tiled=True)
        projection = gather_blk(stacked.reshape(band_rows, 3 * width)).reshape(
            model_width, 3 * width
        )

    with jax.named_scope("tokens_gather"):
        normed_one, inverse_one = normalize_rows(inputs)
        upstream = cotangent[0].astype(F32) * valid
        upstream_low = upstream.astype(BF16)
        gathered = lax.all_gather(
            jnp.stack([normed_one.astype(BF16), upstream_low]), "head", axis=1, tiled=True
        )
        normed_group, upstream_group = gathered[0], gathered[1]

    with jax.named_scope("hidden_weights"):
        down = gather_blk(down_weight).reshape(blocks * chunk, model_width)
        both = jnp.stack([gate_weight, up_weight]).reshape(2, shard_rows, blocks, parts, chunk)
        both = both.transpose(3, 0, 1, 2, 4)
        both = lax.all_to_all(both, "head", split_axis=0, concat_axis=0, tiled=True)
        both = both.reshape(parts, 2, shard_rows, blocks * chunk)
        gate_band = both[:, 0].reshape(band_rows, blocks * chunk)
        up_band = both[:, 1].reshape(band_rows, blocks * chunk)
        gate = gather_blk(gate_band).reshape(model_width, blocks * chunk)
        up = gather_blk(up_band).reshape(model_width, blocks * chunk)
        output_full = lax.all_gather(output_weight, ("blk", "head"), axis=0, tiled=True)

    cosine, sine = rotary_tables(me * block_rows + jnp.arange(block_rows))
    with jax.named_scope("projections"):
        linear = dot(normed_group, projection).astype(BF16)
        query, key_value = rope(linear, cosine, sine, heads, block_rows)

    with jax.named_scope("attention"):
        sent = [swapped(key_value, mask, lambda i, j: j > i) for mask in masks[1:]]
        state = forward_attention(
            place, query, [key_value], [0], None, False, heads, block_rows
        )
        attended, log_total = forward_attention(
            place, query, sent, masks[1:], state, True, heads, block_rows
        )
        joined = lax.all_to_all(
            attended.reshape(parts, token_count, width), "head", split_axis=0, concat_axis=0, tiled=True
        )
        joined = joined.transpose(1, 0, 2).reshape(token_count, model_width)

    with jax.named_scope("feed_forward"):
        residual = inputs + dot(joined, output_full)
        normed_two, inverse_two = normalize_rows(residual)
        normed_two_group = lax.all_gather(normed_two.astype(BF16), "head", axis=0, tiled=True)
        gate_act = dot(normed_two_group, gate)
        up_act = dot(normed_two_group, up)
        sigmoid_gate = jax.nn.sigmoid(gate_act)
        silu_gate = gate_act * sigmoid_gate
        mixed = (silu_gate * up_act).astype(BF16)
        mixed_grad = dot_transposed(upstream_group, down)
        gate_back = (
            mixed_grad * up_act * sigmoid_gate * (1.0 + gate_act * (1.0 - sigmoid_gate))
        ).astype(BF16)
        up_back = (mixed_grad * silu_gate).astype(BF16)
        normed_two_partial = dot_transposed(gate_back, gate) + dot_transposed(up_back, up)
        normed_two_grad = lax.psum_scatter(
            normed_two_partial.astype(BF16), "head", scatter_dimension=0, tiled=True
        ).astype(F32)
        down_act = lax.psum_scatter(
            dot(mixed, down).astype(BF16), "head", scatter_dimension=0, tiled=True
        ).astype(F32)
        layer_output = ((residual + down_act) * valid).astype(BF16)[None]

    residual_grad = upstream + normalize_back(normed_two, inverse_two, normed_two_grad)
    residual_low = residual_grad.astype(BF16)

    with jax.named_scope("attention_back"):
        joined_grad = dot_transposed(residual_low, output_full).astype(BF16)
        attended_grad = lax.all_to_all(
            joined_grad.reshape(token_count, parts, width).transpose(1, 0, 2),
            "head",
            split_axis=0,
            concat_axis=0,
            tiled=True,
        ).reshape(group_rows, width)
        residual_group = lax.all_gather(residual_low, "head", axis=0, tiled=True)
        query_grad = None
        returned = {}
        for mask in masks[:0:-1] + [0]:
            block = key_value if mask == 0 else sent[mask - 1]
            query_grad, key_part, value_part = backward_attention(
                place, query, block, mask, attended, attended_grad, log_total, query_grad,
                heads, block_rows,
            )
            both_part = jnp.concatenate([key_part, value_part], axis=1)
            returned[mask] = (
                both_part if mask == 0 else swapped(both_part, mask, lambda i, j: j < i)
            )
        projection_back = unrope(
            place, query_grad, cosine, sine, [returned[mask] for mask in masks], masks,
            heads, block_rows,
        )
        normed_one_grad = lax.psum_scatter(
            dot_transposed(projection_back, projection).astype(BF16),
            "head",
            scatter_dimension=0,
            tiled=True,
        ).astype(F32)
        tokens_grad = (
            residual_grad + normalize_back(normed_one, inverse_one, normed_one_grad)
        ).astype(BF16)[None]

    def band(values, place_of):
        return lax.dynamic_slice_in_dim(values, place_of * band_rows, band_rows, 1)

    def to_shards(summed):
        return lax.all_to_all(
            summed.astype(BF16).reshape(parts, shard_rows, summed.shape[1]),
            "head",
            split_axis=0,
            concat_axis=0,
            tiled=True,
        ).astype(F32)

    with jax.named_scope("weight_grads"):
        down_grad = sum_to_owner(
            lambda j: outer_sum(lax.dynamic_slice_in_dim(mixed, j * chunk, chunk, 1), upstream_group)
        )

        def hidden_grad(back):
            summed = sum_to_owner(lambda j: outer_sum(band(normed_two_group, j), back))
            shards = to_shards(summed).reshape(parts, shard_rows, blocks, chunk)
            return shards.transpose(1, 2, 0, 3).reshape(shard_rows, hidden_width)

        gate_grad = hidden_grad(gate_back)
        up_grad = hidden_grad(up_back)
        output_part = sum_to_owner(
            lambda j: outer_sum(
                lax.dynamic_slice_in_dim(attended, j * shard_rows, shard_rows, 1), residual_group
            )
        )
        output_grad = lax.ppermute(
            output_part,
            ("blk", "head"),
            [(b * parts + h, h * blocks + b) for b in range(blocks) for h in range(parts)],
        )
        summed = sum_to_owner(lambda j: outer_sum(band(normed_group, j), projection_back))
        shards = to_shards(summed).reshape(parts, shard_rows, 3, width).transpose(2, 1, 0, 3)
        projection_grads = shards.reshape(3, shard_rows, model_width)
    return (
        layer_output,
        tokens_grad,
        projection_grads[0],
        projection_grads[1],
        projection_grads[2],
        output_grad,
        gate_grad,
        up_grad,
        down_grad,
    )


def solution(mesh):
    rows = P(("blk", "head"), None)
    places = P("blk", "head", None)
    in_specs = (places, P(), rows, rows, rows, rows, rows, rows, rows, places)
    out_specs = (places, places, rows, rows, rows, rows, rows, rows, rows)
    return jax.shard_map(local, mesh=mesh, in_specs=in_specs, out_specs=out_specs, check_vma=False)
```

time: 4340 us -> 945 us (0.22)
  waiting for transfers between devices: 3670 us -> 410 us
  matrix products: 335 us -> 145 us
  local copies, waits for them, and re-layouts: 168 us -> 79.8 us
  blocking collectives: 0 us -> 77.2 us
  Pallas kernels: 0 us -> 68.8 us
    reduce_scatter x1 -> x3, waiting for transfers between devices: 2760 us -> 89.4 us  [the longest x1 48.6 us: local(): lax.psum_scatter(dot(mixed, down).astype(BF16), 'head', scatter_dimension...]
    all_gather x6 -> x3, waiting for transfers between devices: 700 us -> 15.3 us  [the longest x1 15.3 us: local(): lax.all_gather(jnp.stack([normed_one.astype(BF16), upstream_low]), 'head'...]
    ppermute x14 -> x34, waiting for transfers between devices: 137 us -> 258 us  [the longest x33 258 us: swapped(): return lax.ppermute(value, 'blk', pairs)]
    dot_general x28 -> x5, matrix products: 151 us -> 39.4 us  [dot(): return jnp.dot(left, right, preferred_element_type=F32)]
    all_to_all x0 -> x2, blocking collectives: none -> 77.2 us  [the longest x1 42.6 us: local(): lax.all_to_all(stacked, 'head', split_axis=0, concat_axis=0, tiled=True)]
    reshape x6 -> x7, local copies, waits for them, and re-layouts: 84.8 us -> 11.9 us  [the longest x4 6.42 us: hidden_grad(): return shards.transpose(1, 2, 0, 3).reshape(shard_rows, hidden_width)]
    pallas_call x0 -> x8, Pallas kernels: none -> 68.8 us  [the longest x2 30.8 us: forward_attention(): pl.pallas_call(functools.partial(forward_kernel, masks=masks, started=sta...]
    concatenate x3 -> x0, local copies, waits for them, and re-layouts: 48.3 us -> none  [the longest x1 44.3 us: local(): jnp.concatenate([outer_sum(normed_low, query_back), outer_sum(normed_low,...]
  transfers between devices with their start and end apart: 30 -> 46, of which waited for: 23 -> 23; matrix products, arithmetic and copies ran while one was open for 6% -> 20% of each run, Pallas kernels for 0% -> 7%
where the time goes in v1:
time: 945 us; the launch traced here: 935 us
  waiting for transfers between devices  410 us (43%)
  matrix products  145 us (15%)
  starting transfers between devices  110 us (12%)
  local copies, waits for them, and re-layouts  79.8 us (8%)
  blocking collectives  77.2 us (8%)
  Pallas kernels  68.8 us (7%)
  other arithmetic  28.4 us (3%)
  between operations  15.9 us (2%)
    ppermute x33, waiting for transfers between devices, swapped(): return lax.ppermute(value, 'blk', pairs)  258 us
    ppermute x33, starting transfers between devices, swapped(): return lax.ppermute(value, 'blk', pairs)  75.4 us
    dot_general x20, matrix products, outer_sum(): lax.dot_general(left, right, (((0,), (0,)), ((), ())), preferred_element_...  66.8 us
    reduce_scatter x1, waiting for transfers between devices, local(): lax.psum_scatter(dot(mixed, down).astype(BF16), 'head', scatter_dimension...  48.6 us
    all_to_all x1, blocking collectives, local(): lax.all_to_all(stacked, 'head', split_axis=0, concat_axis=0, tiled=True)  42.6 us
    reduce_scatter x1, waiting for transfers between devices, local(): lax.psum_scatter(normed_two_partial.astype(BF16), 'head', scatter_dimensi...  40.8 us
    dot_general x5, matrix products, dot(): return jnp.dot(left, right, preferred_element_type=F32)  39.4 us
    dot_general x5, matrix products, dot_transposed(): lax.dot_general(left, right, (((1,), (1,)), ((), ())), preferred_element_...  39.3 us
  transfers between devices with their start and end apart: 46, of which 23 were waited for; matrix products, arithmetic and copies ran while one was open for 20% of the time, Pallas kernels for 7%

profile of v1, /device:TPU:5, one launch (start us, length us, event | category | flops | bytes accessed | tf_op | source)
XLA Modules:
  0.0 935.0 jit_solution(6684501848367799475)
XLA Ops:
  14.5 42.6 %all_to_all.35 = bf16[8,64,3,256]{3,1,2,0:T(8,128)(2,1)S(1)} all-to-all(bf16[8,64,3,256]{3,1,2,0:T(8,128)(2,1)S(1)} %copy.55), channel_id=1, replica_groups=mesh['blk'=4,'head'=8] {'head'}, dimensions={0} | all-to-all | bytes 1572864 | tf_op jit(solution)/shard_map/projection_weights/all_to_all | solution.py:400
  67.8 7.9 collective-permute-done
  79.9 12.7 %collective-permute-done.2 = bf16[512,768]{1,0:T(8,128)(2,1)} collective-permute-done((bf16[512,768]{1,0:T(8,128)(2,1)S(1)}, bf16[512,768]{1,0:T(8,128)(2,1)}, u32[]{:S(2)}, u32[]{:S(2)}) %collective-permute-start.2) | collective-permute-done | bytes 786464 | tf_op jit(solution)/shard_map/projection_weights/ppermute | solution.py:64
  94.6 15.3 %all-gather.5.cloned.1.call-done = bf16[2,1024,2048]{2,1,0:T(8,128)(2,1)} async-done(((bf16[2,128,2048]{2,1,0:T(8,128)(2,1)}), bf16[2,1024,2048]{2,1,0:T(8,128)(2,1)}) %all-gather.5.cloned.1.call-update) | async-done | bytes 8388624 | tf_op jit(solution)/shard_map/tokens_gather/all_gather | solution.py:409
  109.9 7.7 fusion.7.lin_ref
  129.8 5.5 attention_forward.2
  138.2 16.6 %collective-permute-done.3.refs_0_.refs_1_.k_ref.v_ref = bf16[1024,512]{1,0:T(8,128)(2,1)S(1)} collective-permute-done((bf16[1024,512]{1,0:T(8,128)(2,1)}, bf16[1024,512]{1,0:T(8,128)(2,1)S(1)}, u32[]{:S(2)}, u32[]{:S(2)}) %collective-permute-start.3) | collective-permute-done | bytes 1048608 | tf_op jit(solution)/shard_map/attention/ppermute | solution.py:64
  154.8 25.1 %collective-permute-done.4.refs_2_.refs_3_.k_ref.v_ref = bf16[1024,512]{1,0:T(8,128)(2,1)S(1)} collective-permute-done((bf16[1024,512]{1,0:T(8,128)(2,1)}, bf16[1024,512]{1,0:T(8,128)(2,1)S(1)}, u32[]{:S(2)}, u32[]{:S(2)}) %collective-permute-start.4) | collective-permute-done | bytes 1048608 | tf_op jit(solution)/shard_map/attention/ppermute | solution.py:64
  179.9 25.3 %attention_forward.3 = (bf16[1024,256]{1,0:T(8,128)(2,1)S(1)}, f32[1024,256]{1,0:T(8,128)S(1)}) custom-call(s32[2]{0:T(128)S(1)} %pad_add_fusion.place_ref, bf16[1024,256]{1,0:T(8,128)(2,1)S(1)} %copy-done.6, bf16[1024,512]{1,0:T(8,128)(2,1)S(1)} %collective-permute-done.3.refs_0_.refs_1_.k_ref.v_ref, ...), custom_call_target="tpu_custom_call" | custom-call | flops 3221225472 | bytes 8388608 | tf_op jit(solution)/shard_map/attention/attention_forward/pallas_call | solution.py:257
  207.2 7.3 all-to-all-start.1
  219.9 9.2 all-to-all-done.1
  241.2 7.1 collective-permute-start.12
  253.1 18.9 %collective-permute-done.12 = bf16[256,2048]{1,0:T(8,128)(2,1)S(1)} collective-permute-done((bf16[256,2048]{1,0:T(8,128)(2,1)}, bf16[256,2048]{1,0:T(8,128)(2,1)S(1)}, u32[]{:S(2)}, u32[]{:S(2)}) %collective-permute-start.12) | collective-permute-done | bytes 1048608 | tf_op jit(solution)/shard_map/hidden_weights/ppermute | solution.py:64
  273.1 36.6 %all-to-all-done.2 = bf16[8,2,64,4,256]{4,3,2,1,0:T(4,128)(2,1)} async-done(((bf16[8,2,64,4,256]{4,3,2,1,0:T(4,128)(2,1)}), bf16[8,2,64,4,256]{4,3,2,1,0:T(4,128)(2,1)}, u32[]{:S(2)}, u32[]{:S(2)}) %all-to-all-start.2) | async-done | bytes 2097184 | tf_op jit(solution)/shard_map/hidden_weights/all_to_all | solution.py:418
  316.0 10.4 %collective-permute-start.9 = (bf16[512,1024]{1,0:T(8,128)(2,1)S(1)}, bf16[512,1024]{1,0:T(8,128)(2,1)S(1)}, u32[]{:S(2)}, u32[]{:S(2)}) collective-permute-start(bf16[512,1024]{1,0:T(8,128)(2,1)S(1)} %bitcast.206), channel_id=1, source_target_pairs={{0,8},{8,0},{16,24},{24,16},{1,9},{9,1},{17,25},{25,17},{2,10},{10... | collective-permute-start | bytes 3145736 | tf_op jit(solution)/shard_map/hidden_weights/ppermute | solution.py:64
  341.1 6.9 collective-permute-done.9
  349.1 26.7 %collective-permute-done.10 = bf16[512,1024]{1,0:T(8,128)(2,1)S(1)} collective-permute-done((bf16[512,1024]{1,0:T(8,128)(2,1)S(1)}, bf16[512,1024]{1,0:T(8,128)(2,1)S(1)}, u32[]{:S(2)}, u32[]{:S(2)}) %collective-permute-start.10) | collective-permute-done | bytes 1048608 | tf_op jit(solution)/shard_map/hidden_weights/ppermute | solution.py:64
  377.9 15.1 %collective-permute-done.6 = bf16[512,1024]{1,0:T(8,128)(2,1)S(1)} collective-permute-done((bf16[512,1024]{1,0:T(8,128)(2,1)S(1)}, bf16[512,1024]{1,0:T(8,128)(2,1)S(1)}, u32[]{:S(2)}, u32[]{:S(2)}) %collective-permute-start.6) | collective-permute-done | bytes 1048608 | tf_op jit(solution)/shard_map/hidden_weights/ppermute | solution.py:64
  394.1 26.1 %collective-permute-done.7 = bf16[512,1024]{1,0:T(8,128)(2,1)S(1)} collective-permute-done((bf16[512,1024]{1,0:T(8,128)(2,1)S(1)}, bf16[512,1024]{1,0:T(8,128)(2,1)S(1)}, u32[]{:S(2)}, u32[]{:S(2)}) %collective-permute-start.7) | collective-permute-done | bytes 1048608 | tf_op jit(solution)/shard_map/hidden_weights/ppermute | solution.py:64
  422.3 8.2 fusion.6
  430.6 7.6 fusion.92
  438.3 9.7 %multiply_convert_fusion.1 = (bf16[1024,1024]{1,0:T(8,128)(2,1)S(1)}, bf16[1024,1024]{1,0:T(8,128)(2,1)S(1)}, bf16[1024,1024]{1,0:T(8,128)(2,1)}) fusion(f32[1024,1024]{1,0:T(8,128)S(1)} %copy-done.45, f32[1024,1024]{1,0:T(8,128)S(1)} %fusion.92, bf16[1024,2048]{1,0:T(8,128)(2,1)S(1)} %copy-done.27, bf16[2048,1024]{1,0:T(8,128)(2,1)} %bitcast.18), kind=kOutput, calls=%fused_computation.5 | convolution fusion | flops 4310695936 | bytes 23068672 | tf_op jit(solution)/shard_map/feed_forward/dot_general | solution.py:50
  447.9 7.9 fusion.93
  455.8 8.7 add_convert_fusion
  464.6 9.4 %convolution_convert_fusion.1 = bf16[1024,2048]{1,0:T(8,128)(2,1)} fusion(bf16[1024,1024]{1,0:T(8,128)(2,1)} %get-tuple-element.55, bf16[1024,2048]{1,0:T(8,128)(2,1)} %bitcast.29), kind=kOutput, calls=%fused_computation.10 | convolution fusion | flops 4297064448 | bytes 10485760 | tf_op jit(solution)/shard_map/feed_forward/dot_general | solution.py:50
  474.1 40.8 %reduce-scatter.6.cloned.1.call-done = bf16[128,2048]{1,0:T(8,128)(2,1)} async-done(((bf16[1024,2048]{1,0:T(8,128)(2,1)}), bf16[128,2048]{1,0:T(8,128)(2,1)}) %reduce-scatter.6.cloned.1.call-update) | async-done | bytes 524304 | tf_op jit(solution)/shard_map/feed_forward/reduce_scatter | solution.py:459
  516.7 48.6 %reduce-scatter.4.cloned.1.call-done = bf16[128,2048]{1,0:T(8,128)(2,1)} async-done(((bf16[1024,2048]{1,0:T(8,128)(2,1)}), bf16[128,2048]{1,0:T(8,128)(2,1)}) %reduce-scatter.4.cloned.1.call-update) | async-done | bytes 524304 | tf_op jit(solution)/shard_map/feed_forward/reduce_scatter | solution.py:462
  568.9 6.6 convolution_convert_fusion.5
  575.6 34.6 %all_to_all.36 = bf16[8,128,256]{2,1,0:T(8,128)(2,1)S(1)} all-to-all(bf16[8,128,256]{2,1,0:T(8,128)(2,1)S(1)} %bitcast.215), channel_id=1, replica_groups=mesh['blk'=4,'head'=8] {'head'}, dimensions={0} | all-to-all | bytes 1048576 | tf_op jit(solution)/shard_map/attention_back/all_to_all | solution.py:472
  610.2 8.3 attention_backward.4
  619.5 9.2 attention_backward.5
  642.8 7.8 attention_backward.7
  652.7 13.7 %collective-permute-done.15.refs_1_ = bf16[1024,512]{1,0:T(8,128)(2,1)} collective-permute-done((bf16[1024,512]{1,0:T(8,128)(2,1)}, bf16[1024,512]{1,0:T(8,128)(2,1)}, u32[]{:S(2)}, u32[]{:S(2)}) %collective-permute-start.15) | collective-permute-done | bytes 1048608 | tf_op jit(solution)/shard_map/attention_back/ppermute | solution.py:64
  666.4 6.0 unrope.1
  672.4 7.9 convolution_convert_fusion
  684.6 23.1 %collective-permute-start.27 = (bf16[512,1024]{1,0:T(8,128)(2,1)S(1)}, bf16[512,1024]{1,0:T(8,128)(2,1)S(1)}, u32[]{:S(2)}, u32[]{:S(2)}) collective-permute-start(bf16[512,1024]{1,0:T(8,128)(2,1)S(1)} %convolution_convert_fusion.12), channel_id=1, source_target_pairs={{0,24},{8,16},{16,8},{24,0},{1,25},{9,17},{17,9},{25,1},{2,26},{10... | collective-permute-start | bytes 3145736 | tf_op jit(solution)/shard_map/weight_grads/ppermute | solution.py:64
  724.0 7.0 collective-permute-done.27
  733.7 21.7 %collective-permute-done.26 = bf16[512,1024]{1,0:T(8,128)(2,1)} collective-permute-done((bf16[512,1024]{1,0:T(8,128)(2,1)}, bf16[512,1024]{1,0:T(8,128)(2,1)}, u32[]{:S(2)}, u32[]{:S(2)}) %collective-permute-start.26) | collective-permute-done | bytes 1048608 | tf_op jit(solution)/shard_map/weight_grads/ppermute | solution.py:64
  755.4 5.2 add_convert_fusion.2
  760.6 6.5 all-to-all-start.5
  769.7 6.1 convolution_convert_fusion.2
  776.0 24.3 %collective-permute-done.29 = bf16[512,1024]{1,0:T(8,128)(2,1)} collective-permute-done((bf16[512,1024]{1,0:T(8,128)(2,1)}, bf16[512,1024]{1,0:T(8,128)(2,1)}, u32[]{:S(2)}, u32[]{:S(2)}) %collective-permute-start.29) | collective-permute-done | bytes 1048608 | tf_op jit(solution)/shard_map/weight_grads/ppermute | solution.py:64
  814.7 5.3 all-to-all-start.6
  839.5 16.6 %collective-permute-done.19 = bf16[512,768]{1,0:T(8,128)(2,1)S(1)} collective-permute-done((bf16[512,768]{1,0:T(8,128)(2,1)}, bf16[512,768]{1,0:T(8,128)(2,1)S(1)}, u32[]{:S(2)}, u32[]{:S(2)}) %collective-permute-start.19) | collective-permute-done | bytes 786464 | tf_op jit(solution)/shard_map/weight_grads/ppermute | solution.py:64
  865.8 5.2 all-to-all-start.4
  874.1 8.5 collective-permute-done.23
  884.4 5.2 collective-permute-done.22
  898.5 6.0 convert_add_fusion
  (270 shorter events, 220.0 us)
Async XLA Ops:
  7.2 102.7 %all-gather.5.cloned.1.call-start = ((), (), s32[]{:S(2)}) async-start(), calls=%async_computation.10 | async-start | bytes 9437184 | tf_op jit(solution)/shard_map/tokens_gather/all_gather | solution.py:409
  13.2 221.0 %all-gather.7.cloned.1.call-start = ((), (), s32[]{:S(2)}) async-start(), calls=%async_computation.11 | async-start | bytes 8650752 | tf_op jit(solution)/shard_map/hidden_weights/all_gather | solution.py:424
  57.9 17.8 %collective-permute-start = (bf16[512,768]{1,0:T(8,128)(2,1)S(1)}, bf16[512,768]{1,0:T(8,128)(2,1)}, u32[]{:S(2)}, u32[]{:S(2)}) collective-permute-start(bf16[512,768]{1,0:T(8,128)(2,1)S(1)} %bitcast.225), channel_id=1, source_target_pairs={{0,8},{8,0},{16,24},{24,16},{1,9},{9,1},{17,25},{25,17},{2,10},{10... | collective-permute-start | bytes 2359304 | tf_op jit(solution)/shard_map/projection_weights/ppermute | solution.py:64
  59.2 18.6 %collective-permute-start.1 = (bf16[512,768]{1,0:T(8,128)(2,1)S(1)}, bf16[512,768]{1,0:T(8,128)(2,1)}, u32[]{:S(2)}, u32[]{:S(2)}) collective-permute-start(bf16[512,768]{1,0:T(8,128)(2,1)S(1)} %bitcast.226), channel_id=1, source_target_pairs={{0,16},{8,24},{16,0},{24,8},{1,17},{9,25},{17,1},{25,9},{2,18},{10... | collective-permute-start | bytes 2359304 | tf_op jit(solution)/shard_map/projection_weights/ppermute | solution.py:64
  61.4 31.1 %collective-permute-start.2 = (bf16[512,768]{1,0:T(8,128)(2,1)S(1)}, bf16[512,768]{1,0:T(8,128)(2,1)}, u32[]{:S(2)}, u32[]{:S(2)}) collective-permute-start(bf16[512,768]{1,0:T(8,128)(2,1)S(1)} %bitcast.227), channel_id=1, source_target_pairs={{0,24},{8,16},{16,8},{24,0},{1,25},{9,17},{17,9},{25,1},{2,26},{10... | collective-permute-start | bytes 2359304 | tf_op jit(solution)/shard_map/projection_weights/ppermute | solution.py:64
  121.6 33.2 %collective-permute-start.3 = (bf16[1024,512]{1,0:T(8,128)(2,1)}, bf16[1024,512]{1,0:T(8,128)(2,1)S(1)}, u32[]{:S(2)}, u32[]{:S(2)}) collective-permute-start(bf16[1024,512]{1,0:T(8,128)(2,1)} %get-tuple-element.29.refs_0_.refs_1_.k_ref.v_ref), channel_id=1, source_target_pairs={{0,8},{16,24},{1,9},{17,25},{2,10},{18,26},{3,11},{19,27},{4,12},{... | collective-permute-start | bytes 3145736 | tf_op jit(solution)/shard_map/attention/ppermute | solution.py:64
  124.8 55.1 %collective-permute-start.4 = (bf16[1024,512]{1,0:T(8,128)(2,1)}, bf16[1024,512]{1,0:T(8,128)(2,1)S(1)}, u32[]{:S(2)}, u32[]{:S(2)}) collective-permute-start(bf16[1024,512]{1,0:T(8,128)(2,1)} %get-tuple-element.29.refs_0_.refs_1_.k_ref.v_ref), channel_id=1, source_target_pairs={{0,16},{8,24},{1,17},{9,25},{2,18},{10,26},{3,19},{11,27},{4,20},{... | collective-permute-start | bytes 3145736 | tf_op jit(solution)/shard_map/attention/ppermute | solution.py:64
  126.1 53.8 %collective-permute-start.5 = (bf16[1024,512]{1,0:T(8,128)(2,1)}, bf16[1024,512]{1,0:T(8,128)(2,1)S(1)}, u32[]{:S(2)}, u32[]{:S(2)}) collective-permute-start(bf16[1024,512]{1,0:T(8,128)(2,1)} %get-tuple-element.29.refs_0_.refs_1_.k_ref.v_ref), channel_id=1, source_target_pairs={{0,24},{8,16},{1,25},{9,17},{2,26},{10,18},{3,27},{11,19},{4,28},{... | collective-permute-start | bytes 3145736 | tf_op jit(solution)/shard_map/attention/ppermute | solution.py:64
  127.5 514.1 %copy-start.1 = (s32[2]{0:T(128)}, s32[2]{0:T(128)S(1)}, u32[]{:S(2)}) copy-start(s32[2]{0:T(128)S(1)} %pad_add_fusion.place_ref) | copy-start | bytes 28
  207.2 21.9 %all-to-all-start.1 = ((bf16[8,128,256]{1,2,0:T(8,128)(2,1)}), bf16[8,128,256]{1,2,0:T(8,128)(2,1)}, u32[]{:S(2)}, u32[]{:S(2)}) async-start(bf16[8,128,256]{1,2,0:T(8,128)(2,1)} %copy.58), calls=%async_computation.1 | async-start | bytes 1048576 | tf_op jit(solution)/shard_map/attention/all_to_all | solution.py:439
  229.1 80.6 %all-to-all-start.2 = ((bf16[8,2,64,4,256]{4,3,2,1,0:T(4,128)(2,1)}), bf16[8,2,64,4,256]{4,3,2,1,0:T(4,128)(2,1)}, u32[]{:S(2)}, u32[]{:S(2)}) async-start(bf16[8,2,64,4,256]{4,3,2,1,0:T(4,128)(2,1)} %maximum_bitcast_fusion), calls=%async_computation.2 | async-start | bytes 4194304 | tf_op jit(solution)/shard_map/hidden_weights/all_to_all | solution.py:418
  234.2 196.4 %all-gather.9.cloned.1.call-start = ((), (), s32[]{:S(2)}) async-start(), calls=%async_computation.12 | async-start | bytes 4718592 | tf_op jit(solution)/shard_map/feed_forward/all_gather | solution.py:447
  241.1 273.8 %reduce-scatter.6.cloned.1.call-start = ((), (), s32[]{:S(2)}) async-start(), calls=%async_computation.14 | async-start | bytes 4718592 | tf_op jit(solution)/shard_map/feed_forward/reduce_scatter | solution.py:459
  241.2 30.9 %collective-permute-start.12 = (bf16[256,2048]{1,0:T(8,128)(2,1)}, bf16[256,2048]{1,0:T(8,128)(2,1)S(1)}, u32[]{:S(2)}, u32[]{:S(2)}) collective-permute-start(bf16[256,2048]{1,0:T(8,128)(2,1)} %param.18), channel_id=1, source_target_pairs={{0,8},{8,0},{16,24},{24,16},{1,9},{9,1},{17,25},{25,17},{2,10},{10... | collective-permute-start | bytes 3145736 | tf_op jit(solution)/shard_map/hidden_weights/ppermute | solution.py:64
  248.3 78.1 %collective-permute-start.13 = (bf16[256,2048]{1,0:T(8,128)(2,1)}, bf16[256,2048]{1,0:T(8,128)(2,1)}, u32[]{:S(2)}, u32[]{:S(2)}) collective-permute-start(bf16[256,2048]{1,0:T(8,128)(2,1)} %param.18), channel_id=1, source_target_pairs={{0,16},{8,24},{16,0},{24,8},{1,17},{9,25},{17,1},{25,9},{2,18},{10... | collective-permute-start | bytes 3145736 | tf_op jit(solution)/shard_map/hidden_weights/ppermute | solution.py:64
  248.3 81.6 %collective-permute-start.14 = (bf16[256,2048]{1,0:T(8,128)(2,1)}, bf16[256,2048]{1,0:T(8,128)(2,1)}, u32[]{:S(2)}, u32[]{:S(2)}) collective-permute-start(bf16[256,2048]{1,0:T(8,128)(2,1)} %param.18), channel_id=1, source_target_pairs={{0,24},{8,16},{16,8},{24,0},{1,25},{9,17},{17,9},{25,1},{2,26},{10... | collective-permute-start | bytes 3145736 | tf_op jit(solution)/shard_map/hidden_weights/ppermute | solution.py:64
  316.0 32.1 %collective-permute-start.9 = (bf16[512,1024]{1,0:T(8,128)(2,1)S(1)}, bf16[512,1024]{1,0:T(8,128)(2,1)S(1)}, u32[]{:S(2)}, u32[]{:S(2)}) collective-permute-start(bf16[512,1024]{1,0:T(8,128)(2,1)S(1)} %bitcast.206), channel_id=1, source_target_pairs={{0,8},{8,0},{16,24},{24,16},{1,9},{9,1},{17,25},{25,17},{2,10},{10... | collective-permute-start | bytes 3145736 | tf_op jit(solution)/shard_map/hidden_weights/ppermute | solution.py:64
  328.7 47.1 %collective-permute-start.10 = (bf16[512,1024]{1,0:T(8,128)(2,1)S(1)}, bf16[512,1024]{1,0:T(8,128)(2,1)S(1)}, u32[]{:S(2)}, u32[]{:S(2)}) collective-permute-start(bf16[512,1024]{1,0:T(8,128)(2,1)S(1)} %bitcast.207), channel_id=1, source_target_pairs={{0,16},{8,24},{16,0},{24,8},{1,17},{9,25},{17,1},{25,9},{2,18},{10... | collective-permute-start | bytes 3145736 | tf_op jit(solution)/shard_map/hidden_weights/ppermute | solution.py:64
  328.7 48.2 %collective-permute-start.11 = (bf16[512,1024]{1,0:T(8,128)(2,1)S(1)}, bf16[512,1024]{1,0:T(8,128)(2,1)S(1)}, u32[]{:S(2)}, u32[]{:S(2)}) collective-permute-start(bf16[512,1024]{1,0:T(8,128)(2,1)S(1)} %bitcast.208), channel_id=1, source_target_pairs={{0,24},{8,16},{16,8},{24,0},{1,25},{9,17},{17,9},{25,1},{2,26},{10... | collective-permute-start | bytes 3145736 | tf_op jit(solution)/shard_map/hidden_weights/ppermute | solution.py:64
  332.2 60.8 %collective-permute-start.6 = (bf16[512,1024]{1,0:T(8,128)(2,1)S(1)}, bf16[512,1024]{1,0:T(8,128)(2,1)S(1)}, u32[]{:S(2)}, u32[]{:S(2)}) collective-permute-start(bf16[512,1024]{1,0:T(8,128)(2,1)S(1)} %bitcast.202), channel_id=1, source_target_pairs={{0,8},{8,0},{16,24},{24,16},{1,9},{9,1},{17,25},{25,17},{2,10},{10... | collective-permute-start | bytes 3145736 | tf_op jit(solution)/shard_map/hidden_weights/ppermute | solution.py:64
  333.7 86.6 %collective-permute-start.7 = (bf16[512,1024]{1,0:T(8,128)(2,1)S(1)}, bf16[512,1024]{1,0:T(8,128)(2,1)S(1)}, u32[]{:S(2)}, u32[]{:S(2)}) collective-permute-start(bf16[512,1024]{1,0:T(8,128)(2,1)S(1)} %bitcast.203), channel_id=1, source_target_pairs={{0,16},{8,24},{16,0},{24,8},{1,17},{9,25},{17,1},{25,9},{2,18},{10... | collective-permute-start | bytes 3145736 | tf_op jit(solution)/shard_map/hidden_weights/ppermute | solution.py:64
  348.0 73.2 %collective-permute-start.8 = (bf16[512,1024]{1,0:T(8,128)(2,1)S(1)}, bf16[512,1024]{1,0:T(8,128)(2,1)S(1)}, u32[]{:S(2)}, u32[]{:S(2)}) collective-permute-start(bf16[512,1024]{1,0:T(8,128)(2,1)S(1)} %bitcast.205), channel_id=1, source_target_pairs={{0,24},{8,16},{16,8},{24,0},{1,25},{9,17},{17,9},{25,1},{2,26},{10... | collective-permute-start | bytes 3145736 | tf_op jit(solution)/shard_map/hidden_weights/ppermute | solution.py:64
  464.6 100.7 %reduce-scatter.4.cloned.1.call-start = ((), (), s32[]{:S(2)}) async-start(), calls=%async_computation.13 | async-start | bytes 4718592 | tf_op jit(solution)/shard_map/feed_forward/reduce_scatter | solution.py:462
  474.0 91.2 %copy-start.32 = (bf16[1,128,2048]{2,1,0:T(8,128)(2,1)S(1)}, bf16[1,128,2048]{2,1,0:T(8,128)(2,1)}, u32[]{:S(2)}) copy-start(bf16[1,128,2048]{2,1,0:T(8,128)(2,1)} %param.19) | copy-start | bytes 1572868
  474.0 384.5 %all-gather.11.cloned.1.call-start = ((), (), s32[]{:S(2)}) async-start(), calls=%async_computation.16 | async-start | bytes 4718592 | tf_op jit(solution)/shard_map/attention_back/all_gather | solution.py:479
  568.8 353.4 %reduce-scatter.8.cloned.1.call-start = ((), (), s32[]{:S(2)}) async-start(), calls=%async_computation.15 | async-start | bytes 4718592 | tf_op jit(solution)/shard_map/attention_back/reduce_scatter | solution.py:496
  633.5 32.9 %collective-permute-start.15 = (bf16[1024,512]{1,0:T(8,128)(2,1)}, bf16[1024,512]{1,0:T(8,128)(2,1)}, u32[]{:S(2)}, u32[]{:S(2)}) collective-permute-start(bf16[1024,512]{1,0:T(8,128)(2,1)} %pad_maximum_fusion.2), channel_id=1, source_target_pairs={{8,0},{24,16},{9,1},{25,17},{10,2},{26,18},{11,3},{27,19},{12,4},{... | collective-permute-start | bytes 3145736 | tf_op jit(solution)/shard_map/attention_back/ppermute | solution.py:64
  636.0 30.4 %collective-permute-start.16 = (bf16[1024,512]{1,0:T(8,128)(2,1)}, bf16[1024,512]{1,0:T(8,128)(2,1)}, u32[]{:S(2)}, u32[]{:S(2)}) collective-permute-start(bf16[1024,512]{1,0:T(8,128)(2,1)} %pad_maximum_fusion.3), channel_id=1, source_target_pairs={{16,0},{24,8},{17,1},{25,9},{18,2},{26,10},{19,3},{27,11},{20,4},{... | collective-permute-start | bytes 3145736 | tf_op jit(solution)/shard_map/attention_back/ppermute | solution.py:64
  639.3 27.1 %collective-permute-start.17 = (bf16[1024,512]{1,0:T(8,128)(2,1)}, bf16[1024,512]{1,0:T(8,128)(2,1)}, u32[]{:S(2)}, u32[]{:S(2)}) collective-permute-start(bf16[1024,512]{1,0:T(8,128)(2,1)} %pad_maximum_fusion.4), channel_id=1, source_target_pairs={{16,8},{24,0},{17,9},{25,1},{18,10},{26,2},{19,11},{27,3},{20,12},... | collective-permute-start | bytes 3145736 | tf_op jit(solution)/shard_map/attention_back/ppermute | solution.py:64
  684.6 46.4 %collective-permute-start.27 = (bf16[512,1024]{1,0:T(8,128)(2,1)S(1)}, bf16[512,1024]{1,0:T(8,128)(2,1)S(1)}, u32[]{:S(2)}, u32[]{:S(2)}) collective-permute-start(bf16[512,1024]{1,0:T(8,128)(2,1)S(1)} %convolution_convert_fusion.12), channel_id=1, source_target_pairs={{0,24},{8,16},{16,8},{24,0},{1,25},{9,17},{17,9},{25,1},{2,26},{10... | collective-permute-start | bytes 3145736 | tf_op jit(solution)/shard_map/weight_grads/ppermute | solution.py:64
  711.1 44.2 %collective-permute-start.26 = (bf16[512,1024]{1,0:T(8,128)(2,1)}, bf16[512,1024]{1,0:T(8,128)(2,1)}, u32[]{:S(2)}, u32[]{:S(2)}) collective-permute-start(bf16[512,1024]{1,0:T(8,128)(2,1)} %convolution_convert_fusion.13), channel_id=1, source_target_pairs={{0,16},{8,24},{16,0},{24,8},{1,17},{9,25},{17,1},{25,9},{2,18},{10... | collective-permute-start | bytes 3145736 | tf_op jit(solution)/shard_map/weight_grads/ppermute | solution.py:64
  714.5 40.9 %collective-permute-start.25 = (bf16[512,1024]{1,0:T(8,128)(2,1)}, bf16[512,1024]{1,0:T(8,128)(2,1)}, u32[]{:S(2)}, u32[]{:S(2)}) collective-permute-start(bf16[512,1024]{1,0:T(8,128)(2,1)} %convolution_convert_fusion.14), channel_id=1, source_target_pairs={{0,8},{8,0},{16,24},{24,16},{1,9},{9,1},{17,25},{25,17},{2,10},{10... | collective-permute-start | bytes 3145736 | tf_op jit(solution)/shard_map/weight_grads/ppermute | solution.py:64
  717.8 58.2 %collective-permute-start.30 = (bf16[512,1024]{1,0:T(8,128)(2,1)}, bf16[512,1024]{1,0:T(8,128)(2,1)}, u32[]{:S(2)}, u32[]{:S(2)}) collective-permute-start(bf16[512,1024]{1,0:T(8,128)(2,1)} %convolution_convert_fusion.9), channel_id=1, source_target_pairs={{0,24},{8,16},{16,8},{24,0},{1,25},{9,17},{17,9},{25,1},{2,26},{10... | collective-permute-start | bytes 3145736 | tf_op jit(solution)/shard_map/weight_grads/ppermute | solution.py:64
  721.2 79.0 %collective-permute-start.29 = (bf16[512,1024]{1,0:T(8,128)(2,1)}, bf16[512,1024]{1,0:T(8,128)(2,1)}, u32[]{:S(2)}, u32[]{:S(2)}) collective-permute-start(bf16[512,1024]{1,0:T(8,128)(2,1)} %convolution_convert_fusion.10), channel_id=1, source_target_pairs={{0,16},{8,24},{16,0},{24,8},{1,17},{9,25},{17,1},{25,9},{2,18},{10... | collective-permute-start | bytes 3145736 | tf_op jit(solution)/shard_map/weight_grads/ppermute | solution.py:64
  731.9 68.4 %collective-permute-start.28 = (bf16[512,1024]{1,0:T(8,128)(2,1)}, bf16[512,1024]{1,0:T(8,128)(2,1)}, u32[]{:S(2)}, u32[]{:S(2)}) collective-permute-start(bf16[512,1024]{1,0:T(8,128)(2,1)} %convolution_convert_fusion.11), channel_id=1, source_target_pairs={{0,8},{8,0},{16,24},{24,16},{1,9},{9,1},{17,25},{25,17},{2,10},{10... | collective-permute-start | bytes 3145736 | tf_op jit(solution)/shard_map/weight_grads/ppermute | solution.py:64
  760.6 54.1 %all-to-all-start.5 = ((bf16[8,64,1024]{2,1,0:T(8,128)(2,1)}), bf16[8,64,1024]{2,1,0:T(8,128)(2,1)}, u32[]{:S(2)}, u32[]{:S(2)}) async-start(bf16[8,64,1024]{2,1,0:T(8,128)(2,1)} %bitcast.221), calls=%async_computation.8 | async-start | bytes 2097152 | tf_op jit(solution)/shard_map/weight_grads/all_to_all | solution.py:510
  775.8 122.6 %collective-permute-start.33 = (bf16[256,2048]{1,0:T(8,128)(2,1)}, bf16[256,2048]{1,0:T(8,128)(2,1)}, u32[]{:S(2)}, u32[]{:S(2)}) collective-permute-start(bf16[256,2048]{1,0:T(8,128)(2,1)} %convolution_convert_fusion.2), channel_id=1, source_target_pairs={{0,24},{8,16},{16,8},{24,0},{1,25},{9,17},{17,9},{25,1},{2,26},{10... | collective-permute-start | bytes 3145736 | tf_op jit(solution)/shard_map/weight_grads/ppermute | solution.py:64
  806.9 30.8 %collective-permute-start.20 = (bf16[512,768]{1,0:T(8,128)(2,1)}, bf16[512,768]{1,0:T(8,128)(2,1)S(1)}, u32[]{:S(2)}, u32[]{:S(2)}) collective-permute-start(bf16[512,768]{1,0:T(8,128)(2,1)} %convolution_convert_fusion.15), channel_id=1, source_target_pairs={{0,24},{8,16},{16,8},{24,0},{1,25},{9,17},{17,9},{25,1},{2,26},{10... | collective-permute-start | bytes 2359304 | tf_op jit(solution)/shard_map/weight_grads/ppermute | solution.py:64
  810.4 45.7 %collective-permute-start.19 = (bf16[512,768]{1,0:T(8,128)(2,1)}, bf16[512,768]{1,0:T(8,128)(2,1)S(1)}, u32[]{:S(2)}, u32[]{:S(2)}) collective-permute-start(bf16[512,768]{1,0:T(8,128)(2,1)} %convolution_convert_fusion.16), channel_id=1, source_target_pairs={{0,16},{8,24},{16,0},{24,8},{1,17},{9,25},{17,1},{25,9},{2,18},{10... | collective-permute-start | bytes 2359304 | tf_op jit(solution)/shard_map/weight_grads/ppermute | solution.py:64
  813.5 42.6 %collective-permute-start.18 = (bf16[512,768]{1,0:T(8,128)(2,1)}, bf16[512,768]{1,0:T(8,128)(2,1)}, u32[]{:S(2)}, u32[]{:S(2)}) collective-permute-start(bf16[512,768]{1,0:T(8,128)(2,1)} %convolution_convert_fusion.17), channel_id=1, source_target_pairs={{0,8},{8,0},{16,24},{24,16},{1,9},{9,1},{17,25},{25,17},{2,10},{10... | collective-permute-start | bytes 2359304 | tf_op jit(solution)/shard_map/weight_grads/ppermute | solution.py:64
  814.7 51.1 %all-to-all-start.6 = ((bf16[8,64,1024]{2,1,0:T(8,128)(2,1)}), bf16[8,64,1024]{2,1,0:T(8,128)(2,1)S(1)}, u32[]{:S(2)}, u32[]{:S(2)}) async-start(bf16[8,64,1024]{2,1,0:T(8,128)(2,1)} %bitcast.44), calls=%async_computation.9 | async-start | bytes 2097152 | tf_op jit(solution)/shard_map/weight_grads/all_to_all | solution.py:510
  824.6 73.8 %collective-permute-start.32 = (bf16[256,2048]{1,0:T(8,128)(2,1)}, bf16[256,2048]{1,0:T(8,128)(2,1)}, u32[]{:S(2)}, u32[]{:S(2)}) collective-permute-start(bf16[256,2048]{1,0:T(8,128)(2,1)} %convolution_convert_fusion.3), channel_id=1, source_target_pairs={{0,16},{8,24},{16,0},{24,8},{1,17},{9,25},{17,1},{25,9},{2,18},{10... | collective-permute-start | bytes 3145736 | tf_op jit(solution)/shard_map/weight_grads/ppermute | solution.py:64
  837.7 60.8 %collective-permute-start.31 = (bf16[256,2048]{1,0:T(8,128)(2,1)}, bf16[256,2048]{1,0:T(8,128)(2,1)}, u32[]{:S(2)}, u32[]{:S(2)}) collective-permute-start(bf16[256,2048]{1,0:T(8,128)(2,1)} %convolution_convert_fusion.4), channel_id=1, source_target_pairs={{0,8},{8,0},{16,24},{24,16},{1,9},{9,1},{17,25},{25,17},{2,10},{10... | collective-permute-start | bytes 3145736 | tf_op jit(solution)/shard_map/weight_grads/ppermute | solution.py:64
  862.5 20.1 %collective-permute-start.23 = (bf16[64,2048]{1,0:T(8,128)(2,1)}, bf16[64,2048]{1,0:T(8,128)(2,1)S(1)}, u32[]{:S(2)}, u32[]{:S(2)}) collective-permute-start(bf16[64,2048]{1,0:T(8,128)(2,1)} %convolution_convert_fusion.6), channel_id=1, source_target_pairs={{0,24},{8,16},{16,8},{24,0},{1,25},{9,17},{17,9},{25,1},{2,26},{10... | collective-permute-start | bytes 786440 | tf_op jit(solution)/shard_map/weight_grads/ppermute | solution.py:64
  864.8 24.8 %collective-permute-start.22 = (bf16[64,2048]{1,0:T(8,128)(2,1)S(1)}, bf16[64,2048]{1,0:T(8,128)(2,1)S(1)}, u32[]{:S(2)}, u32[]{:S(2)}) collective-permute-start(bf16[64,2048]{1,0:T(8,128)(2,1)S(1)} %convolution_convert_fusion.7), channel_id=1, source_target_pairs={{0,16},{8,24},{16,0},{24,8},{1,17},{9,25},{17,1},{25,9},{2,18},{10... | collective-permute-start | bytes 786440 | tf_op jit(solution)/shard_map/weight_grads/ppermute | solution.py:64
  865.8 50.2 %all-to-all-start.4 = ((bf16[8,64,768]{2,1,0:T(8,128)(2,1)}), bf16[8,64,768]{2,1,0:T(8,128)(2,1)S(1)}, u32[]{:S(2)}, u32[]{:S(2)}) async-start(bf16[8,64,768]{2,1,0:T(8,128)(2,1)} %bitcast.40), calls=%async_computation.7 | async-start | bytes 1572864 | tf_op jit(solution)/shard_map/weight_grads/all_to_all | solution.py:510
  882.7 7.2 collective-permute-start.21
  893.8 28.4 %collective-permute-start.24 = (f32[64,2048]{1,0:T(8,128)}, f32[64,2048]{1,0:T(8,128)}, u32[]{:S(2)}, u32[]{:S(2)}) collective-permute-start(f32[64,2048]{1,0:T(8,128)} %fusion.4), channel_id=1, source_target_pairs={{0,0},{1,4},{2,8},{3,12},{4,16},{5,20},{6,24},{7,28},{8,1},{9,5},{... | collective-permute-start | bytes 1572872 | tf_op jit(solution)/shard_map/weight_grads/ppermute | solution.py:535
  (46 other events, 655.1 us)
Sparse Core Ops, SparseCore 0:
  13.4 96.5 all-gather.4
  112.9 90.4 all-gather.6
  241.2 77.1 all-gather.8
  464.7 50.1 reduce-scatter.5
  517.1 48.1 reduce-scatter.3
  569.0 58.8 all-gather.10
  680.5 67.3 reduce-scatter.7

commit v2 on v1

v2 whole, which is shorter than its diff:
```python
import functools
import math

import jax
import jax.numpy as jnp
from jax import lax
from jax.experimental import pallas as pl
from jax.experimental.pallas import tpu as pltpu
from jax.sharding import PartitionSpec as P

HEADS = 16
HDIM = 128
SEQ = 4096

EPSILON = 1e-05
NEGATIVE = -1e30
SCALE = 1.0 / math.sqrt(HDIM)
SCALE2 = SCALE * math.log2(math.e)
TILE = 512
VMEM_LIMIT = 48 * 1024 * 1024
BF16 = jnp.bfloat16
F32 = jnp.float32


def normalize_rows(values):
    centered = values - jnp.mean(values, axis=-1, keepdims=True)
    variance = jnp.mean(centered * centered, axis=-1, keepdims=True)
    inverse = lax.rsqrt(variance + EPSILON)
    return (centered * inverse, inverse)


def normalize_back(normed, inverse, upstream):
    mean_grad = jnp.mean(upstream, axis=-1, keepdims=True)
    mean_proj = jnp.mean(upstream * normed, axis=-1, keepdims=True)
    return inverse * (upstream - mean_grad - normed * mean_proj)


def rotary_tables(positions):
    half_dim = HDIM // 2
    frequency = jnp.exp(
        jnp.arange(half_dim).astype(F32) * (-2.0 * math.log(10000.0) / HDIM)
    )
    angles = positions.astype(F32)[:, None] * frequency[None, :]
    cosine, sine = jnp.cos(angles), jnp.sin(angles)
    return (
        jnp.concatenate([cosine, cosine], axis=1),
        jnp.concatenate([-sine, sine], axis=1),
    )


def dot(left, right):
    return jnp.dot(left, right, preferred_element_type=F32)


def dot_transposed(left, right):
    return lax.dot_general(left, right, (((1,), (1,)), ((), ())), preferred_element_type=F32)


def outer_sum(left, right):
    return lax.dot_general(left, right, (((0,), (0,)), ((), ())), preferred_element_type=F32)


def swapped(value, mask, keep=None):
    peers = lax.axis_size("blk")
    pairs = [(i, i ^ mask) for i in range(peers) if keep is None or keep(i, i ^ mask)]
    return lax.ppermute(value, "blk", pairs)


def after(value, *others):
    return lax.optimization_barrier((value,) + others)[0]


def send_near(value):
    peers = lax.axis_size("blk")
    return [swapped(value, mask) for mask in range(1, 3 if peers == 4 else peers)]


def send_far(near):
    if lax.axis_size("blk") != 4:
        return []
    first, second = near
    half = first.shape[0] // 2
    return [[swapped(first[:half], 2), swapped(second[half:], 1)]]


def gather_blk(value, arrived):
    peers = lax.axis_size("blk")
    me = lax.axis_index("blk")
    whole = jnp.zeros((peers,) + value.shape, value.dtype)
    whole = lax.dynamic_update_index_in_dim(whole, value, me, 0)
    for mask, part in enumerate(arrived, 1):
        row = 0
        for piece in part if isinstance(part, list) else [part]:
            start = (me ^ mask, row) + (0,) * (value.ndim - 1)
            whole = lax.dynamic_update_slice(whole, piece[None], start)
            row += piece.shape[0]
    return whole


def terms_of(part_for):
    peers = lax.axis_size("blk")
    me = lax.axis_index("blk")
    return [part_for(me)] + [part_for(me ^ mask).astype(BF16) for mask in range(1, peers)]


def near_halves(terms):
    half = terms[0].shape[0] // 2
    return ((slice(0, half), 1, 2), (slice(half, None), 2, 1))


def sum_pass(terms):
    if len(terms) != 4:
        return []
    return [swapped(terms[3][rows], near) for rows, near, _ in near_halves(terms)]


def sum_own(terms):
    if len(terms) != 4:
        return [swapped(term, mask) for mask, term in enumerate(terms) if mask]
    return [swapped(terms[near][rows], near) for rows, near, _ in near_halves(terms)]


def sum_far(terms, passed):
    return [
        swapped((terms[far][rows].astype(F32) + part.astype(F32)).astype(BF16), far)
        for part, (rows, _, far) in zip(passed, near_halves(terms))
    ]


def sum_end(terms, own, far):
    total = terms[0]
    if len(terms) != 4:
        for part in own:
            total = total + part.astype(F32)
        return total
    totals = [
        total[rows] + first.astype(F32) + second.astype(F32)
        for first, second, (rows, _, _) in zip(own, far, near_halves(terms))
    ]
    return jnp.concatenate(totals, axis=0)


def sum_to_owner(terms):
    return sum_end(terms, sum_own(terms), sum_far(terms, sum_pass(terms)))


def collect_kernel(*refs, parts, blocks, chunk):
    *ins, out_ref = refs
    for number, ref in enumerate(ins):
        for block in range(blocks):
            first = (number * blocks + block) * chunk
            for part in range(parts):
                start = (block * parts + part) * chunk
                out_ref[part, :, first : first + chunk] = ref[:, start : start + chunk]


def collect(arrays, parts, blocks, chunk):
    rows = arrays[0].shape[0]
    return pl.pallas_call(
        functools.partial(collect_kernel, parts=parts, blocks=blocks, chunk=chunk),
        out_shape=jax.ShapeDtypeStruct(
            (parts, rows, len(arrays) * blocks * chunk), arrays[0].dtype
        ),
        compiler_params=pltpu.CompilerParams(vmem_limit_bytes=VMEM_LIMIT),
        name="collect",
    )(*arrays)


def spread_kernel(in_ref, *outs, parts, blocks, chunk):
    for number, ref in enumerate(outs):
        for block in range(blocks):
            first = (number * blocks + block) * chunk
            for part in range(parts):
                start = (block * parts + part) * chunk
                ref[:, start : start + chunk] = in_ref[part, :, first : first + chunk].astype(F32)


def spread(array, count, parts, blocks, chunk):
    rows = array.shape[1]
    shape = jax.ShapeDtypeStruct((rows, blocks * parts * chunk), F32)
    return pl.pallas_call(
        functools.partial(spread_kernel, parts=parts, blocks=blocks, chunk=chunk),
        out_shape=[shape] * count,
        compiler_params=pltpu.CompilerParams(vmem_limit_bytes=VMEM_LIMIT),
        name="spread",
    )(array)


def rope_kernel(lin_ref, cos_ref, sin_ref, q_ref, kv_ref, *, heads):
    width = heads * HDIM
    cosine, sine = cos_ref[...], sin_ref[...]
    for part in range(2 * heads):
        columns = slice(part * HDIM, (part + 1) * HDIM)
        value = lin_ref[:, columns].astype(F32)
        turned = (value * cosine + pltpu.roll(value, HDIM // 2, 1) * sine).astype(BF16)
        if part < heads:
            q_ref[:, columns] = turned
        else:
            start = 2 * (part - heads) * HDIM
            kv_ref[:, start : start + HDIM] = turned
            columns = slice((part + heads) * HDIM, (part + heads + 1) * HDIM)
            kv_ref[:, start + HDIM : start + 2 * HDIM] = lin_ref[:, columns]


def rope(linear, cosine, sine, heads, block_rows):
    rows = linear.shape[0]
    width = heads * HDIM
    tile = min(256, block_rows)
    per_block = block_rows // tile
    return pl.pallas_call(
        functools.partial(rope_kernel, heads=heads),
        grid=(rows // tile,),
        in_specs=[
            pl.BlockSpec((tile, 3 * width), lambda i: (i, 0)),
            pl.BlockSpec((tile, HDIM), lambda i: (i % per_block, 0)),
            pl.BlockSpec((tile, HDIM), lambda i: (i % per_block, 0)),
        ],
        out_specs=[
            pl.BlockSpec((tile, width), lambda i: (i, 0)),
            pl.BlockSpec((tile, 2 * width), lambda i: (i, 0)),
        ],
        out_shape=[
            jax.ShapeDtypeStruct((rows, width), BF16),
            jax.ShapeDtypeStruct((rows, 2 * width), BF16),
        ],
        name="rope",
    )(linear, cosine, sine)


def unrope_kernel(place_ref, dq_ref, cos_ref, sin_ref, *refs, heads, masks):
    parts, out_ref = refs[:-1], refs[-1]
    width = heads * HDIM
    me = place_ref[0]
    cosine, sine = cos_ref[...], sin_ref[...]

    def back(value):
        return (value * cosine - pltpu.roll(value, HDIM // 2, 1) * sine).astype(BF16)

    for head in range(heads):
        columns = slice(head * HDIM, (head + 1) * HDIM)
        out_ref[:, columns] = back(dq_ref[:, columns])
    for part in range(2 * heads):
        head, is_value = part // 2, part % 2
        columns = slice(part * HDIM, (part + 1) * HDIM)
        total = parts[0][:, columns].astype(F32)
        for mask, ref in zip(masks[1:], parts[1:]):
            total = total + jnp.where((me ^ mask) > me, ref[:, columns].astype(F32), 0.0)
        start = (1 + is_value) * width + head * HDIM
        out_ref[:, start : start + HDIM] = total.astype(BF16) if is_value else back(total)


def unrope(place, dq, cosine, sine, parts, masks, heads, block_rows):
    rows = dq.shape[0]
    width = heads * HDIM
    tile = min(256, block_rows)
    per_block = block_rows // tile
    return pl.pallas_call(
        functools.partial(unrope_kernel, heads=heads, masks=masks),
        grid_spec=pltpu.PrefetchScalarGridSpec(
            num_scalar_prefetch=1,
            grid=(rows // tile,),
            in_specs=[
                pl.BlockSpec((tile, width), lambda i, *_: (i, 0)),
                pl.BlockSpec((tile, HDIM), lambda i, *_: (i % per_block, 0)),
                pl.BlockSpec((tile, HDIM), lambda i, *_: (i % per_block, 0)),
            ]
            + [pl.BlockSpec((tile, 2 * width), lambda i, *_: (i, 0))] * len(parts),
            out_specs=pl.BlockSpec((tile, 3 * width), lambda i, *_: (i, 0)),
        ),
        out_shape=jax.ShapeDtypeStruct((rows, 3 * width), BF16),
        name="unrope",
    )(place, dq, cosine, sine, *parts)


def visible(first_row, rows, first_key, keys, length):
    row = first_row + lax.broadcasted_iota(jnp.int32, (keys, rows), 1)
    key = first_key + lax.broadcasted_iota(jnp.int32, (keys, rows), 0)
    return (key <= row) & (key < length)

def block_cases(place_ref, mask, block_rows, body):
    me = place_ref[0]
    length = place_ref[1 + pl.program_id(0)]
    if mask == 0:
        body(True, True, me, length)
        return
    source = me ^ mask
    whole = (source + 1) * block_rows <= length
    @pl.when((source < me) & whole)
    def _():
        body(False, False, source, length)
    @pl.when((source < me) & jnp.logical_not(whole))
    def _():
        body(False, True, source, length)

def forward_kernel(place_ref, q_ref, *refs, masks, started, final, tile, block_rows):
    kv_refs, refs = refs[: len(masks)], refs[len(masks) :]
    if started:
        (m_in, l_in, acc_in), refs = refs[:3], refs[3:]
    outs, (m_ref, l_ref, acc_ref) = refs[:-3], refs[-3:]
    if started:
        m_ref[...] = m_in[0]
        l_ref[...] = l_in[0]
        acc_ref[...] = acc_in[0]
    else:
        m_ref[...] = jnp.full(m_ref.shape, NEGATIVE, F32)
        l_ref[...] = jnp.zeros(l_ref.shape, F32)
        acc_ref[...] = jnp.zeros(acc_ref.shape, F32)
    me = place_ref[0]
    for mask, kv_ref in zip(masks, kv_refs):

        def body(diagonal, masked, source, length, kv_ref=kv_ref):
            for first in range(0, block_rows, tile):
                rows = slice(first, first + tile)
                keys = first + tile if diagonal else block_rows
                scores = dot_transposed(kv_ref[:keys, :HDIM], q_ref[rows, :])
                if masked:
                    seen = visible(me * block_rows + first, tile, source * block_rows, keys, length)
                    scores = jnp.where(seen, scores, NEGATIVE)
                peak_old = m_ref[:, rows]
                peak = jnp.maximum(peak_old, jnp.max(scores, axis=0, keepdims=True) * SCALE2)
                shrink = jnp.exp2(peak_old - peak)
                weights = jnp.exp2(scores * SCALE2 - peak)
                l_ref[:, rows] = l_ref[:, rows] * shrink + jnp.sum(weights, axis=0, keepdims=True)
                acc_ref[:, rows] = acc_ref[:, rows] * shrink + outer_sum(
                    kv_ref[:keys, HDIM:], weights.astype(BF16)
                )
                m_ref[:, rows] = peak
        block_cases(place_ref, mask, block_rows, body)
    if final:
        o_ref, lse_ref = outs
        total = l_ref[...]
        o_ref[...] = (acc_ref[...] / total).T.astype(BF16)
        lse_ref[0] = m_ref[...] + jnp.log2(total)
    else:
        for out, ref in zip(outs, (m_ref, l_ref, acc_ref)):
            out[0] = ref[...]

def forward_attention(place, query, blocks, masks, state, final, heads, block_rows):
    rows, width = query.shape
    groups = rows // block_rows * heads
    head_block = pl.BlockSpec((block_rows, HDIM), lambda s, n, *_: (s, n))
    pair_block = pl.BlockSpec((block_rows, 2 * HDIM), lambda s, n, *_: (s, n))
    row_block = pl.BlockSpec((1, 1, block_rows), lambda s, n, *_: (s * heads + n, 0, 0))
    acc_block = pl.BlockSpec((1, HDIM, block_rows), lambda s, n, *_: (s * heads + n, 0, 0))
    row_shape = jax.ShapeDtypeStruct((groups, 1, block_rows), F32)
    acc_shape = jax.ShapeDtypeStruct((groups, HDIM, block_rows), F32)
    if final:
        out_specs, out_shape = [head_block, row_block], [jax.ShapeDtypeStruct((rows, width), BF16), row_shape]
    else:
        out_specs, out_shape = [row_block, row_block, acc_block], [row_shape, row_shape, acc_shape]
    started = state is not None
    operands = [query, *blocks] + (list(state) if started else [])
    return pl.pallas_call(
        functools.partial(forward_kernel, masks=masks, started=started, final=final, tile=min(TILE, block_rows), block_rows=block_rows),
        grid_spec=pltpu.PrefetchScalarGridSpec(
            num_scalar_prefetch=1, grid=(rows // block_rows, heads),
            in_specs=[head_block] + [pair_block] * len(blocks) + ([row_block, row_block, acc_block] if started else []),
            out_specs=out_specs,
            scratch_shapes=[pltpu.VMEM((1, block_rows), F32)] * 2 + [pltpu.VMEM((HDIM, block_rows), F32)],
        ),
        out_shape=out_shape,
        compiler_params=pltpu.CompilerParams(vmem_limit_bytes=VMEM_LIMIT),
        name="attention_forward",
    )(place, *operands)

def backward_kernel(
    place_ref, q_ref, o_ref, do_ref, lse_ref, *refs, masks, started, final, tile, block_rows
):
    kv_refs, refs = refs[: len(masks)], refs[len(masks) :]
    if started:
        dq_in, refs = refs[0], refs[1:]
    dq_ref, dkv_refs, (dq_acc, dk_acc, dv_acc) = refs[0], refs[1:-3], refs[-3:]
    dq_acc[...] = dq_in[0] if started else jnp.zeros(dq_acc.shape, F32)
    me = place_ref[0]
    for mask, kv_ref, dkv_ref in zip(masks, kv_refs, dkv_refs):

        def body(diagonal, masked, source, length, kv_ref=kv_ref, dkv_ref=dkv_ref):
            for first in range(0, block_rows, tile):
                rows = slice(first, first + tile)
                keys = first + tile if diagonal else block_rows
                query, grad = q_ref[rows, :], do_ref[rows, :]
                key, value = kv_ref[:keys, :HDIM], kv_ref[:keys, HDIM:]
                delta = jnp.sum(
                    (grad.astype(F32) * o_ref[rows, :].astype(F32)).T, axis=0, keepdims=True
                )
                scores = dot_transposed(key, query)
                if masked:
                    seen = visible(
                        me * block_rows + first, tile, source * block_rows, keys, length
                    )
                    scores = jnp.where(seen, scores, NEGATIVE)
                probs = jnp.exp2(scores * SCALE2 - lse_ref[0, :, rows])
                prob_grad = dot_transposed(value, grad)
                score_grad = (probs * (prob_grad - delta)).astype(BF16)
                dv = dot(probs.astype(BF16), grad)
                dk = dot(score_grad, query)
                dq_acc[:, rows] += outer_sum(key, score_grad) * SCALE
                if diagonal:
                    if first:
                        dk_acc[:first, :] += dk[:first]
                        dv_acc[:first, :] += dv[:first]
                    dk_acc[rows, :] = dk[first:]
                    dv_acc[rows, :] = dv[first:]
                elif first == 0:
                    dk_acc[...] = dk
                    dv_acc[...] = dv
                else:
                    dk_acc[...] += dk
                    dv_acc[...] += dv
            dkv_ref[:, :HDIM] = (dk_acc[...] * SCALE).astype(BF16)
            dkv_ref[:, HDIM:] = dv_acc[...].astype(BF16)

        block_cases(place_ref, mask, block_rows, body)
    if final:
        dq_ref[...] = dq_acc[...].T
    else:
        dq_ref[0] = dq_acc[...]


def backward_attention(
    place, query, blocks, masks, out, grad, lse, dq, final, heads, block_rows
):
    rows, width = query.shape
    groups = rows // block_rows * heads
    head_block = pl.BlockSpec((block_rows, HDIM), lambda s, n, *_: (s, n))
    pair_block = pl.BlockSpec((block_rows, 2 * HDIM), lambda s, n, *_: (s, n))
    row_block = pl.BlockSpec((1, 1, block_rows), lambda s, n, *_: (s * heads + n, 0, 0))
    acc_block = pl.BlockSpec((1, HDIM, block_rows), lambda s, n, *_: (s * heads + n, 0, 0))
    started = dq is not None
    if final:
        dq_shape = jax.ShapeDtypeStruct((rows, width), F32)
    else:
        dq_shape = jax.ShapeDtypeStruct((groups, HDIM, block_rows), F32)
    dkv_shape = jax.ShapeDtypeStruct((rows, 2 * width), BF16)
    return pl.pallas_call(
        functools.partial(
            backward_kernel,
            masks=masks,
            started=started,
            final=final,
            tile=min(TILE, block_rows),
            block_rows=block_rows,
        ),
        grid_spec=pltpu.PrefetchScalarGridSpec(
            num_scalar_prefetch=1,
            grid=(rows // block_rows, heads),
            in_specs=[head_block] * 3
            + [row_block]
            + [pair_block] * len(masks)
            + ([acc_block] if started else []),
            out_specs=[head_block if final else acc_block] + [pair_block] * len(masks),
            scratch_shapes=[pltpu.VMEM((HDIM, block_rows), F32)]
            + [pltpu.VMEM((block_rows, HDIM), F32)] * 2,
        ),
        out_shape=[dq_shape] + [dkv_shape] * len(masks),
        compiler_params=pltpu.CompilerParams(vmem_limit_bytes=VMEM_LIMIT),
        name="attention_backward",
    )(place, query, out, grad, lse, *blocks, *([dq] if started else []))


def local(
    tokens,
    lengths,
    query_weight,
    key_weight,
    value_weight,
    output_weight,
    gate_weight,
    up_weight,
    down_weight,
    cotangent,
):
    blocks = lax.axis_size("blk")
    parts = lax.axis_size("head")
    me = lax.axis_index("blk")
    part = lax.axis_index("head")
    inputs = tokens[0].astype(F32)
    token_count, model_width = inputs.shape
    hidden_width = gate_weight.shape[1]
    heads = HEADS // parts
    width = heads * HDIM
    block_rows = SEQ // blocks
    group_rows = token_count * parts
    slots = group_rows // block_rows
    shard_rows = query_weight.shape[0]
    band_rows = shard_rows * parts
    chunk = hidden_width // (blocks * parts)
    masks = list(range(blocks))
    place = jnp.concatenate([me[None].astype(jnp.int32), lengths.astype(jnp.int32)])

    row_ids = part * token_count + jnp.arange(token_count)
    my_length = jnp.sum(
        jnp.where((row_ids // block_rows)[:, None] == jnp.arange(slots)[None, :], lengths[None, :], 0),
        axis=1,
    )
    valid = (me * block_rows + row_ids % block_rows < my_length).astype(F32)[:, None]

    with jax.named_scope("projection_weights"):
        stacked = collect([query_weight, key_weight, value_weight], parts, 1, width)
        stacked = lax.all_to_all(stacked, "head", split_axis=0, concat_axis=0, tiled=True)
        stacked = stacked.reshape(band_rows, 3 * width)
        down_near = send_near(down_weight)
        output_rows = lax.ppermute(
            output_weight,
            ("blk", "head"),
            [(h * blocks + b, b * parts + h) for b in range(blocks) for h in range(parts)],
        )
        stacked, down_near, output_rows = lax.optimization_barrier(
            (stacked, down_near, output_rows)
        )
        near = send_near(stacked)
        projection = gather_blk(stacked, near + send_far(near)).reshape(model_width, 3 * width)

    with jax.named_scope("tokens_gather"):
        normed_one, inverse_one = normalize_rows(inputs)
        upstream = cotangent[0].astype(F32) * valid
        upstream_low = upstream.astype(BF16)
        normed_group = lax.all_gather(
            after(normed_one.astype(BF16), stacked), "head", axis=0, tiled=True
        )

    with jax.named_scope("hidden_weights"):
        both = collect([gate_weight, up_weight], parts, blocks, chunk)
        normed_group, projection = lax.optimization_barrier((normed_group, projection))

    cosine, sine = rotary_tables(me * block_rows + jnp.arange(block_rows))
    with jax.named_scope("projections"):
        linear = dot(normed_group, projection).astype(BF16)
        query, key_value = rope(linear, cosine, sine, heads, block_rows)

    with jax.named_scope("attention"):
        sent = [swapped(key_value, mask, lambda i, j: j > i) for mask in masks[1:]]
        state = forward_attention(
            place, query, [key_value], [0], None, False, heads, block_rows
        )
        both = lax.all_to_all(
            after(both, normed_group), "head", split_axis=0, concat_axis=0, tiled=True
        ).reshape(band_rows, 2 * blocks * chunk)
        output_near = send_near(after(output_rows, key_value))
        output = gather_blk(output_rows, output_near + send_far(output_near))
        output = output.reshape(width, model_width)
        upstream_group = lax.all_gather(
            after(upstream_low, normed_group), "head", axis=0, tiled=True
        )
        state, sent, both, output, upstream_group = lax.optimization_barrier(
            (state, sent, both, output, upstream_group)
        )
        near, down_far = send_near(both), send_far(down_near)
        attended, log_total = forward_attention(
            place, query, sent, masks[1:], state, True, heads, block_rows
        )
        joined = lax.psum_scatter(
            dot(attended, output).astype(BF16), "head", scatter_dimension=0, tiled=True
        )
        joined, near = lax.optimization_barrier((joined, near))
        both = gather_blk(both, near + send_far(near)).reshape(model_width, 2 * blocks * chunk)
        down = gather_blk(down_weight, down_near + down_far).reshape(blocks * chunk, model_width)

    with jax.named_scope("feed_forward"):
        residual = inputs + joined.astype(F32)
        normed_two, inverse_two = normalize_rows(residual)
        normed_two_group = lax.all_gather(normed_two.astype(BF16), "head", axis=0, tiled=True)
        both_act = dot(normed_two_group, both)
        gate_act, up_act = jnp.split(both_act, 2, axis=1)
        sigmoid_gate = jax.nn.sigmoid(gate_act)
        silu_gate = gate_act * sigmoid_gate
        mixed = (silu_gate * up_act).astype(BF16)
        mixed_grad = dot_transposed(upstream_group, down)
        gate_back = (
            mixed_grad * up_act * sigmoid_gate * (1.0 + gate_act * (1.0 - sigmoid_gate))
        ).astype(BF16)
        up_back = (mixed_grad * silu_gate).astype(BF16)
        both_back = jnp.concatenate([gate_back, up_back], axis=1)
        normed_two_partial = dot_transposed(both_back, both)
        normed_two_grad = lax.psum_scatter(
            normed_two_partial.astype(BF16), "head", scatter_dimension=0, tiled=True
        ).astype(F32)
        down_partial = dot(mixed, down).astype(BF16)

        def band(values, place_of):
            return lax.dynamic_slice_in_dim(values, place_of * band_rows, band_rows, 1)

        both_terms = terms_of(lambda j: outer_sum(band(normed_two_group, j), both_back))
        both_passed = sum_pass(both_terms)
        down_terms = terms_of(
            lambda j: outer_sum(lax.dynamic_slice_in_dim(mixed, j * chunk, chunk, 1), upstream_group)
        )
        normed_two_grad, down_partial, both_terms, both_passed, down_terms = (
            lax.optimization_barrier(
                (normed_two_grad, down_partial, both_terms, both_passed, down_terms)
            )
        )

    residual_grad = upstream + normalize_back(normed_two, inverse_two, normed_two_grad)
    residual_low = residual_grad.astype(BF16)

    def to_shards(summed):
        return lax.all_to_all(
            summed.astype(BF16).reshape(parts, shard_rows, summed.shape[1]),
            "head",
            split_axis=0,
            concat_axis=0,
            tiled=True,
        )

    with jax.named_scope("attention_back"):
        residual_group = lax.all_gather(residual_low, "head", axis=0, tiled=True)
        both_own, both_far = sum_own(both_terms), sum_far(both_terms, both_passed)
        down_passed = sum_pass(down_terms)
        residual_group, both_own, both_far, down_terms, down_passed = lax.optimization_barrier(
            (residual_group, both_own, both_far, down_terms, down_passed)
        )
        both_sum = sum_end(both_terms, both_own, both_far)
        attended_grad = dot_transposed(residual_group, output).astype(BF16)
        down_act = lax.psum_scatter(
            after(down_partial, residual_group), "head", scatter_dimension=0, tiled=True
        ).astype(F32)
        query_grad, *remote = backward_attention(
            place, query, sent, masks[1:], attended, attended_grad, log_total, None,
            False, heads, block_rows,
        )
        returned = [
            swapped(part, mask, lambda i, j: j < i) for mask, part in zip(masks[1:], remote)
        ]
        hidden_shards = to_shards(both_sum)
        query_grad, returned, hidden_shards = lax.optimization_barrier(
            (query_grad, returned, hidden_shards)
        )
        query_grad, own = backward_attention(
            place, query, [key_value], [0], attended, attended_grad, log_total, query_grad,
            True, heads, block_rows,
        )
        down_sum = sum_end(down_terms, sum_own(down_terms), sum_far(down_terms, down_passed))
        output_terms = terms_of(
            lambda j: outer_sum(
                lax.dynamic_slice_in_dim(attended, j * shard_rows, shard_rows, 1), residual_group
            )
        )
        output_grad = lax.ppermute(
            sum_to_owner(output_terms).astype(BF16),
            ("blk", "head"),
            [(b * parts + h, h * blocks + b) for b in range(blocks) for h in range(parts)],
        ).astype(F32)
        down_act = after(down_act, query_grad)
        layer_output = ((residual + down_act) * valid).astype(BF16)[None]
        projection_back = unrope(
            place, query_grad, cosine, sine, [own] + returned, masks,
            heads, block_rows,
        )
        normed_one_grad = lax.psum_scatter(
            dot_transposed(projection_back, projection).astype(BF16),
            "head",
            scatter_dimension=0,
            tiled=True,
        ).astype(F32)
        tokens_grad = (
            residual_grad + normalize_back(normed_one, inverse_one, normed_one_grad)
        ).astype(BF16)[None]

    with jax.named_scope("weight_grads"):

        gate_grad, up_grad = spread(hidden_shards, 2, parts, blocks, chunk)
        summed = sum_to_owner(terms_of(lambda j: outer_sum(band(normed_group, j), projection_back)))
        projection_grads = spread(to_shards(summed), 3, parts, 1, width)
    return (
        layer_output,
        tokens_grad,
        projection_grads[0],
        projection_grads[1],
        projection_grads[2],
        output_grad,
        gate_grad,
        up_grad,
        down_sum,
    )


def solution(mesh):
    rows = P(("blk", "head"), None)
    places = P("blk", "head", None)
    in_specs = (places, P(), rows, rows, rows, rows, rows, rows, rows, places)
    out_specs = (places, places, rows, rows, rows, rows, rows, rows, rows)
    return jax.shard_map(local, mesh=mesh, in_specs=in_specs, out_specs=out_specs, check_vma=False)
```

time: 945 us -> 705 us (0.75)
  waiting for transfers between devices: 410 us -> 314 us
  blocking collectives: 77.2 us -> 0 us
  matrix products: 145 us -> 106 us
  Pallas kernels: 68.8 us -> 50.5 us
  local copies, waits for them, and re-layouts: 79.8 us -> 67.8 us
  other arithmetic: 28.4 us -> 39.4 us
  starting transfers between devices: 110 us -> 99.3 us
    all_to_all x2 -> x0, blocking collectives: 77.2 us -> none  [the longest x1 42.6 us: local(): lax.all_to_all(stacked, 'head', split_axis=0, concat_axis=0, tiled=True)]
    reduce_scatter x1 -> x2, waiting for transfers between devices: 48.6 us -> 0.01 us  [the longest x1 0.01 us: local(): lax.psum_scatter(dot(attended, output).astype(BF16), 'head', scatter_dime...]
    ppermute x33 -> x46, waiting for transfers between devices: 258 us -> 214 us  [swapped(): return lax.ppermute(value, 'blk', pairs)]
    all_to_all x2, waiting for transfers between devices: 45.7 us -> 10 us  [the longest x1 10 us: local(): lax.all_to_all(after(both, normed_group), 'head', split_axis=0, concat_ax...]
    dot_general x20 -> x16, matrix products: 66.8 us -> 37.1 us  [outer_sum(): lax.dot_general(left, right, (((0,), (0,)), ((), ())), preferred_element_...]
    ppermute x1 -> x2, waiting for transfers between devices: 0.01 us -> 29.3 us  [the longest x1 17.9 us: local(): lax.ppermute(sum_to_owner(output_terms).astype(BF16), ('blk', 'head'), [(...]
    all_to_all x3 -> x2, waiting for transfers between devices: 0.01 us -> 26.4 us  [to_shards(): lax.all_to_all(summed.astype(BF16).reshape(parts, shard_rows, summed.shap...]
    reduce_scatter x1, waiting for transfers between devices: 40.8 us -> 16.4 us  [local(): lax.psum_scatter(normed_two_partial.astype(BF16), 'head', scatter_dimensi...]
  transfers between devices with their start and end apart: 46 -> 60, of which waited for: 23 -> 25; matrix products, arithmetic and copies ran while one was open for 20% -> 20% of each run, Pallas kernels for 7% -> 6%
where the time goes in v2:
time: 705 us; the launch traced here: 693 us
  waiting for transfers between devices  314 us (45%)
  matrix products  106 us (15%)
  starting transfers between devices  99.3 us (14%)
  local copies, waits for them, and re-layouts  67.8 us (10%)
  Pallas kernels  50.5 us (7%)
  other arithmetic  39.4 us (6%)
  between operations  16.2 us (2%)
    ppermute x46, waiting for transfers between devices, swapped(): return lax.ppermute(value, 'blk', pairs)  214 us
    ppermute x46, starting transfers between devices, swapped(): return lax.ppermute(value, 'blk', pairs)  55.2 us
    dot_general x16, matrix products, outer_sum(): lax.dot_general(left, right, (((0,), (0,)), ((), ())), preferred_element_...  37.1 us
    dot_general x4, matrix products, dot_transposed(): lax.dot_general(left, right, (((1,), (1,)), ((), ())), preferred_element_...  35.6 us
    dot_general x4, matrix products, dot(): return jnp.dot(left, right, preferred_element_type=F32)  33 us
    all_to_all x2, waiting for transfers between devices, to_shards(): lax.all_to_all(summed.astype(BF16).reshape(parts, shard_rows, summed.shap...  26.4 us
    unnamed x124, local copies, waits for them, and re-layouts  22.4 us
    all_to_all x2, starting transfers between devices, to_shards(): lax.all_to_all(summed.astype(BF16).reshape(parts, shard_rows, summed.shap...  20.8 us
  transfers between devices with their start and end apart: 60, of which 25 were waited for; matrix products, arithmetic and copies ran while one was open for 20% of the time, Pallas kernels for 6%

profile of v2, /device:TPU:5, one launch (start us, length us, event | category | flops | bytes accessed | tf_op | source)
XLA Modules:
  0.0 692.6 jit_solution(17703455726900306709)
XLA Ops:
  11.0 5.5 all-to-all-start
  18.0 5.9 collective-permute-start.2
  28.1 11.3 %collective-permute-done.2 = bf16[64,2048]{1,0:T(8,128)(2,1)} collective-permute-done((bf16[64,2048]{1,0:T(8,128)(2,1)}, bf16[64,2048]{1,0:T(8,128)(2,1)}, u32[]{:S(2)}, u32[]{:S(2)}) %collective-permute-start.2) | collective-permute-done | bytes 262176 | tf_op jit(solution)/shard_map/projection_weights/ppermute | solution.py:503
  41.6 6.0 collective-permute-done.1
  49.1 4.4 collective-permute-start.4
  58.3 7.5 %collective-permute-done.3 = bf16[512,768]{1,0:T(8,128)(2,1)} collective-permute-done((bf16[512,768]{1,0:T(8,128)(2,1)S(1)}, bf16[512,768]{1,0:T(8,128)(2,1)}, u32[]{:S(2)}, u32[]{:S(2)}) %collective-permute-start.3) | collective-permute-done | bytes 786464 | tf_op jit(solution)/shard_map/projection_weights/ppermute | solution.py:66
  66.9 5.9 collective-permute-start.5
  83.3 17.1 %all-gather.5.cloned.1.call-done = bf16[1024,2048]{1,0:T(8,128)(2,1)} async-done(((bf16[128,2048]{1,0:T(8,128)(2,1)}), bf16[1024,2048]{1,0:T(8,128)(2,1)}) %all-gather.5.cloned.1.call-update) | async-done | bytes 4194320 | tf_op jit(solution)/shard_map/tokens_gather/all_gather | solution.py:518
  102.0 4.5 all-to-all-start.1
  109.9 6.5 convolution_convert_fusion.13.lin_ref
  116.3 4.0 rope.1
  130.0 4.2 attention_forward.2
  137.8 38.7 %collective-permute-done.12 = bf16[32,2048]{1,0:T(8,128)(2,1)S(1)} collective-permute-done((bf16[32,2048]{1,0:T(8,128)(2,1)S(1)}, bf16[32,2048]{1,0:T(8,128)(2,1)S(1)}, u32[]{:S(2)}, u32[]{:S(2)}) %collective-permute-start.12) | collective-permute-done | bytes 131104 | tf_op jit(solution)/shard_map/attention/ppermute | solution.py:66
  178.6 10.0 %all-to-all-done.1 = bf16[8,64,2048]{2,1,0:T(8,128)(2,1)} async-done(((bf16[8,64,2048]{2,1,0:T(8,128)(2,1)}), bf16[8,64,2048]{2,1,0:T(8,128)(2,1)}, u32[]{:S(2)}, u32[]{:S(2)}) %all-to-all-start.1) | async-done | bytes 2097184 | tf_op jit(solution)/shard_map/attention/all_to_all | solution.py:536
  191.1 10.0 %attention_forward.3 = (bf16[1024,256]{1,0:T(8,128)(2,1)S(1)}, f32[2,1,1024]{2,1,0:T(1,128)S(1)}) custom-call(s32[2]{0:T(128)S(1)} %pad_add_fusion.place_ref, bf16[1024,256]{1,0:T(8,128)(2,1)S(1)} %copy-done.1, bf16[1024,512]{1,0:T(8,128)(2,1)S(1)} %collective-permute-done.7.refs_0_, bf16[1024,512]{1,0:T(8,128)(2,1)S(1)} %collective-permute-done.8.refs_1_, ...), custom_call_target="tpu_custom_call" | custom-call | tf_op jit(solution)/shard_map/attention/attention_forward/pallas_call | solution.py:353
  204.5 5.3 collective-permute-start.14
  209.7 45.4 %collective-permute-done.14 = bf16[512,2048]{1,0:T(8,128)(2,1)} collective-permute-done((bf16[512,2048]{1,0:T(8,128)(2,1)}, bf16[512,2048]{1,0:T(8,128)(2,1)}, u32[]{:S(2)}, u32[]{:S(2)}) %collective-permute-start.14) | collective-permute-done | bytes 2097184 | tf_op jit(solution)/shard_map/attention/ppermute | solution.py:66
  267.6 8.1 %collective-permute-done.16 = bf16[128,2048]{1,0:T(8,128)(2,1)S(1)} collective-permute-done((bf16[128,2048]{1,0:T(8,128)(2,1)S(1)}, bf16[128,2048]{1,0:T(8,128)(2,1)S(1)}, u32[]{:S(2)}, u32[]{:S(2)}) %collective-permute-start.16) | collective-permute-done | bytes 524320 | tf_op jit(solution)/shard_map/attention/ppermute | solution.py:66
  277.9 4.4 broadcast_in_dim.131
  289.4 3.3 bitcast_dynamic-update-slice_fusion.1
  295.9 12.3 %collective-permute-done.18 = bf16[256,2048]{1,0:T(8,128)(2,1)S(1)} collective-permute-done((bf16[256,2048]{1,0:T(8,128)(2,1)S(1)}, bf16[256,2048]{1,0:T(8,128)(2,1)S(1)}, u32[]{:S(2)}, u32[]{:S(2)}) %collective-permute-start.18) | collective-permute-done | bytes 1048608 | tf_op jit(solution)/shard_map/attention/ppermute | solution.py:66
  311.3 14.7 %fusion.72 = f32[1024,2048]{0,1:T(8,128)} fusion(bf16[1024,2048]{1,0:T(8,128)(2,1)} %all-gather.9.cloned.1.call-done, bf16[2048,2048]{1,0:T(8,128)(2,1)} %bitcast.29), kind=kOutput, calls=%fused_computation.166 | convolution fusion | flops 8589934592 | bytes 20971520 | tf_op jit(solution)/shard_map/feed_forward/dot_general | solution.py:52
  326.0 10.9 %multiply_convert_fusion.2 = (bf16[1024,1024]{0,1:T(8,128)(2,1)S(1)}, bf16[1024,1024]{0,1:T(8,128)(2,1)S(1)}, bf16[1024,1024]{0,1:T(8,128)(2,1)}) fusion(f32[1024,2048]{0,1:T(8,128)} %fusion.72, bf16[1024,2048]{1,0:T(8,128)(2,1)S(1)} %copy-done.54, bf16[1024,2048]{1,0:T(8,128)(2,1)} %bitcast.23), kind=kOutput, calls=%fused_computation.3 | convolution fusion | flops 4310695936 | bytes 23068672 | tf_op jit(solution)/shard_map/feed_forward/dot_general | solution.py:56
  338.9 13.0 %convolution_convert_fusion = bf16[1024,2048]{1,0:T(8,128)(2,1)} fusion(bf16[2048,2048]{1,0:T(8,128)(2,1)} %bitcast.29, bf16[1024,1024]{0,1:T(8,128)(2,1)S(1)} %get-tuple-element.152, bf16[1024,1024]{0,1:T(8,128)(2,1)S(1)} %get-tuple-element.151), kind=kOutput, calls=%fused_computation.6 | convolution fusion | flops 8600420352 | bytes 16777216 | tf_op jit(solution)/shard_map/feed_forward/dot_general | solution.py:56
  352.0 5.1 convolution_convert_fusion.4
  360.0 3.8 convolution_convert_fusion.6
  363.8 3.7 convolution_convert_fusion.5
  376.9 4.8 fusion.23
  381.7 8.5 %convolution_convert_fusion.3 = bf16[1024,2048]{1,0:T(8,128)(2,1)} fusion(bf16[1024,1024]{0,1:T(8,128)(2,1)S(1)} %copy-done.57, bf16[1024,2048]{1,0:T(8,128)(2,1)} %bitcast.23), kind=kOutput, calls=%fused_computation.9 | convolution fusion | flops 4297064448 | bytes 10485760 | tf_op jit(solution)/shard_map/feed_forward/dot_general | solution.py:52
  390.2 16.4 %reduce-scatter.7.cloned.1.call-done = bf16[128,2048]{1,0:T(8,128)(2,1)} async-done(((bf16[1024,2048]{1,0:T(8,128)(2,1)}), bf16[128,2048]{1,0:T(8,128)(2,1)}) %reduce-scatter.7.cloned.1.call-update) | async-done | bytes 524304 | tf_op jit(solution)/shard_map/feed_forward/reduce_scatter | solution.py:575
  420.5 24.3 %collective-permute-done.26 = bf16[128,2048]{1,0:T(8,128)(2,1)S(1)} collective-permute-done((bf16[128,2048]{1,0:T(8,128)(2,1)S(1)}, bf16[128,2048]{1,0:T(8,128)(2,1)S(1)}, u32[]{:S(2)}, u32[]{:S(2)}) %collective-permute-start.26) | collective-permute-done | bytes 524320 | tf_op jit(solution)/shard_map/attention_back/ppermute | solution.py:66
  445.0 24.4 %collective-permute-done.27 = bf16[128,2048]{1,0:T(8,128)(2,1)S(1)} collective-permute-done((bf16[128,2048]{1,0:T(8,128)(2,1)S(1)}, bf16[128,2048]{1,0:T(8,128)(2,1)S(1)}, u32[]{:S(2)}, u32[]{:S(2)}) %collective-permute-start.27) | collective-permute-done | bytes 524320 | tf_op jit(solution)/shard_map/attention_back/ppermute | solution.py:66
  470.2 3.7 add_convert_fusion.1
  475.4 8.2 %all-to-all-start.2 = ((bf16[8,64,2048]{2,1,0:T(8,128)(2,1)}), bf16[8,64,2048]{2,1,0:T(8,128)(2,1)S(1)}, u32[]{:S(2)}, u32[]{:S(2)}) async-start(bf16[8,64,2048]{2,1,0:T(8,128)(2,1)} %bitcast.134), calls=%async_computation.5 | async-start | bytes 4194304 | tf_op jit(solution)/shard_map/attention_back/all_to_all | solution.py:598
  483.6 3.8 convolution_convert_fusion.17.do_ref
  487.5 13.5 %attention_backward.2 = (f32[2,128,1024]{2,1,0:T(8,128)S(1)}, bf16[1024,512]{1,0:T(8,128)(2,1)S(1)}, bf16[1024,512]{1,0:T(8,128)(2,1)S(1)}, bf16[1024,512]{1,0:T(8,128)(2,1)S(1)}) custom-call(s32[2]{0:T(128)S(1)} %pad_add_fusion.place_ref, bf16[1024,256]{1,0:T(8,128)(2,1)S(1)} %copy-done.1, bf16[1024,256]{1,0:T(8,128)(2,1)S(1)} %get-tuple-element.96.o_ref, ...), custom_call_target="tpu_custom_call" | custom-call | tf_op jit(solution)/shard_map/attention_back/attention_backward/pallas_call | solution.py:435
  504.7 4.1 collective-permute-start.30
  508.8 23.8 %collective-permute-done.28.refs_1_ = bf16[1024,512]{1,0:T(8,128)(2,1)S(1)} collective-permute-done((bf16[1024,512]{1,0:T(8,128)(2,1)S(1)}, bf16[1024,512]{1,0:T(8,128)(2,1)S(1)}, u32[]{:S(2)}, u32[]{:S(2)}) %collective-permute-start.28) | collective-permute-done | bytes 1048608 | tf_op jit(solution)/shard_map/attention_back/ppermute | solution.py:66
  534.6 26.4 %all-to-all-done.2.in_ref = bf16[8,64,2048]{2,1,0:T(8,128)(2,1)S(1)} async-done(((bf16[8,64,2048]{2,1,0:T(8,128)(2,1)}), bf16[8,64,2048]{2,1,0:T(8,128)(2,1)S(1)}, u32[]{:S(2)}, u32[]{:S(2)}) %all-to-all-start.2) | async-done | bytes 2097184 | tf_op jit(solution)/shard_map/attention_back/all_to_all | solution.py:598
  564.5 6.1 attention_backward.3
  572.5 5.6 unrope.1
  578.2 7.9 %convolution_convert_fusion.2 = bf16[1024,2048]{1,0:T(8,128)(2,1)} fusion(bf16[1024,768]{1,0:T(8,128)(2,1)} %unrope.1, bf16[2048,768]{1,0:T(8,128)(2,1)} %bitcast.8), kind=kOutput, calls=%fused_computation.8 | convolution fusion | flops 3223322624 | bytes 8912896 | tf_op jit(solution)/shard_map/attention_back/dot_general | solution.py:56
  605.3 4.3 collective-permute-done.32
  614.3 3.7 collective-permute-done.31
  619.5 7.2 %collective-permute-done.33 = bf16[256,768]{1,0:T(8,128)(2,1)S(1)} collective-permute-done((bf16[256,768]{1,0:T(8,128)(2,1)S(1)}, bf16[256,768]{1,0:T(8,128)(2,1)S(1)}, u32[]{:S(2)}, u32[]{:S(2)}) %collective-permute-start.33) | collective-permute-done | bytes 393248 | tf_op jit(solution)/shard_map/weight_grads/ppermute | solution.py:66
  629.5 12.7 %all-to-all-start.3 = ((bf16[8,64,768]{2,1,0:T(8,128)(2,1)}), bf16[8,64,768]{2,1,0:T(8,128)(2,1)}, u32[]{:S(2)}, u32[]{:S(2)}) async-start(bf16[8,64,768]{2,1,0:T(8,128)(2,1)} %bitcast.140), calls=%async_computation.7 | async-start | bytes 1572864 | tf_op jit(solution)/shard_map/weight_grads/all_to_all | solution.py:598
  645.9 7.1 %collective-permute-start.43 = (bf16[64,2048]{1,0:T(8,128)(2,1)S(1)}, bf16[64,2048]{1,0:T(8,128)(2,1)S(1)}, u32[]{:S(2)}, u32[]{:S(2)}) collective-permute-start(bf16[64,2048]{1,0:T(8,128)(2,1)S(1)} %pad_maximum_fusion.6), channel_id=1, source_target_pairs={{0,0},{1,4},{2,8},{3,12},{4,16},{5,20},{6,24},{7,28},{8,1},{9,5},{... | collective-permute-start | bytes 786440 | tf_op jit(solution)/shard_map/attention_back/ppermute | solution.py:639
  653.0 17.9 %collective-permute-done.43 = bf16[64,2048]{1,0:T(8,128)(2,1)S(1)} collective-permute-done((bf16[64,2048]{1,0:T(8,128)(2,1)S(1)}, bf16[64,2048]{1,0:T(8,128)(2,1)S(1)}, u32[]{:S(2)}, u32[]{:S(2)}) %collective-permute-start.43) | collective-permute-done | bytes 262176 | tf_op jit(solution)/shard_map/attention_back/ppermute | solution.py:639
  (326 shorter events, 170.6 us)
Async XLA Ops:
  11.0 36.6 %all-to-all-start = ((bf16[8,64,768]{2,1,0:T(8,128)(2,1)}), bf16[8,64,768]{2,1,0:T(8,128)(2,1)S(1)}, u32[]{:S(2)}, u32[]{:S(2)}) async-start(bf16[8,64,768]{2,1,0:T(8,128)(2,1)} %collect.2), calls=%async_computation | async-start | bytes 1572864 | tf_op jit(solution)/shard_map/projection_weights/all_to_all | solution.py:500
  16.5 83.9 %all-gather.5.cloned.1.call-start = ((), (), s32[]{:S(2)}) async-start(), calls=%async_computation.8 | async-start | bytes 4718592 | tf_op jit(solution)/shard_map/tokens_gather/all_gather | solution.py:518
  16.5 25.0 %collective-permute-start = (bf16[256,2048]{1,0:T(8,128)(2,1)}, bf16[256,2048]{1,0:T(8,128)(2,1)S(1)}, u32[]{:S(2)}, u32[]{:S(2)}) collective-permute-start(bf16[256,2048]{1,0:T(8,128)(2,1)} %param.18), channel_id=1, source_target_pairs={{0,8},{8,0},{16,24},{24,16},{1,9},{9,1},{17,25},{25,17},{2,10},{10... | collective-permute-start | bytes 3145736 | tf_op jit(solution)/shard_map/projection_weights/ppermute | solution.py:66
  17.8 29.9 %collective-permute-start.1 = (bf16[256,2048]{1,0:T(8,128)(2,1)}, bf16[256,2048]{1,0:T(8,128)(2,1)S(1)}, u32[]{:S(2)}, u32[]{:S(2)}) collective-permute-start(bf16[256,2048]{1,0:T(8,128)(2,1)} %param.18), channel_id=1, source_target_pairs={{0,16},{8,24},{16,0},{24,8},{1,17},{9,25},{17,1},{25,9},{2,18},{10... | collective-permute-start | bytes 3145736 | tf_op jit(solution)/shard_map/projection_weights/ppermute | solution.py:66
  18.0 21.5 %collective-permute-start.2 = (bf16[64,2048]{1,0:T(8,128)(2,1)}, bf16[64,2048]{1,0:T(8,128)(2,1)}, u32[]{:S(2)}, u32[]{:S(2)}) collective-permute-start(bf16[64,2048]{1,0:T(8,128)(2,1)} %param.15), channel_id=1, source_target_pairs={{0,0},{4,1},{8,2},{12,3},{16,4},{20,5},{24,6},{28,7},{1,8},{5,9},{... | collective-permute-start | bytes 786440 | tf_op jit(solution)/shard_map/projection_weights/ppermute | solution.py:503
  47.6 141.0 %all-gather.7.cloned.1.call-start = ((), (), s32[]{:S(2)}) async-start(), calls=%async_computation.9 | async-start | bytes 4718592 | tf_op jit(solution)/shard_map/attention/all_gather | solution.py:542
  48.4 17.5 %collective-permute-start.3 = (bf16[512,768]{1,0:T(8,128)(2,1)S(1)}, bf16[512,768]{1,0:T(8,128)(2,1)}, u32[]{:S(2)}, u32[]{:S(2)}) collective-permute-start(bf16[512,768]{1,0:T(8,128)(2,1)S(1)} %bitcast.137), channel_id=1, source_target_pairs={{0,8},{8,0},{16,24},{24,16},{1,9},{9,1},{17,25},{25,17},{2,10},{10... | collective-permute-start | bytes 2359304 | tf_op jit(solution)/shard_map/projection_weights/ppermute | solution.py:66
  49.1 23.7 %collective-permute-start.4 = (bf16[512,768]{1,0:T(8,128)(2,1)S(1)}, bf16[512,768]{1,0:T(8,128)(2,1)}, u32[]{:S(2)}, u32[]{:S(2)}) collective-permute-start(bf16[512,768]{1,0:T(8,128)(2,1)S(1)} %bitcast.138), channel_id=1, source_target_pairs={{0,16},{8,24},{16,0},{24,8},{1,17},{9,25},{17,1},{25,9},{2,18},{10... | collective-permute-start | bytes 2359304 | tf_op jit(solution)/shard_map/projection_weights/ppermute | solution.py:66
  102.0 86.6 %all-to-all-start.1 = ((bf16[8,64,2048]{2,1,0:T(8,128)(2,1)}), bf16[8,64,2048]{2,1,0:T(8,128)(2,1)}, u32[]{:S(2)}, u32[]{:S(2)}) async-start(bf16[8,64,2048]{2,1,0:T(8,128)(2,1)} %collect.3), calls=%async_computation.1 | async-start | bytes 4194304 | tf_op jit(solution)/shard_map/attention/all_to_all | solution.py:536
  106.6 149.4 %reduce-scatter.5.cloned.1.call-start = ((), (), s32[]{:S(2)}) async-start(), calls=%async_computation.10 | async-start | bytes 4718592 | tf_op jit(solution)/shard_map/attention/reduce_scatter | solution.py:552
  122.9 53.7 %collective-permute-start.7 = (bf16[1024,512]{1,0:T(8,128)(2,1)}, bf16[1024,512]{1,0:T(8,128)(2,1)S(1)}, u32[]{:S(2)}, u32[]{:S(2)}) collective-permute-start(bf16[1024,512]{1,0:T(8,128)(2,1)} %get-tuple-element.82.refs_0_), channel_id=1, source_target_pairs={{0,8},{16,24},{1,9},{17,25},{2,10},{18,26},{3,11},{19,27},{4,12},{... | collective-permute-start | bytes 3145736 | tf_op jit(solution)/shard_map/attention/ppermute | solution.py:66
  125.1 51.5 %collective-permute-start.8 = (bf16[1024,512]{1,0:T(8,128)(2,1)}, bf16[1024,512]{1,0:T(8,128)(2,1)S(1)}, u32[]{:S(2)}, u32[]{:S(2)}) collective-permute-start(bf16[1024,512]{1,0:T(8,128)(2,1)} %get-tuple-element.82.refs_0_), channel_id=1, source_target_pairs={{0,16},{8,24},{1,17},{9,25},{2,18},{10,26},{3,19},{11,27},{4,20},{... | collective-permute-start | bytes 3145736 | tf_op jit(solution)/shard_map/attention/ppermute | solution.py:66
  126.4 51.1 %collective-permute-start.9 = (bf16[1024,512]{1,0:T(8,128)(2,1)}, bf16[1024,512]{1,0:T(8,128)(2,1)S(1)}, u32[]{:S(2)}, u32[]{:S(2)}) collective-permute-start(bf16[1024,512]{1,0:T(8,128)(2,1)} %get-tuple-element.82.refs_0_), channel_id=1, source_target_pairs={{0,24},{8,16},{1,25},{9,17},{2,26},{10,18},{3,27},{11,19},{4,28},{... | collective-permute-start | bytes 3145736 | tf_op jit(solution)/shard_map/attention/ppermute | solution.py:66
  134.3 42.2 %collective-permute-start.12 = (bf16[32,2048]{1,0:T(8,128)(2,1)S(1)}, bf16[32,2048]{1,0:T(8,128)(2,1)S(1)}, u32[]{:S(2)}, u32[]{:S(2)}) collective-permute-start(bf16[32,2048]{1,0:T(8,128)(2,1)S(1)} %slice.162), channel_id=1, source_target_pairs={{0,16},{8,24},{16,0},{24,8},{1,17},{9,25},{17,1},{25,9},{2,18},{10... | collective-permute-start | bytes 393224 | tf_op jit(solution)/shard_map/attention/ppermute | solution.py:66
  136.6 40.0 %collective-permute-start.13 = (bf16[32,2048]{1,0:T(8,128)(2,1)S(1)}, bf16[32,2048]{1,0:T(8,128)(2,1)S(1)}, u32[]{:S(2)}, u32[]{:S(2)}) collective-permute-start(bf16[32,2048]{1,0:T(8,128)(2,1)S(1)} %slice.163), channel_id=1, source_target_pairs={{0,8},{8,0},{16,24},{24,16},{1,9},{9,1},{17,25},{25,17},{2,10},{10... | collective-permute-start | bytes 393224 | tf_op jit(solution)/shard_map/attention/ppermute | solution.py:66
  204.4 106.9 %all-gather.9.cloned.1.call-start = ((), (), s32[]{:S(2)}) async-start(), calls=%async_computation.11 | async-start | bytes 4718592 | tf_op jit(solution)/shard_map/feed_forward/all_gather | solution.py:562
  204.5 50.7 %collective-permute-start.14 = (bf16[512,2048]{1,0:T(8,128)(2,1)}, bf16[512,2048]{1,0:T(8,128)(2,1)}, u32[]{:S(2)}, u32[]{:S(2)}) collective-permute-start(bf16[512,2048]{1,0:T(8,128)(2,1)} %bitcast.9), channel_id=1, source_target_pairs={{0,8},{8,0},{16,24},{24,16},{1,9},{9,1},{17,25},{25,17},{2,10},{10... | collective-permute-start | bytes 6291464 | tf_op jit(solution)/shard_map/attention/ppermute | solution.py:66
  209.7 46.3 %collective-permute-start.15 = (bf16[512,2048]{1,0:T(8,128)(2,1)}, bf16[512,2048]{1,0:T(8,128)(2,1)}, u32[]{:S(2)}, u32[]{:S(2)}) collective-permute-start(bf16[512,2048]{1,0:T(8,128)(2,1)} %bitcast.9), channel_id=1, source_target_pairs={{0,16},{8,24},{16,0},{24,8},{1,17},{9,25},{17,1},{25,9},{2,18},{10... | collective-permute-start | bytes 6291464 | tf_op jit(solution)/shard_map/attention/ppermute | solution.py:66
  260.7 145.9 %reduce-scatter.7.cloned.1.call-start = ((), (), s32[]{:S(2)}) async-start(), calls=%async_computation.12 | async-start | bytes 4718592 | tf_op jit(solution)/shard_map/feed_forward/reduce_scatter | solution.py:575
  286.8 21.4 %collective-permute-start.18 = (bf16[256,2048]{1,0:T(8,128)(2,1)S(1)}, bf16[256,2048]{1,0:T(8,128)(2,1)S(1)}, u32[]{:S(2)}, u32[]{:S(2)}) collective-permute-start(bf16[256,2048]{1,0:T(8,128)(2,1)S(1)} %slice.126), channel_id=1, source_target_pairs={{0,16},{8,24},{16,0},{24,8},{1,17},{9,25},{17,1},{25,9},{2,18},{10... | collective-permute-start | bytes 3145736 | tf_op jit(solution)/shard_map/attention/ppermute | solution.py:66
  289.1 21.0 %collective-permute-start.19 = (bf16[256,2048]{1,0:T(8,128)(2,1)S(1)}, bf16[256,2048]{1,0:T(8,128)(2,1)S(1)}, u32[]{:S(2)}, u32[]{:S(2)}) collective-permute-start(bf16[256,2048]{1,0:T(8,128)(2,1)S(1)} %slice.127), channel_id=1, source_target_pairs={{0,8},{8,0},{16,24},{24,16},{1,9},{9,1},{17,25},{25,17},{2,10},{10... | collective-permute-start | bytes 3145736 | tf_op jit(solution)/shard_map/attention/ppermute | solution.py:66
  351.9 118.3 %all-gather.11.cloned.1.call-start = ((), (), s32[]{:S(2)}) async-start(), calls=%async_computation.13 | async-start | bytes 4718592 | tf_op jit(solution)/shard_map/attention_back/all_gather | solution.py:607
  358.6 49.2 %collective-permute-start.20 = (bf16[256,2048]{1,0:T(8,128)(2,1)}, bf16[256,2048]{1,0:T(8,128)(2,1)}, u32[]{:S(2)}, u32[]{:S(2)}) collective-permute-start(bf16[256,2048]{1,0:T(8,128)(2,1)} %get-tuple-element.159), channel_id=1, source_target_pairs={{0,8},{8,0},{16,24},{24,16},{1,9},{9,1},{17,25},{25,17},{2,10},{10... | collective-permute-start | bytes 3145736 | tf_op jit(solution)/shard_map/feed_forward/ppermute | solution.py:66
  358.6 49.2 %collective-permute-start.21 = (bf16[256,2048]{1,0:T(8,128)(2,1)}, bf16[256,2048]{1,0:T(8,128)(2,1)}, u32[]{:S(2)}, u32[]{:S(2)}) collective-permute-start(bf16[256,2048]{1,0:T(8,128)(2,1)} %get-tuple-element.158), channel_id=1, source_target_pairs={{0,16},{8,24},{16,0},{24,8},{1,17},{9,25},{17,1},{25,9},{2,18},{10... | collective-permute-start | bytes 3145736 | tf_op jit(solution)/shard_map/feed_forward/ppermute | solution.py:66
  410.0 269.9 %reduce-scatter.9.cloned.1.call-start = ((), (), s32[]{:S(2)}) async-start(), calls=%async_computation.14 | async-start | bytes 4718592 | tf_op jit(solution)/shard_map/attention_back/reduce_scatter | solution.py:615
  411.5 57.9 %collective-permute-start.22 = (bf16[256,2048]{1,0:T(8,128)(2,1)S(1)}, bf16[256,2048]{1,0:T(8,128)(2,1)}, u32[]{:S(2)}, u32[]{:S(2)}) collective-permute-start(bf16[256,2048]{1,0:T(8,128)(2,1)S(1)} %slice.130), channel_id=1, source_target_pairs={{0,8},{8,0},{16,24},{24,16},{1,9},{9,1},{17,25},{25,17},{2,10},{10... | collective-permute-start | bytes 3145736 | tf_op jit(solution)/shard_map/attention_back/ppermute | solution.py:66
  414.1 55.3 %collective-permute-start.23 = (bf16[256,2048]{1,0:T(8,128)(2,1)S(1)}, bf16[256,2048]{1,0:T(8,128)(2,1)}, u32[]{:S(2)}, u32[]{:S(2)}) collective-permute-start(bf16[256,2048]{1,0:T(8,128)(2,1)S(1)} %slice.131), channel_id=1, source_target_pairs={{0,16},{8,24},{16,0},{24,8},{1,17},{9,25},{17,1},{25,9},{2,18},{10... | collective-permute-start | bytes 3145736 | tf_op jit(solution)/shard_map/attention_back/ppermute | solution.py:66
  415.9 53.5 %collective-permute-start.24 = (bf16[256,2048]{1,0:T(8,128)(2,1)S(1)}, bf16[256,2048]{1,0:T(8,128)(2,1)S(1)}, u32[]{:S(2)}, u32[]{:S(2)}) collective-permute-start(bf16[256,2048]{1,0:T(8,128)(2,1)S(1)} %add_convert_fusion.3), channel_id=1, source_target_pairs={{0,16},{8,24},{16,0},{24,8},{1,17},{9,25},{17,1},{25,9},{2,18},{10... | collective-permute-start | bytes 3145736 | tf_op jit(solution)/shard_map/attention_back/ppermute | solution.py:66
  417.3 27.5 %collective-permute-start.26 = (bf16[128,2048]{1,0:T(8,128)(2,1)S(1)}, bf16[128,2048]{1,0:T(8,128)(2,1)S(1)}, u32[]{:S(2)}, u32[]{:S(2)}) collective-permute-start(bf16[128,2048]{1,0:T(8,128)(2,1)S(1)} %get-tuple-element.163), channel_id=1, source_target_pairs={{0,8},{8,0},{16,24},{24,16},{1,9},{9,1},{17,25},{25,17},{2,10},{10... | collective-permute-start | bytes 1572872 | tf_op jit(solution)/shard_map/attention_back/ppermute | solution.py:66
  419.4 50.8 %collective-permute-start.25 = (bf16[256,2048]{1,0:T(8,128)(2,1)S(1)}, bf16[256,2048]{1,0:T(8,128)(2,1)S(1)}, u32[]{:S(2)}, u32[]{:S(2)}) collective-permute-start(bf16[256,2048]{1,0:T(8,128)(2,1)S(1)} %add_convert_fusion.2), channel_id=1, source_target_pairs={{0,8},{8,0},{16,24},{24,16},{1,9},{9,1},{17,25},{25,17},{2,10},{10... | collective-permute-start | bytes 3145736 | tf_op jit(solution)/shard_map/attention_back/ppermute | solution.py:66
  444.8 24.6 %collective-permute-start.27 = (bf16[128,2048]{1,0:T(8,128)(2,1)S(1)}, bf16[128,2048]{1,0:T(8,128)(2,1)S(1)}, u32[]{:S(2)}, u32[]{:S(2)}) collective-permute-start(bf16[128,2048]{1,0:T(8,128)(2,1)S(1)} %get-tuple-element.162), channel_id=1, source_target_pairs={{0,16},{8,24},{16,0},{24,8},{1,17},{9,25},{17,1},{25,9},{2,18},{10... | collective-permute-start | bytes 1572872 | tf_op jit(solution)/shard_map/attention_back/ppermute | solution.py:66
  475.4 85.6 %all-to-all-start.2 = ((bf16[8,64,2048]{2,1,0:T(8,128)(2,1)}), bf16[8,64,2048]{2,1,0:T(8,128)(2,1)S(1)}, u32[]{:S(2)}, u32[]{:S(2)}) async-start(bf16[8,64,2048]{2,1,0:T(8,128)(2,1)} %bitcast.134), calls=%async_computation.5 | async-start | bytes 4194304 | tf_op jit(solution)/shard_map/attention_back/all_to_all | solution.py:598
  483.6 197.5 %reduce-scatter.11.cloned.1.call-start = ((), (), s32[]{:S(2)}) async-start(), calls=%async_computation.15 | async-start | bytes 4718592 | tf_op jit(solution)/shard_map/attention_back/reduce_scatter | solution.py:650
  501.9 30.7 %collective-permute-start.28 = (bf16[1024,512]{1,0:T(8,128)(2,1)S(1)}, bf16[1024,512]{1,0:T(8,128)(2,1)S(1)}, u32[]{:S(2)}, u32[]{:S(2)}) collective-permute-start(bf16[1024,512]{1,0:T(8,128)(2,1)S(1)} %get-tuple-element.119), channel_id=1, source_target_pairs={{8,0},{24,16},{9,1},{25,17},{10,2},{26,18},{11,3},{27,19},{12,4},{... | collective-permute-start | bytes 3145736 | tf_op jit(solution)/shard_map/attention_back/ppermute | solution.py:66
  503.2 29.4 %collective-permute-start.29 = (bf16[1024,512]{1,0:T(8,128)(2,1)S(1)}, bf16[1024,512]{1,0:T(8,128)(2,1)S(1)}, u32[]{:S(2)}, u32[]{:S(2)}) collective-permute-start(bf16[1024,512]{1,0:T(8,128)(2,1)S(1)} %get-tuple-element.120), channel_id=1, source_target_pairs={{16,0},{24,8},{17,1},{25,9},{18,2},{26,10},{19,3},{27,11},{20,4},{... | collective-permute-start | bytes 3145736 | tf_op jit(solution)/shard_map/attention_back/ppermute | solution.py:66
  504.7 29.9 %collective-permute-start.30 = (bf16[1024,512]{1,0:T(8,128)(2,1)S(1)}, bf16[1024,512]{1,0:T(8,128)(2,1)}, u32[]{:S(2)}, u32[]{:S(2)}) collective-permute-start(bf16[1024,512]{1,0:T(8,128)(2,1)S(1)} %get-tuple-element.121), channel_id=1, source_target_pairs={{16,8},{24,0},{17,9},{25,1},{18,10},{26,2},{19,11},{27,3},{20,12},... | collective-permute-start | bytes 3145736 | tf_op jit(solution)/shard_map/attention_back/ppermute | solution.py:66
  592.0 50.2 %collective-permute-start.37 = (bf16[32,2048]{1,0:T(8,128)(2,1)}, bf16[32,2048]{1,0:T(8,128)(2,1)S(1)}, u32[]{:S(2)}, u32[]{:S(2)}) collective-permute-start(bf16[32,2048]{1,0:T(8,128)(2,1)} %slice.175), channel_id=1, source_target_pairs={{0,8},{8,0},{16,24},{24,16},{1,9},{9,1},{17,25},{25,17},{2,10},{10... | collective-permute-start | bytes 393224 | tf_op jit(solution)/shard_map/attention_back/ppermute | solution.py:66
  592.6 19.9 %collective-permute-start.41 = (bf16[32,2048]{1,0:T(8,128)(2,1)S(1)}, bf16[32,2048]{1,0:T(8,128)(2,1)S(1)}, u32[]{:S(2)}, u32[]{:S(2)}) collective-permute-start(bf16[32,2048]{1,0:T(8,128)(2,1)S(1)} %get-tuple-element.171), channel_id=1, source_target_pairs={{0,16},{8,24},{16,0},{24,8},{1,17},{9,25},{17,1},{25,9},{2,18},{10... | collective-permute-start | bytes 393224 | tf_op jit(solution)/shard_map/attention_back/ppermute | solution.py:66
  611.2 15.4 %collective-permute-start.33 = (bf16[256,768]{1,0:T(8,128)(2,1)S(1)}, bf16[256,768]{1,0:T(8,128)(2,1)S(1)}, u32[]{:S(2)}, u32[]{:S(2)}) collective-permute-start(bf16[256,768]{1,0:T(8,128)(2,1)S(1)} %add_convert_fusion.7), channel_id=1, source_target_pairs={{0,16},{8,24},{16,0},{24,8},{1,17},{9,25},{17,1},{25,9},{2,18},{10... | collective-permute-start | bytes 1179656 | tf_op jit(solution)/shard_map/weight_grads/ppermute | solution.py:66
  618.0 24.9 %collective-permute-start.40 = (bf16[32,2048]{1,0:T(8,128)(2,1)}, bf16[32,2048]{1,0:T(8,128)(2,1)}, u32[]{:S(2)}, u32[]{:S(2)}) collective-permute-start(bf16[32,2048]{1,0:T(8,128)(2,1)} %slice.179), channel_id=1, source_target_pairs={{0,16},{8,24},{16,0},{24,8},{1,17},{9,25},{17,1},{25,9},{2,18},{10... | collective-permute-start | bytes 393224 | tf_op jit(solution)/shard_map/attention_back/ppermute | solution.py:66
  619.2 52.6 %collective-permute-start.45 = (bf16[128,2048]{1,0:T(8,128)(2,1)}, bf16[128,2048]{1,0:T(8,128)(2,1)}, u32[]{:S(2)}, u32[]{:S(2)}) collective-permute-start(bf16[128,2048]{1,0:T(8,128)(2,1)} %add_convert_fusion.5), channel_id=1, source_target_pairs={{0,16},{8,24},{16,0},{24,8},{1,17},{9,25},{17,1},{25,9},{2,18},{10... | collective-permute-start | bytes 1572872 | tf_op jit(solution)/shard_map/attention_back/ppermute | solution.py:66
  626.6 17.0 %collective-permute-start.39 = (bf16[32,2048]{1,0:T(8,128)(2,1)S(1)}, bf16[32,2048]{1,0:T(8,128)(2,1)}, u32[]{:S(2)}, u32[]{:S(2)}) collective-permute-start(bf16[32,2048]{1,0:T(8,128)(2,1)S(1)} %add_convert_fusion.9), channel_id=1, source_target_pairs={{0,16},{8,24},{16,0},{24,8},{1,17},{9,25},{17,1},{25,9},{2,18},{10... | collective-permute-start | bytes 393224 | tf_op jit(solution)/shard_map/attention_back/ppermute | solution.py:66
  627.9 16.9 %collective-permute-start.42 = (bf16[32,2048]{1,0:T(8,128)(2,1)S(1)}, bf16[32,2048]{1,0:T(8,128)(2,1)}, u32[]{:S(2)}, u32[]{:S(2)}) collective-permute-start(bf16[32,2048]{1,0:T(8,128)(2,1)S(1)} %add_convert_fusion.8), channel_id=1, source_target_pairs={{0,8},{8,0},{16,24},{24,16},{1,9},{9,1},{17,25},{25,17},{2,10},{10... | collective-permute-start | bytes 393224 | tf_op jit(solution)/shard_map/attention_back/ppermute | solution.py:66
  629.5 48.0 %all-to-all-start.3 = ((bf16[8,64,768]{2,1,0:T(8,128)(2,1)}), bf16[8,64,768]{2,1,0:T(8,128)(2,1)}, u32[]{:S(2)}, u32[]{:S(2)}) async-start(bf16[8,64,768]{2,1,0:T(8,128)(2,1)} %bitcast.140), calls=%async_computation.7 | async-start | bytes 1572864 | tf_op jit(solution)/shard_map/weight_grads/all_to_all | solution.py:598
  642.2 29.6 %collective-permute-start.44 = (bf16[128,2048]{1,0:T(8,128)(2,1)}, bf16[128,2048]{1,0:T(8,128)(2,1)S(1)}, u32[]{:S(2)}, u32[]{:S(2)}) collective-permute-start(bf16[128,2048]{1,0:T(8,128)(2,1)} %slice.155), channel_id=1, source_target_pairs={{0,8},{8,0},{16,24},{24,16},{1,9},{9,1},{17,25},{25,17},{2,10},{10... | collective-permute-start | bytes 1572872 | tf_op jit(solution)/shard_map/attention_back/ppermute | solution.py:66
  642.9 28.9 %collective-permute-start.47 = (bf16[128,2048]{1,0:T(8,128)(2,1)}, bf16[128,2048]{1,0:T(8,128)(2,1)S(1)}, u32[]{:S(2)}, u32[]{:S(2)}) collective-permute-start(bf16[128,2048]{1,0:T(8,128)(2,1)} %add_convert_fusion.4), channel_id=1, source_target_pairs={{0,8},{8,0},{16,24},{24,16},{1,9},{9,1},{17,25},{25,17},{2,10},{10... | collective-permute-start | bytes 1572872 | tf_op jit(solution)/shard_map/attention_back/ppermute | solution.py:66
  643.7 28.1 %collective-permute-start.46 = (bf16[128,2048]{1,0:T(8,128)(2,1)}, bf16[128,2048]{1,0:T(8,128)(2,1)S(1)}, u32[]{:S(2)}, u32[]{:S(2)}) collective-permute-start(bf16[128,2048]{1,0:T(8,128)(2,1)} %slice.158), channel_id=1, source_target_pairs={{0,16},{8,24},{16,0},{24,8},{1,17},{9,25},{17,1},{25,9},{2,18},{10... | collective-permute-start | bytes 1572872 | tf_op jit(solution)/shard_map/attention_back/ppermute | solution.py:66
  645.9 25.0 %collective-permute-start.43 = (bf16[64,2048]{1,0:T(8,128)(2,1)S(1)}, bf16[64,2048]{1,0:T(8,128)(2,1)S(1)}, u32[]{:S(2)}, u32[]{:S(2)}) collective-permute-start(bf16[64,2048]{1,0:T(8,128)(2,1)S(1)} %pad_maximum_fusion.6), channel_id=1, source_target_pairs={{0,0},{1,4},{2,8},{3,12},{4,16},{5,20},{6,24},{7,28},{8,1},{9,5},{... | collective-permute-start | bytes 786440 | tf_op jit(solution)/shard_map/attention_back/ppermute | solution.py:639
  (74 other events, 1263.8 us)
Sparse Core Ops, SparseCore 0:
  47.8 52.5 all-gather.4
  102.5 84.0 all-gather.6
  204.5 50.8 reduce-scatter.4
  260.9 47.2 all-gather.8
  352.0 54.6 reduce-scatter.6
  410.1 47.8 all-gather.10
  470.4 95.9 reduce-scatter.8
  586.2 46.1 reduce-scatter.10

commit v3 on v2

--- a/solution.py
+++ b/solution.py
@@ -141,7 +141,11 @@
 
 
 def sum_to_owner(terms):
-    return sum_end(terms, sum_own(terms), sum_far(terms, sum_pass(terms)))
+    arrived = [swapped(term, mask) for mask, term in enumerate(terms) if mask]
+    total = terms[0]
+    for part in arrived:
+        total = total + part.astype(F32)
+    return total
 
 
 def collect_kernel(*refs, parts, blocks, chunk):
@@ -458,6 +462,51 @@
     )(place, query, out, grad, lse, *blocks, *([dq] if started else []))
 
 
+def feed_kernel(
+    normed_ref, grad_ref, both_ref, down_ref, mixed_ref, back_ref, out_ref, *, columns
+):
+    hidden = down_ref.shape[0]
+    for first in range(0, hidden, columns):
+        gates = slice(first, first + columns)
+        ups = slice(hidden + first, hidden + first + columns)
+        gate_act = dot(normed_ref[...], both_ref[:, gates])
+        up_act = dot(normed_ref[...], both_ref[:, ups])
+        mixed_grad = dot_transposed(grad_ref[...], down_ref[gates, :])
+        sigmoid_gate = 1.0 / (1.0 + jnp.exp(-gate_act))
+        silu_gate = gate_act * sigmoid_gate
+        mixed_ref[:, gates] = (silu_gate * up_act).astype(BF16)
+        slope = sigmoid_gate * (1.0 + gate_act * (1.0 - sigmoid_gate))
+        back_ref[:, gates] = (mixed_grad * up_act * slope).astype(BF16)
+        back_ref[:, ups] = (mixed_grad * silu_gate).astype(BF16)
+    out_ref[...] = dot_transposed(back_ref[...], both_ref[...]).astype(BF16)
+
+
+def feed_forward(normed, grad, both, down):
+    rows, width = normed.shape
+    hidden = down.shape[0]
+    tile = min(256, rows)
+
+    def by_rows(columns):
+        return pl.BlockSpec((tile, columns), lambda i: (i, 0))
+
+    def whole(array):
+        return pl.BlockSpec(array.shape, lambda i: (0, 0), pipeline_mode=pl.Buffered(1))
+
+    return pl.pallas_call(
+        functools.partial(feed_kernel, columns=min(256, hidden)),
+        grid=(rows // tile,),
+        in_specs=[by_rows(width), by_rows(width), whole(both), whole(down)],
+        out_specs=[by_rows(hidden), by_rows(2 * hidden), by_rows(width)],
+        out_shape=[
+            jax.ShapeDtypeStruct((rows, hidden), BF16),
+            jax.ShapeDtypeStruct((rows, 2 * hidden), BF16),
+            jax.ShapeDtypeStruct((rows, width), BF16),
+        ],
+        compiler_params=pltpu.CompilerParams(vmem_limit_bytes=VMEM_LIMIT),
+        name="feed_forward",
+    )(normed, grad, both, down)
+
+
 def local(
     tokens,
     lengths,
@@ -495,33 +544,35 @@
     )
     valid = (me * block_rows + row_ids % block_rows < my_length).astype(F32)[:, None]
 
+    normed_one, inverse_one = normalize_rows(inputs)
     with jax.named_scope("projection_weights"):
         stacked = collect([query_weight, key_weight, value_weight], parts, 1, width)
         stacked = lax.all_to_all(stacked, "head", split_axis=0, concat_axis=0, tiled=True)
         stacked = stacked.reshape(band_rows, 3 * width)
-        down_near = send_near(down_weight)
-        output_rows = lax.ppermute(
-            output_weight,
-            ("blk", "head"),
-            [(h * blocks + b, b * parts + h) for b in range(blocks) for h in range(parts)],
-        )
-        stacked, down_near, output_rows = lax.optimization_barrier(
-            (stacked, down_near, output_rows)
-        )
+        normed_start = after(normed_one.astype(BF16), stacked)
         near = send_near(stacked)
         projection = gather_blk(stacked, near + send_far(near)).reshape(model_width, 3 * width)
 
     with jax.named_scope("tokens_gather"):
-        normed_one, inverse_one = normalize_rows(inputs)
         upstream = cotangent[0].astype(F32) * valid
         upstream_low = upstream.astype(BF16)
         normed_group = lax.all_gather(
-            after(normed_one.astype(BF16), stacked), "head", axis=0, tiled=True
+            normed_start, "head", axis=0, tiled=True
         )
 
     with jax.named_scope("hidden_weights"):
         both = collect([gate_weight, up_weight], parts, blocks, chunk)
-        normed_group, projection = lax.optimization_barrier((normed_group, projection))
+        output_rows = lax.ppermute(
+            after(output_weight, stacked),
+            ("blk", "head"),
+            [(h * blocks + b, b * parts + h) for b in range(blocks) for h in range(parts)],
+        )
+        output_near = send_near(output_rows)
+        output = gather_blk(output_rows, output_near + send_far(output_near))
+        output = output.reshape(width, model_width)
+        normed_group, projection, output = lax.optimization_barrier(
+            (normed_group, projection, output)
+        )
 
     cosine, sine = rotary_tables(me * block_rows + jnp.arange(block_rows))
     with jax.named_scope("projections"):
@@ -534,46 +585,39 @@
             place, query, [key_value], [0], None, False, heads, block_rows
         )
         both = lax.all_to_all(
-            after(both, normed_group), "head", split_axis=0, concat_axis=0, tiled=True
+            after(both, state[0]), "head", split_axis=0, concat_axis=0, tiled=True
         ).reshape(band_rows, 2 * blocks * chunk)
-        output_near = send_near(after(output_rows, key_value))
-        output = gather_blk(output_rows, output_near + send_far(output_near))
-        output = output.reshape(width, model_width)
         upstream_group = lax.all_gather(
             after(upstream_low, normed_group), "head", axis=0, tiled=True
         )
-        state, sent, both, output, upstream_group = lax.optimization_barrier(
-            (state, sent, both, output, upstream_group)
-        )
-        near, down_far = send_near(both), send_far(down_near)
+        state, sent, both, upstream_group = lax.optimization_barrier(
+            (state, sent, both, upstream_group)
+        )
+        near = send_near(both)
         attended, log_total = forward_attention(
             place, query, sent, masks[1:], state, True, heads, block_rows
         )
+        down_near = send_near(after(down_weight, sent[0]))
+        attended, down_near = lax.optimization_barrier((attended, down_near))
         joined = lax.psum_scatter(
             dot(attended, output).astype(BF16), "head", scatter_dimension=0, tiled=True
         )
         joined, near = lax.optimization_barrier((joined, near))
-        both = gather_blk(both, near + send_far(near)).reshape(model_width, 2 * blocks * chunk)
+        near, far = lax.optimization_barrier((near, send_far(near)))
+        both = gather_blk(both, near + far).reshape(model_width, 2 * blocks * chunk)
+        down_near = after(down_near, far)
+        down_near, down_far = lax.optimization_barrier((down_near, send_far(down_near)))
         down = gather_blk(down_weight, down_near + down_far).reshape(blocks * chunk, model_width)
 
     with jax.named_scope("feed_forward"):
         residual = inputs + joined.astype(F32)
         normed_two, inverse_two = normalize_rows(residual)
         normed_two_group = lax.all_gather(normed_two.astype(BF16), "head", axis=0, tiled=True)
-        both_act = dot(normed_two_group, both)
-        gate_act, up_act = jnp.split(both_act, 2, axis=1)
-        sigmoid_gate = jax.nn.sigmoid(gate_act)
-        silu_gate = gate_act * sigmoid_gate
-        mixed = (silu_gate * up_act).astype(BF16)
-        mixed_grad = dot_transposed(upstream_group, down)
-        gate_back = (
-            mixed_grad * up_act * sigmoid_gate * (1.0 + gate_act * (1.0 - sigmoid_gate))
-        ).astype(BF16)
-        up_back = (mixed_grad * silu_gate).astype(BF16)
-        both_back = jnp.concatenate([gate_back, up_back], axis=1)
-        normed_two_partial = dot_transposed(both_back, both)
+        mixed, both_back, normed_two_partial = feed_forward(
+            normed_two_group, upstream_group, both, down
+        )
         normed_two_grad = lax.psum_scatter(
-            normed_two_partial.astype(BF16), "head", scatter_dimension=0, tiled=True
+            normed_two_partial, "head", scatter_dimension=0, tiled=True
         ).astype(F32)
         down_partial = dot(mixed, down).astype(BF16)
 
@@ -581,13 +625,13 @@
             return lax.dynamic_slice_in_dim(values, place_of * band_rows, band_rows, 1)
 
         both_terms = terms_of(lambda j: outer_sum(band(normed_two_group, j), both_back))
-        both_passed = sum_pass(both_terms)
+        both_passed, both_own = sum_pass(both_terms), sum_own(both_terms)
         down_terms = terms_of(
             lambda j: outer_sum(lax.dynamic_slice_in_dim(mixed, j * chunk, chunk, 1), upstream_group)
         )
-        normed_two_grad, down_partial, both_terms, both_passed, down_terms = (
+        normed_two_grad, down_partial, both_terms, both_passed, both_own, down_terms = (
             lax.optimization_barrier(
-                (normed_two_grad, down_partial, both_terms, both_passed, down_terms)
+                (normed_two_grad, down_partial, both_terms, both_passed, both_own, down_terms)
             )
         )
 
@@ -605,46 +649,42 @@
 
     with jax.named_scope("attention_back"):
         residual_group = lax.all_gather(residual_low, "head", axis=0, tiled=True)
-        both_own, both_far = sum_own(both_terms), sum_far(both_terms, both_passed)
-        down_passed = sum_pass(down_terms)
-        residual_group, both_own, both_far, down_terms, down_passed = lax.optimization_barrier(
-            (residual_group, both_own, both_far, down_terms, down_passed)
-        )
-        both_sum = sum_end(both_terms, both_own, both_far)
+        both_far = sum_far(both_terms, both_passed)
+        both_far, down_terms = lax.optimization_barrier((both_far, down_terms))
+        both_sum = sum_end(both_terms, both_own, both_far).astype(BF16)
+        down_passed, down_own = sum_pass(down_terms), sum_own(down_terms)
+        residual_group, both_sum, down_terms, down_passed, down_own = lax.optimization_barrier(
+            (residual_group, both_sum, down_terms, down_passed, down_own)
+        )
         attended_grad = dot_transposed(residual_group, output).astype(BF16)
         down_act = lax.psum_scatter(
             after(down_partial, residual_group), "head", scatter_dimension=0, tiled=True
         ).astype(F32)
-        query_grad, *remote = backward_attention(
-            place, query, sent, masks[1:], attended, attended_grad, log_total, None,
-            False, heads, block_rows,
-        )
-        returned = [
-            swapped(part, mask, lambda i, j: j < i) for mask, part in zip(masks[1:], remote)
+        order = masks[:0:-1] + [0]
+        query_grad, *pairs = backward_attention(
+            place, query, [([key_value] + sent)[mask] for mask in order], order, attended,
+            attended_grad, log_total, None, True, heads, block_rows,
+        )
+        key_value_grads = [pairs[-1]] + [
+            swapped(pairs[order.index(mask)], mask, lambda i, j: j < i) for mask in masks[1:]
         ]
+        down_far = sum_far(down_terms, down_passed)
+        query_grad, both_sum, down_far = lax.optimization_barrier((query_grad, both_sum, down_far))
         hidden_shards = to_shards(both_sum)
-        query_grad, returned, hidden_shards = lax.optimization_barrier(
-            (query_grad, returned, hidden_shards)
-        )
-        query_grad, own = backward_attention(
-            place, query, [key_value], [0], attended, attended_grad, log_total, query_grad,
-            True, heads, block_rows,
-        )
-        down_sum = sum_end(down_terms, sum_own(down_terms), sum_far(down_terms, down_passed))
+        residual_group = after(residual_group, key_value_grads[1])
         output_terms = terms_of(
             lambda j: outer_sum(
                 lax.dynamic_slice_in_dim(attended, j * shard_rows, shard_rows, 1), residual_group
             )
         )
-        output_grad = lax.ppermute(
-            sum_to_owner(output_terms).astype(BF16),
-            ("blk", "head"),
-            [(b * parts + h, h * blocks + b) for b in range(blocks) for h in range(parts)],
-        ).astype(F32)
+        query_grad, key_value_grads, hidden_shards, output_terms = lax.optimization_barrier(
+            (query_grad, key_value_grads, hidden_shards, output_terms)
+        )
+        down_sum = sum_end(down_terms, down_own, down_far)
         down_act = after(down_act, query_grad)
         layer_output = ((residual + down_act) * valid).astype(BF16)[None]
         projection_back = unrope(
-            place, query_grad, cosine, sine, [own] + returned, masks,
+            place, query_grad, cosine, sine, key_value_grads, masks,
             heads, block_rows,
         )
         normed_one_grad = lax.psum_scatter(
@@ -660,8 +700,19 @@
     with jax.named_scope("weight_grads"):
 
         gate_grad, up_grad = spread(hidden_shards, 2, parts, blocks, chunk)
-        summed = sum_to_owner(terms_of(lambda j: outer_sum(band(normed_group, j), projection_back)))
-        projection_grads = spread(to_shards(summed), 3, parts, 1, width)
+        terms = terms_of(lambda j: outer_sum(band(normed_group, j), projection_back))
+        summed = sum_end(terms, sum_own(terms), sum_far(terms, sum_pass(terms)))
+        summed, output_part = lax.optimization_barrier((summed, sum_to_owner(output_terms)))
+        output_grad = lax.ppermute(
+            output_part.astype(BF16),
+            ("blk", "head"),
+            [(b * parts + h, h * blocks + b) for b in range(blocks) for h in range(parts)],
+        )
+        shards, output_grad, tokens_grad = lax.optimization_barrier(
+            (to_shards(summed), output_grad, tokens_grad)
+        )
+        output_grad = output_grad.astype(F32)
+        projection_grads = spread(shards, 3, parts, 1, width)
     return (
         layer_output,
         tokens_grad,

time: 705 us -> 667 us (0.946)
  matrix products: 106 us -> 66.6 us
  Pallas kernels: 50.5 us -> 79.2 us
  waiting for transfers between devices: 314 us -> 290 us
  local copies, waits for them, and re-layouts: 67.8 us -> 60.6 us
    pallas_call x0 -> x1, Pallas kernels: none -> 29.2 us  [feed_forward(): pl.pallas_call(functools.partial(feed_kernel, columns=min(256, hidden)),...]
    dot_general x4 -> x2, matrix products: 35.6 us -> 11.6 us  [dot_transposed(): lax.dot_general(left, right, (((1,), (1,)), ((), ())), preferred_element_...]
    all_gather x1, waiting for transfers between devices: 17.1 us -> 0.01 us  [local(): normed_group = lax.all_gather(normed_start, 'head', axis=0, tiled=True)]
    all_to_all x1, waiting for transfers between devices: 0.01 us -> 16.5 us  [local(): lax.all_to_all(stacked, 'head', split_axis=0, concat_axis=0, tiled=True)]
    dot_general x4 -> x3, matrix products: 33 us -> 19.1 us  [dot(): return jnp.dot(left, right, preferred_element_type=F32)]
    ppermute x2, waiting for transfers between devices: 29.3 us -> 18.8 us  [the longest x1 12.2 us: local(): lax.ppermute(output_part.astype(BF16), ('blk', 'head'), [(b * parts + h,...]
    all_to_all x2, waiting for transfers between devices: 26.4 us -> 18 us  [to_shards(): lax.all_to_all(summed.astype(BF16).reshape(parts, shard_rows, summed.shap...]
    unnamed x124 -> x86, local copies, waits for them, and re-layouts: 22.4 us -> 14.8 us
  transfers between devices with their start and end apart: 60 -> 57, of which waited for: 25 -> 34; matrix products, arithmetic and copies ran while one was open for 20% -> 22% of each run, Pallas kernels for 6% -> 7%
where the time goes in v3:
time: 667 us; the launch traced here: 658 us
  waiting for transfers between devices  290 us (43%)
  starting transfers between devices  101 us (15%)
  Pallas kernels  79.2 us (12%)
  matrix products  66.6 us (10%)
  local copies, waits for them, and re-layouts  60.6 us (9%)
  other arithmetic  44.8 us (7%)
  between operations  15.9 us (2%)
    ppermute x43, waiting for transfers between devices, swapped(): return lax.ppermute(value, 'blk', pairs)  209 us
    ppermute x43, starting transfers between devices, swapped(): return lax.ppermute(value, 'blk', pairs)  60.3 us
    dot_general x16, matrix products, outer_sum(): lax.dot_general(left, right, (((0,), (0,)), ((), ())), preferred_element_...  35.8 us
    pallas_call x1, Pallas kernels, feed_forward(): pl.pallas_call(functools.partial(feed_kernel, columns=min(256, hidden)),...  29.2 us
    dynamic_update_slice x16, local copies, waits for them, and re-layouts, gather_blk(): whole = lax.dynamic_update_slice(whole, piece[None], start)  21.1 us
    pallas_call x1, Pallas kernels, backward_attention(): pl.pallas_call(functools.partial(backward_kernel, masks=masks, started=st...  19.4 us
    dot_general x3, matrix products, dot(): return jnp.dot(left, right, preferred_element_type=F32)  19.1 us
    all_to_all x2, waiting for transfers between devices, to_shards(): lax.all_to_all(summed.astype(BF16).reshape(parts, shard_rows, summed.shap...  18 us
  transfers between devices with their start and end apart: 57, of which 34 were waited for; matrix products, arithmetic and copies ran while one was open for 22% of the time, Pallas kernels for 7%

profile of v3, /device:TPU:5, one launch (start us, length us, event | category | flops | bytes accessed | tf_op | source)
XLA Modules:
  0.0 657.9 jit_solution(6195191153711979356)
XLA Ops:
  11.0 5.5 all-to-all-start
  20.2 16.5 %all-to-all-done = bf16[8,64,768]{2,1,0:T(8,128)(2,1)S(1)} async-done(((bf16[8,64,768]{2,1,0:T(8,128)(2,1)}), bf16[8,64,768]{2,1,0:T(8,128)(2,1)S(1)}, u32[]{:S(2)}, u32[]{:S(2)}) %all-to-all-start) | async-done | bytes 786464 | tf_op jit(solution)/shard_map/projection_weights/all_to_all | solution.py:550
  46.0 6.6 %collective-permute-done.4 = bf16[64,2048]{1,0:T(8,128)(2,1)S(1)} collective-permute-done((bf16[64,2048]{1,0:T(8,128)(2,1)S(1)}, bf16[64,2048]{1,0:T(8,128)(2,1)S(1)}, u32[]{:S(2)}, u32[]{:S(2)}) %collective-permute-start.4) | collective-permute-done | bytes 262176 | tf_op jit(solution)/shard_map/hidden_weights/ppermute | solution.py:565
  54.6 13.8 %collective-permute-start.6 = (bf16[64,2048]{1,0:T(8,128)(2,1)S(1)}, bf16[64,2048]{1,0:T(8,128)(2,1)S(1)}, u32[]{:S(2)}, u32[]{:S(2)}) collective-permute-start(bf16[64,2048]{1,0:T(8,128)(2,1)S(1)} %collective-permute-done.4), channel_id=1, source_target_pairs={{0,16},{8,24},{16,0},{24,8},{1,17},{9,25},{17,1},{25,9},{2,18},{10... | collective-permute-start | bytes 786440 | tf_op jit(solution)/shard_map/hidden_weights/ppermute | solution.py:66
  70.2 5.6 collective-permute-start.7
  95.9 6.4 convolution_convert_fusion.12.lin_ref
  102.3 4.1 rope.1
  107.4 5.1 attention_forward.2
  113.6 11.3 %all-to-all-start.1 = ((bf16[8,64,2048]{2,1,0:T(8,128)(2,1)}), bf16[8,64,2048]{2,1,0:T(8,128)(2,1)}, u32[]{:S(2)}, u32[]{:S(2)}) async-start(bf16[8,64,2048]{2,1,0:T(8,128)(2,1)} %collect.3), calls=%async_computation.1 | async-start | bytes 4194304 | tf_op jit(solution)/shard_map/attention/all_to_all | solution.py:587
  129.0 20.1 %collective-permute-done.9.refs_0_.refs_2_ = bf16[1024,512]{1,0:T(8,128)(2,1)S(1)} collective-permute-done((bf16[1024,512]{1,0:T(8,128)(2,1)}, bf16[1024,512]{1,0:T(8,128)(2,1)S(1)}, u32[]{:S(2)}, u32[]{:S(2)}) %collective-permute-start.9) | collective-permute-done | bytes 1048608 | tf_op jit(solution)/shard_map/attention/ppermute | solution.py:66
  149.1 26.2 %collective-permute-done.10.refs_1_ = bf16[1024,512]{1,0:T(8,128)(2,1)S(1)} collective-permute-done((bf16[1024,512]{1,0:T(8,128)(2,1)}, bf16[1024,512]{1,0:T(8,128)(2,1)S(1)}, u32[]{:S(2)}, u32[]{:S(2)}) %collective-permute-start.10) | collective-permute-done | bytes 1048608 | tf_op jit(solution)/shard_map/attention/ppermute | solution.py:66
  176.3 9.8 %all-to-all-done.1 = bf16[8,64,2048]{2,1,0:T(8,128)(2,1)} async-done(((bf16[8,64,2048]{2,1,0:T(8,128)(2,1)}), bf16[8,64,2048]{2,1,0:T(8,128)(2,1)}, u32[]{:S(2)}, u32[]{:S(2)}) %all-to-all-start.1) | async-done | bytes 2097184 | tf_op jit(solution)/shard_map/attention/all_to_all | solution.py:587
  190.1 9.7 %attention_forward.3 = (bf16[1024,256]{1,0:T(8,128)(2,1)S(1)}, f32[2,1,1024]{2,1,0:T(1,128)S(1)}) custom-call(s32[2]{0:T(128)S(1)} %pad_add_fusion.place_ref, bf16[1024,256]{1,0:T(8,128)(2,1)S(1)} %copy-done.1, bf16[1024,512]{1,0:T(8,128)(2,1)S(1)} %collective-permute-done.9.refs_0_.refs_2_, bf16[1024,512]{1,0:T(8,128)(2,1)S(1)} %collective-permute-done.10.refs_1_, ...), custom_call_target="tpu_custom_call" | custom-call | tf_op jit(solution)/shard_map/attention/attention_forward/pallas_call | solution.py:357
  199.9 10.9 %collective-permute-done.12 = bf16[256,2048]{1,0:T(8,128)(2,1)} collective-permute-done((bf16[256,2048]{1,0:T(8,128)(2,1)}, bf16[256,2048]{1,0:T(8,128)(2,1)}, u32[]{:S(2)}, u32[]{:S(2)}) %collective-permute-start.12) | collective-permute-done | bytes 1048608 | tf_op jit(solution)/shard_map/attention/ppermute | solution.py:66
  211.3 4.5 convolution_convert_fusion
  217.0 44.7 %collective-permute-done.14 = bf16[512,2048]{1,0:T(8,128)(2,1)} collective-permute-done((bf16[512,2048]{1,0:T(8,128)(2,1)}, bf16[512,2048]{1,0:T(8,128)(2,1)}, u32[]{:S(2)}, u32[]{:S(2)}) %collective-permute-start.14) | collective-permute-done | bytes 2097184 | tf_op jit(solution)/shard_map/attention/ppermute | solution.py:66
  275.5 4.4 broadcast_in_dim.125
  279.9 3.2 bitcast_dynamic-update-slice_fusion.2
  283.1 7.9 %collective-permute-done.16 = bf16[256,2048]{1,0:T(8,128)(2,1)S(1)} collective-permute-done((bf16[256,2048]{1,0:T(8,128)(2,1)S(1)}, bf16[256,2048]{1,0:T(8,128)(2,1)S(1)}, u32[]{:S(2)}, u32[]{:S(2)}) %collective-permute-start.16) | collective-permute-done | bytes 1048608 | tf_op jit(solution)/shard_map/attention/ppermute | solution.py:66
  297.0 3.3 bitcast_dynamic-update-slice_fusion.1
  300.4 3.2 bitcast_dynamic-update-slice_fusion
  312.0 3.6 all-gather.9.cloned.1.call-done.normed_ref
  315.6 29.2 %feed_forward.1 = (bf16[1024,1024]{1,0:T(8,128)(2,1)S(1)}, bf16[1024,2048]{1,0:T(8,128)(2,1)}, bf16[1024,2048]{1,0:T(8,128)(2,1)}) custom-call(bf16[1024,2048]{1,0:T(8,128)(2,1)} %all-gather.9.cloned.1.call-done.normed_ref, bf16[1024,2048]{1,0:T(8,128)(2,1)} %all-gather.7.cloned.1.call-done.grad_ref, bf16[2048,2048]{1,0:T(8,128)(2,1)} %bitcast.23.both_ref, ...), custom_call_target="tpu_custom_call" | custom-call | tf_op jit(solution)/shard_map/feed_forward/feed_forward/pallas_call | solution.py:495
  345.1 5.0 convolution_convert_fusion.3
  370.3 4.8 fusion.22
  377.3 8.3 %convolution_convert_fusion.2 = bf16[1024,2048]{1,0:T(8,128)(2,1)} fusion(bf16[1024,1024]{1,0:T(8,128)(2,1)S(1)} %get-tuple-element.150, bf16[1024,2048]{1,0:T(8,128)(2,1)} %bitcast.29.down_ref), kind=kOutput, calls=%fused_computation.2 | convolution fusion | flops 4297064448 | bytes 10485760 | tf_op jit(solution)/shard_map/feed_forward/dot_general | solution.py:52
  385.6 10.8 %reduce-scatter.7.cloned.1.call-done = bf16[128,2048]{1,0:T(8,128)(2,1)} async-done(((bf16[1024,2048]{1,0:T(8,128)(2,1)}), bf16[128,2048]{1,0:T(8,128)(2,1)}) %reduce-scatter.7.cloned.1.call-update) | async-done | bytes 524304 | tf_op jit(solution)/shard_map/feed_forward/reduce_scatter | solution.py:619
  400.7 3.2 fusion.59
  408.5 20.3 %collective-permute-done.24 = bf16[256,2048]{1,0:T(8,128)(2,1)S(1)} collective-permute-done((bf16[256,2048]{1,0:T(8,128)(2,1)S(1)}, bf16[256,2048]{1,0:T(8,128)(2,1)S(1)}, u32[]{:S(2)}, u32[]{:S(2)}) %collective-permute-start.24) | collective-permute-done | bytes 1048608 | tf_op jit(solution)/shard_map/attention_back/ppermute | solution.py:66
  437.9 3.0 collective-permute-done.26
  440.9 11.2 %collective-permute-done.28 = bf16[128,2048]{1,0:T(8,128)(2,1)} collective-permute-done((bf16[128,2048]{1,0:T(8,128)(2,1)S(1)}, bf16[128,2048]{1,0:T(8,128)(2,1)}, u32[]{:S(2)}, u32[]{:S(2)}) %collective-permute-start.28) | collective-permute-done | bytes 524320 | tf_op jit(solution)/shard_map/attention_back/ppermute | solution.py:66
  459.0 3.8 convolution_convert_fusion.16.do_ref
  462.8 19.4 %attention_backward.1 = (f32[1024,256]{1,0:T(8,128)S(1)}, bf16[1024,512]{1,0:T(8,128)(2,1)S(1)}, bf16[1024,512]{1,0:T(8,128)(2,1)S(1)}, bf16[1024,512]{1,0:T(8,128)(2,1)S(1)}, bf16[1024,512]{1,0:T(8,128)(2,1)}) custom-call(s32[2]{0:T(128)S(1)} %pad_add_fusion.place_ref, bf16[1024,256]{1,0:T(8,128)(2,1)S(1)} %copy-done.1, ...), custom_call_target="tpu_custom_call" | custom-call | tf_op jit(solution)/shard_map/attention_back/attention_backward/pallas_call | solution.py:439
  486.2 9.8 %all-to-all-start.2 = ((bf16[8,64,2048]{2,1,0:T(8,128)(2,1)}), bf16[8,64,2048]{2,1,0:T(8,128)(2,1)S(1)}, u32[]{:S(2)}, u32[]{:S(2)}) async-start(bf16[8,64,2048]{2,1,0:T(8,128)(2,1)} %bitcast.134), calls=%async_computation.5 | async-start | bytes 4194304 | tf_op jit(solution)/shard_map/attention_back/all_to_all | solution.py:642
  501.2 25.7 %collective-permute-done.32.refs_1_ = bf16[1024,512]{1,0:T(8,128)(2,1)} collective-permute-done((bf16[1024,512]{1,0:T(8,128)(2,1)}, bf16[1024,512]{1,0:T(8,128)(2,1)}, u32[]{:S(2)}, u32[]{:S(2)}) %collective-permute-start.32) | collective-permute-done | bytes 1048608 | tf_op jit(solution)/shard_map/attention_back/ppermute | solution.py:66
  527.0 3.1 convolution_convert_fusion.11
  535.4 18.0 %all-to-all-done.2.in_ref = bf16[8,64,2048]{2,1,0:T(8,128)(2,1)S(1)} async-done(((bf16[8,64,2048]{2,1,0:T(8,128)(2,1)}), bf16[8,64,2048]{2,1,0:T(8,128)(2,1)S(1)}, u32[]{:S(2)}, u32[]{:S(2)}) %all-to-all-start.2) | async-done | bytes 2097184 | tf_op jit(solution)/shard_map/attention_back/all_to_all | solution.py:642
  553.5 5.6 unrope.1
  559.1 7.8 %convolution_convert_fusion.1 = bf16[1024,2048]{1,0:T(8,128)(2,1)} fusion(bf16[1024,768]{1,0:T(8,128)(2,1)} %unrope.1, bf16[2048,768]{1,0:T(8,128)(2,1)} %bitcast.8), kind=kOutput, calls=%fused_computation.1 | convolution fusion | flops 3223322624 | bytes 8912896 | tf_op jit(solution)/shard_map/attention_back/dot_general | solution.py:56
  567.0 4.1 convert_add_fusion.1
  586.1 10.6 %collective-permute-done.43 = bf16[64,2048]{1,0:T(8,128)(2,1)S(1)} collective-permute-done((bf16[64,2048]{1,0:T(8,128)(2,1)S(1)}, bf16[64,2048]{1,0:T(8,128)(2,1)S(1)}, u32[]{:S(2)}, u32[]{:S(2)}) %collective-permute-start.43) | collective-permute-done | bytes 262176 | tf_op jit(solution)/shard_map/weight_grads/ppermute | solution.py:66
  599.1 3.3 collective-permute-done.41
  605.4 8.4 %collective-permute-done.37 = bf16[256,768]{1,0:T(8,128)(2,1)S(1)} collective-permute-done((bf16[256,768]{1,0:T(8,128)(2,1)S(1)}, bf16[256,768]{1,0:T(8,128)(2,1)S(1)}, u32[]{:S(2)}, u32[]{:S(2)}) %collective-permute-start.37) | collective-permute-done | bytes 393248 | tf_op jit(solution)/shard_map/weight_grads/ppermute | solution.py:66
  615.0 5.0 all-to-all-start.3
  620.0 3.1 pad_maximum_fusion.1
  625.4 5.3 collective-permute-start.44
  633.4 3.0 fusion.29
  636.4 12.2 %collective-permute-done.44 = bf16[64,2048]{1,0:T(8,128)(2,1)S(1)} collective-permute-done((bf16[64,2048]{1,0:T(8,128)(2,1)}, bf16[64,2048]{1,0:T(8,128)(2,1)S(1)}, u32[]{:S(2)}, u32[]{:S(2)}) %collective-permute-start.44) | collective-permute-done | bytes 262176 | tf_op jit(solution)/shard_map/weight_grads/ppermute | solution.py:706
  (273 shorter events, 171.1 us)
Async XLA Ops:
  11.0 25.7 %all-to-all-start = ((bf16[8,64,768]{2,1,0:T(8,128)(2,1)}), bf16[8,64,768]{2,1,0:T(8,128)(2,1)S(1)}, u32[]{:S(2)}, u32[]{:S(2)}) async-start(bf16[8,64,768]{2,1,0:T(8,128)(2,1)} %collect.2), calls=%async_computation | async-start | bytes 1572864 | tf_op jit(solution)/shard_map/projection_weights/all_to_all | solution.py:550
  16.5 74.5 %all-gather.5.cloned.1.call-start = ((), (), s32[]{:S(2)}) async-start(), calls=%async_computation.8 | async-start | bytes 4718592 | tf_op jit(solution)/shard_map/tokens_gather/all_gather | solution.py:559
  36.7 149.5 %all-gather.7.cloned.1.call-start = ((), (), s32[]{:S(2)}) async-start(), calls=%async_computation.9 | async-start | bytes 4718592 | tf_op jit(solution)/shard_map/attention/all_gather | solution.py:590
  37.4 15.2 %collective-permute-start.4 = (bf16[64,2048]{1,0:T(8,128)(2,1)S(1)}, bf16[64,2048]{1,0:T(8,128)(2,1)S(1)}, u32[]{:S(2)}, u32[]{:S(2)}) collective-permute-start(bf16[64,2048]{1,0:T(8,128)(2,1)S(1)} %copy-done.42), channel_id=1, source_target_pairs={{0,0},{4,1},{8,2},{12,3},{16,4},{20,5},{24,6},{28,7},{1,8},{5,9},{... | collective-permute-start | bytes 786440 | tf_op jit(solution)/shard_map/hidden_weights/ppermute | solution.py:565
  41.3 40.2 %collective-permute-start = (bf16[512,768]{1,0:T(8,128)(2,1)S(1)}, bf16[512,768]{1,0:T(8,128)(2,1)S(1)}, u32[]{:S(2)}, u32[]{:S(2)}) collective-permute-start(bf16[512,768]{1,0:T(8,128)(2,1)S(1)} %bitcast.135), channel_id=1, source_target_pairs={{0,8},{8,0},{16,24},{24,16},{1,9},{9,1},{17,25},{25,17},{2,10},{10... | collective-permute-start | bytes 2359304 | tf_op jit(solution)/shard_map/projection_weights/ppermute | solution.py:66
  43.1 39.3 %collective-permute-start.1 = (bf16[512,768]{1,0:T(8,128)(2,1)S(1)}, bf16[512,768]{1,0:T(8,128)(2,1)S(1)}, u32[]{:S(2)}, u32[]{:S(2)}) collective-permute-start(bf16[512,768]{1,0:T(8,128)(2,1)S(1)} %bitcast.136), channel_id=1, source_target_pairs={{0,16},{8,24},{16,0},{24,8},{1,17},{9,25},{17,1},{25,9},{2,18},{10... | collective-permute-start | bytes 2359304 | tf_op jit(solution)/shard_map/projection_weights/ppermute | solution.py:66
  52.6 17.6 %collective-permute-start.5 = (bf16[64,2048]{1,0:T(8,128)(2,1)S(1)}, bf16[64,2048]{1,0:T(8,128)(2,1)S(1)}, u32[]{:S(2)}, u32[]{:S(2)}) collective-permute-start(bf16[64,2048]{1,0:T(8,128)(2,1)S(1)} %collective-permute-done.4), channel_id=1, source_target_pairs={{0,8},{8,0},{16,24},{24,16},{1,9},{9,1},{17,25},{25,17},{2,10},{10... | collective-permute-start | bytes 786440 | tf_op jit(solution)/shard_map/hidden_weights/ppermute | solution.py:66
  54.6 21.2 %collective-permute-start.6 = (bf16[64,2048]{1,0:T(8,128)(2,1)S(1)}, bf16[64,2048]{1,0:T(8,128)(2,1)S(1)}, u32[]{:S(2)}, u32[]{:S(2)}) collective-permute-start(bf16[64,2048]{1,0:T(8,128)(2,1)S(1)} %collective-permute-done.4), channel_id=1, source_target_pairs={{0,16},{8,24},{16,0},{24,8},{1,17},{9,25},{17,1},{25,9},{2,18},{10... | collective-permute-start | bytes 786440 | tf_op jit(solution)/shard_map/hidden_weights/ppermute | solution.py:66
  113.6 72.6 %all-to-all-start.1 = ((bf16[8,64,2048]{2,1,0:T(8,128)(2,1)}), bf16[8,64,2048]{2,1,0:T(8,128)(2,1)}, u32[]{:S(2)}, u32[]{:S(2)}) async-start(bf16[8,64,2048]{2,1,0:T(8,128)(2,1)} %collect.3), calls=%async_computation.1 | async-start | bytes 4194304 | tf_op jit(solution)/shard_map/attention/all_to_all | solution.py:587
  124.8 138.1 %reduce-scatter.5.cloned.1.call-start = ((), (), s32[]{:S(2)}) async-start(), calls=%async_computation.10 | async-start | bytes 4718592 | tf_op jit(solution)/shard_map/attention/reduce_scatter | solution.py:602
  124.8 24.3 %collective-permute-start.9 = (bf16[1024,512]{1,0:T(8,128)(2,1)}, bf16[1024,512]{1,0:T(8,128)(2,1)S(1)}, u32[]{:S(2)}, u32[]{:S(2)}) collective-permute-start(bf16[1024,512]{1,0:T(8,128)(2,1)} %get-tuple-element.116.refs_0_.refs_3_), channel_id=1, source_target_pairs={{0,8},{16,24},{1,9},{17,25},{2,10},{18,26},{3,11},{19,27},{4,12},{... | collective-permute-start | bytes 3145736 | tf_op jit(solution)/shard_map/attention/ppermute | solution.py:66
  126.2 49.1 %collective-permute-start.10 = (bf16[1024,512]{1,0:T(8,128)(2,1)}, bf16[1024,512]{1,0:T(8,128)(2,1)S(1)}, u32[]{:S(2)}, u32[]{:S(2)}) collective-permute-start(bf16[1024,512]{1,0:T(8,128)(2,1)} %get-tuple-element.116.refs_0_.refs_3_), channel_id=1, source_target_pairs={{0,16},{8,24},{1,17},{9,25},{2,18},{10,26},{3,19},{11,27},{4,20},{... | collective-permute-start | bytes 3145736 | tf_op jit(solution)/shard_map/attention/ppermute | solution.py:66
  127.5 47.8 %collective-permute-start.11 = (bf16[1024,512]{1,0:T(8,128)(2,1)}, bf16[1024,512]{1,0:T(8,128)(2,1)S(1)}, u32[]{:S(2)}, u32[]{:S(2)}) collective-permute-start(bf16[1024,512]{1,0:T(8,128)(2,1)} %get-tuple-element.116.refs_0_.refs_3_), channel_id=1, source_target_pairs={{0,24},{8,16},{1,25},{9,17},{2,26},{10,18},{3,27},{11,19},{4,28},{... | collective-permute-start | bytes 3145736 | tf_op jit(solution)/shard_map/attention/ppermute | solution.py:66
  186.2 24.6 %collective-permute-start.12 = (bf16[256,2048]{1,0:T(8,128)(2,1)}, bf16[256,2048]{1,0:T(8,128)(2,1)}, u32[]{:S(2)}, u32[]{:S(2)}) collective-permute-start(bf16[256,2048]{1,0:T(8,128)(2,1)} %param.18), channel_id=1, source_target_pairs={{0,8},{8,0},{16,24},{24,16},{1,9},{9,1},{17,25},{25,17},{2,10},{10... | collective-permute-start | bytes 3145736 | tf_op jit(solution)/shard_map/attention/ppermute | solution.py:66
  187.2 24.1 %collective-permute-start.13 = (bf16[256,2048]{1,0:T(8,128)(2,1)}, bf16[256,2048]{1,0:T(8,128)(2,1)}, u32[]{:S(2)}, u32[]{:S(2)}) collective-permute-start(bf16[256,2048]{1,0:T(8,128)(2,1)} %param.18), channel_id=1, source_target_pairs={{0,16},{8,24},{16,0},{24,8},{1,17},{9,25},{17,1},{25,9},{2,18},{10... | collective-permute-start | bytes 3145736 | tf_op jit(solution)/shard_map/attention/ppermute | solution.py:66
  215.8 99.7 %all-gather.9.cloned.1.call-start = ((), (), s32[]{:S(2)}) async-start(), calls=%async_computation.11 | async-start | bytes 4718592 | tf_op jit(solution)/shard_map/feed_forward/all_gather | solution.py:615
  215.9 45.7 %collective-permute-start.14 = (bf16[512,2048]{1,0:T(8,128)(2,1)}, bf16[512,2048]{1,0:T(8,128)(2,1)}, u32[]{:S(2)}, u32[]{:S(2)}) collective-permute-start(bf16[512,2048]{1,0:T(8,128)(2,1)} %bitcast.15), channel_id=1, source_target_pairs={{0,8},{8,0},{16,24},{24,16},{1,9},{9,1},{17,25},{25,17},{2,10},{10... | collective-permute-start | bytes 6291464 | tf_op jit(solution)/shard_map/attention/ppermute | solution.py:66
  216.5 45.6 %collective-permute-start.15 = (bf16[512,2048]{1,0:T(8,128)(2,1)}, bf16[512,2048]{1,0:T(8,128)(2,1)}, u32[]{:S(2)}, u32[]{:S(2)}) collective-permute-start(bf16[512,2048]{1,0:T(8,128)(2,1)} %bitcast.15), channel_id=1, source_target_pairs={{0,16},{8,24},{16,0},{24,8},{1,17},{9,25},{17,1},{25,9},{2,18},{10... | collective-permute-start | bytes 6291464 | tf_op jit(solution)/shard_map/attention/ppermute | solution.py:66
  267.6 128.8 %reduce-scatter.7.cloned.1.call-start = ((), (), s32[]{:S(2)}) async-start(), calls=%async_computation.12 | async-start | bytes 4718592 | tf_op jit(solution)/shard_map/feed_forward/reduce_scatter | solution.py:619
  269.0 22.0 %collective-permute-start.16 = (bf16[256,2048]{1,0:T(8,128)(2,1)S(1)}, bf16[256,2048]{1,0:T(8,128)(2,1)S(1)}, u32[]{:S(2)}, u32[]{:S(2)}) collective-permute-start(bf16[256,2048]{1,0:T(8,128)(2,1)S(1)} %slice.100), channel_id=1, source_target_pairs={{0,16},{8,24},{16,0},{24,8},{1,17},{9,25},{17,1},{25,9},{2,18},{10... | collective-permute-start | bytes 3145736 | tf_op jit(solution)/shard_map/attention/ppermute | solution.py:66
  270.7 21.7 %collective-permute-start.17 = (bf16[256,2048]{1,0:T(8,128)(2,1)S(1)}, bf16[256,2048]{1,0:T(8,128)(2,1)S(1)}, u32[]{:S(2)}, u32[]{:S(2)}) collective-permute-start(bf16[256,2048]{1,0:T(8,128)(2,1)S(1)} %slice.101), channel_id=1, source_target_pairs={{0,8},{8,0},{16,24},{24,16},{1,9},{9,1},{17,25},{25,17},{2,10},{10... | collective-permute-start | bytes 3145736 | tf_op jit(solution)/shard_map/attention/ppermute | solution.py:66
  293.4 12.2 %collective-permute-start.18 = (bf16[128,2048]{1,0:T(8,128)(2,1)S(1)}, bf16[128,2048]{1,0:T(8,128)(2,1)S(1)}, u32[]{:S(2)}, u32[]{:S(2)}) collective-permute-start(bf16[128,2048]{1,0:T(8,128)(2,1)S(1)} %slice.102), channel_id=1, source_target_pairs={{0,16},{8,24},{16,0},{24,8},{1,17},{9,25},{17,1},{25,9},{2,18},{10... | collective-permute-start | bytes 1572872 | tf_op jit(solution)/shard_map/attention/ppermute | solution.py:66
  344.8 110.2 %all-gather.11.cloned.1.call-start = ((), (), s32[]{:S(2)}) async-start(), calls=%async_computation.13 | async-start | bytes 4718592 | tf_op jit(solution)/shard_map/attention_back/all_gather | solution.py:651
  351.6 46.0 %collective-permute-start.20 = (bf16[256,2048]{1,0:T(8,128)(2,1)}, bf16[256,2048]{1,0:T(8,128)(2,1)}, u32[]{:S(2)}, u32[]{:S(2)}) collective-permute-start(bf16[256,2048]{1,0:T(8,128)(2,1)} %get-tuple-element.224), channel_id=1, source_target_pairs={{0,8},{8,0},{16,24},{24,16},{1,9},{9,1},{17,25},{25,17},{2,10},{10... | collective-permute-start | bytes 3145736 | tf_op jit(solution)/shard_map/feed_forward/ppermute | solution.py:66
  352.8 44.8 %collective-permute-start.21 = (bf16[256,2048]{1,0:T(8,128)(2,1)}, bf16[256,2048]{1,0:T(8,128)(2,1)}, u32[]{:S(2)}, u32[]{:S(2)}) collective-permute-start(bf16[256,2048]{1,0:T(8,128)(2,1)} %get-tuple-element.223), channel_id=1, source_target_pairs={{0,16},{8,24},{16,0},{24,8},{1,17},{9,25},{17,1},{25,9},{2,18},{10... | collective-permute-start | bytes 3145736 | tf_op jit(solution)/shard_map/feed_forward/ppermute | solution.py:66
  357.9 40.2 %collective-permute-start.22 = (bf16[256,2048]{1,0:T(8,128)(2,1)}, bf16[256,2048]{1,0:T(8,128)(2,1)}, u32[]{:S(2)}, u32[]{:S(2)}) collective-permute-start(bf16[256,2048]{1,0:T(8,128)(2,1)} %slice.134), channel_id=1, source_target_pairs={{0,8},{8,0},{16,24},{24,16},{1,9},{9,1},{17,25},{25,17},{2,10},{10... | collective-permute-start | bytes 3145736 | tf_op jit(solution)/shard_map/feed_forward/ppermute | solution.py:66
  362.8 36.2 %collective-permute-start.23 = (bf16[256,2048]{1,0:T(8,128)(2,1)}, bf16[256,2048]{1,0:T(8,128)(2,1)}, u32[]{:S(2)}, u32[]{:S(2)}) collective-permute-start(bf16[256,2048]{1,0:T(8,128)(2,1)} %slice.135), channel_id=1, source_target_pairs={{0,16},{8,24},{16,0},{24,8},{1,17},{9,25},{17,1},{25,9},{2,18},{10... | collective-permute-start | bytes 3145736 | tf_op jit(solution)/shard_map/feed_forward/ppermute | solution.py:66
  403.9 226.8 %reduce-scatter.9.cloned.1.call-start = ((), (), s32[]{:S(2)}) async-start(), calls=%async_computation.14 | async-start | bytes 4718592 | tf_op jit(solution)/shard_map/attention_back/reduce_scatter | solution.py:660
  406.1 22.7 %collective-permute-start.24 = (bf16[256,2048]{1,0:T(8,128)(2,1)S(1)}, bf16[256,2048]{1,0:T(8,128)(2,1)S(1)}, u32[]{:S(2)}, u32[]{:S(2)}) collective-permute-start(bf16[256,2048]{1,0:T(8,128)(2,1)S(1)} %add_convert_fusion.3), channel_id=1, source_target_pairs={{0,16},{8,24},{16,0},{24,8},{1,17},{9,25},{17,1},{25,9},{2,18},{10... | collective-permute-start | bytes 3145736 | tf_op jit(solution)/shard_map/attention_back/ppermute | solution.py:66
  408.1 22.3 %collective-permute-start.25 = (bf16[256,2048]{1,0:T(8,128)(2,1)S(1)}, bf16[256,2048]{1,0:T(8,128)(2,1)S(1)}, u32[]{:S(2)}, u32[]{:S(2)}) collective-permute-start(bf16[256,2048]{1,0:T(8,128)(2,1)S(1)} %add_convert_fusion.2), channel_id=1, source_target_pairs={{0,8},{8,0},{16,24},{24,16},{1,9},{9,1},{17,25},{25,17},{2,10},{10... | collective-permute-start | bytes 3145736 | tf_op jit(solution)/shard_map/attention_back/ppermute | solution.py:66
  432.1 20.0 %collective-permute-start.28 = (bf16[128,2048]{1,0:T(8,128)(2,1)S(1)}, bf16[128,2048]{1,0:T(8,128)(2,1)}, u32[]{:S(2)}, u32[]{:S(2)}) collective-permute-start(bf16[128,2048]{1,0:T(8,128)(2,1)S(1)} %slice.114), channel_id=1, source_target_pairs={{0,8},{8,0},{16,24},{24,16},{1,9},{9,1},{17,25},{25,17},{2,10},{10... | collective-permute-start | bytes 1572872 | tf_op jit(solution)/shard_map/attention_back/ppermute | solution.py:66
  433.5 18.6 %collective-permute-start.29 = (bf16[128,2048]{1,0:T(8,128)(2,1)S(1)}, bf16[128,2048]{1,0:T(8,128)(2,1)}, u32[]{:S(2)}, u32[]{:S(2)}) collective-permute-start(bf16[128,2048]{1,0:T(8,128)(2,1)S(1)} %slice.115), channel_id=1, source_target_pairs={{0,16},{8,24},{16,0},{24,8},{1,17},{9,25},{17,1},{25,9},{2,18},{10... | collective-permute-start | bytes 1572872 | tf_op jit(solution)/shard_map/attention_back/ppermute | solution.py:66
  456.3 29.9 %collective-permute-start.30 = (bf16[128,2048]{1,0:T(8,128)(2,1)S(1)}, bf16[128,2048]{1,0:T(8,128)(2,1)}, u32[]{:S(2)}, u32[]{:S(2)}) collective-permute-start(bf16[128,2048]{1,0:T(8,128)(2,1)S(1)} %add_convert_fusion.5), channel_id=1, source_target_pairs={{0,16},{8,24},{16,0},{24,8},{1,17},{9,25},{17,1},{25,9},{2,18},{10... | collective-permute-start | bytes 1572872 | tf_op jit(solution)/shard_map/attention_back/ppermute | solution.py:66
  457.8 28.4 %collective-permute-start.31 = (bf16[128,2048]{1,0:T(8,128)(2,1)S(1)}, bf16[128,2048]{1,0:T(8,128)(2,1)}, u32[]{:S(2)}, u32[]{:S(2)}) collective-permute-start(bf16[128,2048]{1,0:T(8,128)(2,1)S(1)} %add_convert_fusion.4), channel_id=1, source_target_pairs={{0,8},{8,0},{16,24},{24,16},{1,9},{9,1},{17,25},{25,17},{2,10},{10... | collective-permute-start | bytes 1572872 | tf_op jit(solution)/shard_map/attention_back/ppermute | solution.py:66
  486.2 67.3 %all-to-all-start.2 = ((bf16[8,64,2048]{2,1,0:T(8,128)(2,1)}), bf16[8,64,2048]{2,1,0:T(8,128)(2,1)S(1)}, u32[]{:S(2)}, u32[]{:S(2)}) async-start(bf16[8,64,2048]{2,1,0:T(8,128)(2,1)} %bitcast.134), calls=%async_computation.5 | async-start | bytes 4194304 | tf_op jit(solution)/shard_map/attention_back/all_to_all | solution.py:642
  496.0 135.9 %reduce-scatter.11.cloned.1.call-start = ((), (), s32[]{:S(2)}) async-start(), calls=%async_computation.15 | async-start | bytes 4718592 | tf_op jit(solution)/shard_map/attention_back/reduce_scatter | solution.py:690
  496.0 31.0 %collective-permute-start.32 = (bf16[1024,512]{1,0:T(8,128)(2,1)}, bf16[1024,512]{1,0:T(8,128)(2,1)}, u32[]{:S(2)}, u32[]{:S(2)}) collective-permute-start(bf16[1024,512]{1,0:T(8,128)(2,1)} %copy-done.17), channel_id=1, source_target_pairs={{8,0},{24,16},{9,1},{25,17},{10,2},{26,18},{11,3},{27,19},{12,4},{... | collective-permute-start | bytes 3145736 | tf_op jit(solution)/shard_map/attention_back/ppermute | solution.py:66
  497.3 37.1 %collective-permute-start.33 = (bf16[1024,512]{1,0:T(8,128)(2,1)}, bf16[1024,512]{1,0:T(8,128)(2,1)S(1)}, u32[]{:S(2)}, u32[]{:S(2)}) collective-permute-start(bf16[1024,512]{1,0:T(8,128)(2,1)} %copy-done.16), channel_id=1, source_target_pairs={{16,0},{24,8},{17,1},{25,9},{18,2},{26,10},{19,3},{27,11},{20,4},{... | collective-permute-start | bytes 3145736 | tf_op jit(solution)/shard_map/attention_back/ppermute | solution.py:66
  499.0 36.5 %collective-permute-start.34 = (bf16[1024,512]{1,0:T(8,128)(2,1)}, bf16[1024,512]{1,0:T(8,128)(2,1)}, u32[]{:S(2)}, u32[]{:S(2)}) collective-permute-start(bf16[1024,512]{1,0:T(8,128)(2,1)} %copy-done.15), channel_id=1, source_target_pairs={{16,8},{24,0},{17,9},{25,1},{18,10},{26,2},{19,11},{27,3},{20,12},... | collective-permute-start | bytes 3145736 | tf_op jit(solution)/shard_map/attention_back/ppermute | solution.py:66
  577.1 26.1 %collective-permute-start.35 = (bf16[256,768]{1,0:T(8,128)(2,1)S(1)}, bf16[256,768]{1,0:T(8,128)(2,1)S(1)}, u32[]{:S(2)}, u32[]{:S(2)}) collective-permute-start(bf16[256,768]{1,0:T(8,128)(2,1)S(1)} %slice.137), channel_id=1, source_target_pairs={{0,8},{8,0},{16,24},{24,16},{1,9},{9,1},{17,25},{25,17},{2,10},{10... | collective-permute-start | bytes 1179656 | tf_op jit(solution)/shard_map/weight_grads/ppermute | solution.py:66
  577.6 19.2 %collective-permute-start.43 = (bf16[64,2048]{1,0:T(8,128)(2,1)S(1)}, bf16[64,2048]{1,0:T(8,128)(2,1)S(1)}, u32[]{:S(2)}, u32[]{:S(2)}) collective-permute-start(bf16[64,2048]{1,0:T(8,128)(2,1)S(1)} %copy-done.38), channel_id=1, source_target_pairs={{0,24},{8,16},{16,8},{24,0},{1,25},{9,17},{17,9},{25,1},{2,26},{10... | collective-permute-start | bytes 786440 | tf_op jit(solution)/shard_map/weight_grads/ppermute | solution.py:66
  579.7 18.3 %collective-permute-start.42 = (bf16[64,2048]{1,0:T(8,128)(2,1)S(1)}, bf16[64,2048]{1,0:T(8,128)(2,1)S(1)}, u32[]{:S(2)}, u32[]{:S(2)}) collective-permute-start(bf16[64,2048]{1,0:T(8,128)(2,1)S(1)} %copy-done.37), channel_id=1, source_target_pairs={{0,16},{8,24},{16,0},{24,8},{1,17},{9,25},{17,1},{25,9},{2,18},{10... | collective-permute-start | bytes 786440 | tf_op jit(solution)/shard_map/weight_grads/ppermute | solution.py:66
  582.7 19.7 %collective-permute-start.41 = (bf16[64,2048]{1,0:T(8,128)(2,1)S(1)}, bf16[64,2048]{1,0:T(8,128)(2,1)S(1)}, u32[]{:S(2)}, u32[]{:S(2)}) collective-permute-start(bf16[64,2048]{1,0:T(8,128)(2,1)S(1)} %convolution_convert_fusion.11), channel_id=1, source_target_pairs={{0,8},{8,0},{16,24},{24,16},{1,9},{9,1},{17,25},{25,17},{2,10},{10... | collective-permute-start | bytes 786440 | tf_op jit(solution)/shard_map/weight_grads/ppermute | solution.py:66
  585.7 19.7 %collective-permute-start.38 = (bf16[256,768]{1,0:T(8,128)(2,1)S(1)}, bf16[256,768]{1,0:T(8,128)(2,1)S(1)}, u32[]{:S(2)}, u32[]{:S(2)}) collective-permute-start(bf16[256,768]{1,0:T(8,128)(2,1)S(1)} %slice.141), channel_id=1, source_target_pairs={{0,16},{8,24},{16,0},{24,8},{1,17},{9,25},{17,1},{25,9},{2,18},{10... | collective-permute-start | bytes 1179656 | tf_op jit(solution)/shard_map/weight_grads/ppermute | solution.py:66
  596.8 17.1 %collective-permute-start.37 = (bf16[256,768]{1,0:T(8,128)(2,1)S(1)}, bf16[256,768]{1,0:T(8,128)(2,1)S(1)}, u32[]{:S(2)}, u32[]{:S(2)}) collective-permute-start(bf16[256,768]{1,0:T(8,128)(2,1)S(1)} %add_convert_fusion.7), channel_id=1, source_target_pairs={{0,16},{8,24},{16,0},{24,8},{1,17},{9,25},{17,1},{25,9},{2,18},{10... | collective-permute-start | bytes 1179656 | tf_op jit(solution)/shard_map/weight_grads/ppermute | solution.py:66
  598.0 15.9 %collective-permute-start.40 = (bf16[256,768]{1,0:T(8,128)(2,1)S(1)}, bf16[256,768]{1,0:T(8,128)(2,1)S(1)}, u32[]{:S(2)}, u32[]{:S(2)}) collective-permute-start(bf16[256,768]{1,0:T(8,128)(2,1)S(1)} %add_convert_fusion.6), channel_id=1, source_target_pairs={{0,8},{8,0},{16,24},{24,16},{1,9},{9,1},{17,25},{25,17},{2,10},{10... | collective-permute-start | bytes 1179656 | tf_op jit(solution)/shard_map/weight_grads/ppermute | solution.py:66
  615.0 33.6 %all-to-all-start.3 = ((bf16[8,64,768]{2,1,0:T(8,128)(2,1)}), bf16[8,64,768]{2,1,0:T(8,128)(2,1)S(1)}, u32[]{:S(2)}, u32[]{:S(2)}) async-start(bf16[8,64,768]{2,1,0:T(8,128)(2,1)} %bitcast.138), calls=%async_computation.6 | async-start | bytes 1572864 | tf_op jit(solution)/shard_map/weight_grads/all_to_all | solution.py:642
  625.4 23.2 %collective-permute-start.44 = (bf16[64,2048]{1,0:T(8,128)(2,1)}, bf16[64,2048]{1,0:T(8,128)(2,1)S(1)}, u32[]{:S(2)}, u32[]{:S(2)}) collective-permute-start(bf16[64,2048]{1,0:T(8,128)(2,1)} %convert_add_fusion.2), channel_id=1, source_target_pairs={{0,0},{1,4},{2,8},{3,12},{4,16},{5,20},{6,24},{7,28},{8,1},{9,5},{... | collective-permute-start | bytes 786440 | tf_op jit(solution)/shard_map/weight_grads/ppermute | solution.py:706
  (52 other events, 1043.3 us)
Sparse Core Ops, SparseCore 0:
  36.8 45.2 all-gather.4
  91.1 64.7 all-gather.6
  216.0 46.8 reduce-scatter.4
  267.7 47.8 all-gather.8
  344.9 51.4 reduce-scatter.6
  404.1 50.9 all-gather.10
  457.3 64.6 reduce-scatter.8
  567.1 46.2 reduce-scatter.10

commit v4 on v3

--- a/solution.py
+++ b/solution.py
@@ -190,32 +190,32 @@
     )(array)
 
 
-def rope_kernel(lin_ref, cos_ref, sin_ref, q_ref, kv_ref, *, heads):
-    width = heads * HDIM
+def project_kernel(normed_ref, weight_ref, cos_ref, sin_ref, q_ref, kv_ref, *, heads):
     cosine, sine = cos_ref[...], sin_ref[...]
+    linear = dot(normed_ref[...], weight_ref[...]).astype(BF16)
     for part in range(2 * heads):
-        columns = slice(part * HDIM, (part + 1) * HDIM)
-        value = lin_ref[:, columns].astype(F32)
+        value = linear[:, part * HDIM : (part + 1) * HDIM].astype(F32)
         turned = (value * cosine + pltpu.roll(value, HDIM // 2, 1) * sine).astype(BF16)
         if part < heads:
-            q_ref[:, columns] = turned
+            q_ref[:, part * HDIM : (part + 1) * HDIM] = turned
         else:
             start = 2 * (part - heads) * HDIM
             kv_ref[:, start : start + HDIM] = turned
-            columns = slice((part + heads) * HDIM, (part + heads + 1) * HDIM)
-            kv_ref[:, start + HDIM : start + 2 * HDIM] = lin_ref[:, columns]
-
-
-def rope(linear, cosine, sine, heads, block_rows):
-    rows = linear.shape[0]
+            first = (part + heads) * HDIM
+            kv_ref[:, start + HDIM : start + 2 * HDIM] = linear[:, first : first + HDIM]
+
+
+def project(normed, weight, cosine, sine, heads, block_rows):
+    rows, model_width = normed.shape
     width = heads * HDIM
     tile = min(256, block_rows)
     per_block = block_rows // tile
     return pl.pallas_call(
-        functools.partial(rope_kernel, heads=heads),
+        functools.partial(project_kernel, heads=heads),
         grid=(rows // tile,),
         in_specs=[
-            pl.BlockSpec((tile, 3 * width), lambda i: (i, 0)),
+            pl.BlockSpec((tile, model_width), lambda i: (i, 0)),
+            pl.BlockSpec(weight.shape, lambda i: (0, 0), pipeline_mode=pl.Buffered(1)),
             pl.BlockSpec((tile, HDIM), lambda i: (i % per_block, 0)),
             pl.BlockSpec((tile, HDIM), lambda i: (i % per_block, 0)),
         ],
@@ -227,12 +227,15 @@
             jax.ShapeDtypeStruct((rows, width), BF16),
             jax.ShapeDtypeStruct((rows, 2 * width), BF16),
         ],
-        name="rope",
-    )(linear, cosine, sine)
-
-
-def unrope_kernel(place_ref, dq_ref, cos_ref, sin_ref, *refs, heads, masks):
-    parts, out_ref = refs[:-1], refs[-1]
+        compiler_params=pltpu.CompilerParams(vmem_limit_bytes=VMEM_LIMIT),
+        name="project",
+    )(normed, weight, cosine, sine)
+
+
+def project_back_kernel(
+    place_ref, dq_ref, weight_ref, cos_ref, sin_ref, *refs, heads, masks
+):
+    parts, out_ref, sum_ref = refs[:-2], refs[-2], refs[-1]
     width = heads * HDIM
     me = place_ref[0]
     cosine, sine = cos_ref[...], sin_ref[...]
@@ -251,29 +254,87 @@
             total = total + jnp.where((me ^ mask) > me, ref[:, columns].astype(F32), 0.0)
         start = (1 + is_value) * width + head * HDIM
         out_ref[:, start : start + HDIM] = total.astype(BF16) if is_value else back(total)
-
-
-def unrope(place, dq, cosine, sine, parts, masks, heads, block_rows):
+    sum_ref[...] = dot_transposed(out_ref[...], weight_ref[...]).astype(BF16)
+
+
+def project_back(place, dq, weight, cosine, sine, parts, masks, heads, block_rows):
     rows = dq.shape[0]
     width = heads * HDIM
+    model_width = weight.shape[0]
     tile = min(256, block_rows)
     per_block = block_rows // tile
     return pl.pallas_call(
-        functools.partial(unrope_kernel, heads=heads, masks=masks),
+        functools.partial(project_back_kernel, heads=heads, masks=masks),
         grid_spec=pltpu.PrefetchScalarGridSpec(
             num_scalar_prefetch=1,
             grid=(rows // tile,),
             in_specs=[
                 pl.BlockSpec((tile, width), lambda i, *_: (i, 0)),
+                pl.BlockSpec(weight.shape, lambda i, *_: (0, 0), pipeline_mode=pl.Buffered(1)),
                 pl.BlockSpec((tile, HDIM), lambda i, *_: (i % per_block, 0)),
                 pl.BlockSpec((tile, HDIM), lambda i, *_: (i % per_block, 0)),
             ]
             + [pl.BlockSpec((tile, 2 * width), lambda i, *_: (i, 0))] * len(parts),
-            out_specs=pl.BlockSpec((tile, 3 * width), lambda i, *_: (i, 0)),
+            out_specs=[
+                pl.BlockSpec((tile, 3 * width), lambda i, *_: (i, 0)),
+                pl.BlockSpec((tile, model_width), lambda i, *_: (i, 0)),
+            ],
         ),
-        out_shape=jax.ShapeDtypeStruct((rows, 3 * width), BF16),
-        name="unrope",
-    )(place, dq, cosine, sine, *parts)
+        out_shape=[
+            jax.ShapeDtypeStruct((rows, 3 * width), BF16),
+            jax.ShapeDtypeStruct((rows, model_width), BF16),
+        ],
+        compiler_params=pltpu.CompilerParams(vmem_limit_bytes=VMEM_LIMIT),
+        name="project_back",
+    )(place, dq, weight, cosine, sine, *parts)
+
+
+def norm_kernel(in_ref, part_ref, sum_ref, low_ref):
+    total = in_ref[...].astype(F32) + part_ref[...].astype(F32)
+    sum_ref[...] = total
+    low_ref[...] = normalize_rows(total)[0].astype(BF16)
+
+
+def add_and_norm(inputs, part):
+    rows, width = inputs.shape
+    tile = min(64, rows)
+    spec = pl.BlockSpec((tile, width), lambda i: (i, 0))
+    return pl.pallas_call(
+        norm_kernel,
+        grid=(rows // tile,),
+        in_specs=[spec] * 2,
+        out_specs=[spec] * 2,
+        out_shape=[
+            jax.ShapeDtypeStruct((rows, width), F32),
+            jax.ShapeDtypeStruct((rows, width), BF16),
+        ],
+        compiler_params=pltpu.CompilerParams(vmem_limit_bytes=VMEM_LIMIT),
+        name="add_and_norm",
+    )(inputs, part)
+
+
+def norm_back_kernel(in_ref, upstream_ref, grad_ref, *out_refs):
+    normed, inverse = normalize_rows(in_ref[...].astype(F32))
+    total = upstream_ref[...].astype(F32) + normalize_back(
+        normed, inverse, grad_ref[...].astype(F32)
+    )
+    for ref in out_refs:
+        ref[...] = total.astype(ref.dtype)
+
+
+def norm_back(values, upstream, grad, dtypes):
+    rows, width = values.shape
+    tile = min(64, rows)
+    spec = pl.BlockSpec((tile, width), lambda i: (i, 0))
+    return pl.pallas_call(
+        norm_back_kernel,
+        grid=(rows // tile,),
+        in_specs=[spec] * 3,
+        out_specs=[spec] * len(dtypes),
+        out_shape=[jax.ShapeDtypeStruct((rows, width), dtype) for dtype in dtypes],
+        compiler_params=pltpu.CompilerParams(vmem_limit_bytes=VMEM_LIMIT),
+        name="norm_back",
+    )(values, upstream, grad)
 
 
 def visible(first_row, rows, first_key, keys, length):
@@ -435,7 +496,10 @@
         dq_shape = jax.ShapeDtypeStruct((rows, width), F32)
     else:
         dq_shape = jax.ShapeDtypeStruct((groups, HDIM, block_rows), F32)
-    dkv_shape = jax.ShapeDtypeStruct((rows, 2 * width), BF16)
+    dkv_shapes = [
+        pltpu.HBM((rows, 2 * width), BF16) if mask else jax.ShapeDtypeStruct((rows, 2 * width), BF16)
+        for mask in masks
+    ]
     return pl.pallas_call(
         functools.partial(
             backward_kernel,
@@ -456,7 +520,7 @@
             scratch_shapes=[pltpu.VMEM((HDIM, block_rows), F32)]
             + [pltpu.VMEM((block_rows, HDIM), F32)] * 2,
         ),
-        out_shape=[dq_shape] + [dkv_shape] * len(masks),
+        out_shape=[dq_shape] + dkv_shapes,
         compiler_params=pltpu.CompilerParams(vmem_limit_bytes=VMEM_LIMIT),
         name="attention_backward",
     )(place, query, out, grad, lse, *blocks, *([dq] if started else []))
@@ -544,18 +608,18 @@
     )
     valid = (me * block_rows + row_ids % block_rows < my_length).astype(F32)[:, None]
 
-    normed_one, inverse_one = normalize_rows(inputs)
+    normed_one = normalize_rows(inputs)[0]
     with jax.named_scope("projection_weights"):
         stacked = collect([query_weight, key_weight, value_weight], parts, 1, width)
         stacked = lax.all_to_all(stacked, "head", split_axis=0, concat_axis=0, tiled=True)
         stacked = stacked.reshape(band_rows, 3 * width)
         normed_start = after(normed_one.astype(BF16), stacked)
         near = send_near(stacked)
-        projection = gather_blk(stacked, near + send_far(near)).reshape(model_width, 3 * width)
+        far = send_far(near)
+        projection = gather_blk(stacked, near + far).reshape(model_width, 3 * width)
 
     with jax.named_scope("tokens_gather"):
-        upstream = cotangent[0].astype(F32) * valid
-        upstream_low = upstream.astype(BF16)
+        upstream_low = (cotangent[0].astype(F32) * valid).astype(BF16)
         normed_group = lax.all_gather(
             normed_start, "head", axis=0, tiled=True
         )
@@ -567,6 +631,7 @@
             ("blk", "head"),
             [(h * blocks + b, b * parts + h) for b in range(blocks) for h in range(parts)],
         )
+        output_rows = after(output_rows, far)
         output_near = send_near(output_rows)
         output = gather_blk(output_rows, output_near + send_far(output_near))
         output = output.reshape(width, model_width)
@@ -576,32 +641,26 @@
 
     cosine, sine = rotary_tables(me * block_rows + jnp.arange(block_rows))
     with jax.named_scope("projections"):
-        linear = dot(normed_group, projection).astype(BF16)
-        query, key_value = rope(linear, cosine, sine, heads, block_rows)
+        query, key_value = project(normed_group, projection, cosine, sine, heads, block_rows)
 
     with jax.named_scope("attention"):
         sent = [swapped(key_value, mask, lambda i, j: j > i) for mask in masks[1:]]
-        state = forward_attention(
-            place, query, [key_value], [0], None, False, heads, block_rows
-        )
-        both = lax.all_to_all(
-            after(both, state[0]), "head", split_axis=0, concat_axis=0, tiled=True
-        ).reshape(band_rows, 2 * blocks * chunk)
         upstream_group = lax.all_gather(
             after(upstream_low, normed_group), "head", axis=0, tiled=True
         )
-        state, sent, both, upstream_group = lax.optimization_barrier(
-            (state, sent, both, upstream_group)
+        both = lax.all_to_all(
+            after(both, upstream_group, *sent), "head", split_axis=0, concat_axis=0, tiled=True
+        ).reshape(band_rows, 2 * blocks * chunk)
+        attended, log_total = forward_attention(
+            place, query, [key_value] + sent, masks, None, True, heads, block_rows
+        )
+        down_near = send_near(after(down_weight, sent[0]))
+        joined_partial = dot(after(attended, down_near), output).astype(BF16)
+        joined_partial, down_near, both = lax.optimization_barrier(
+            (joined_partial, down_near, both)
         )
         near = send_near(both)
-        attended, log_total = forward_attention(
-            place, query, sent, masks[1:], state, True, heads, block_rows
-        )
-        down_near = send_near(after(down_weight, sent[0]))
-        attended, down_near = lax.optimization_barrier((attended, down_near))
-        joined = lax.psum_scatter(
-            dot(attended, output).astype(BF16), "head", scatter_dimension=0, tiled=True
-        )
+        joined = lax.psum_scatter(joined_partial, "head", scatter_dimension=0, tiled=True)
         joined, near = lax.optimization_barrier((joined, near))
         near, far = lax.optimization_barrier((near, send_far(near)))
         both = gather_blk(both, near + far).reshape(model_width, 2 * blocks * chunk)
@@ -610,33 +669,31 @@
         down = gather_blk(down_weight, down_near + down_far).reshape(blocks * chunk, model_width)
 
     with jax.named_scope("feed_forward"):
-        residual = inputs + joined.astype(F32)
-        normed_two, inverse_two = normalize_rows(residual)
-        normed_two_group = lax.all_gather(normed_two.astype(BF16), "head", axis=0, tiled=True)
+        residual, normed_two = add_and_norm(tokens[0], joined)
+        normed_two_group = lax.all_gather(normed_two, "head", axis=0, tiled=True)
         mixed, both_back, normed_two_partial = feed_forward(
             normed_two_group, upstream_group, both, down
         )
         normed_two_grad = lax.psum_scatter(
             normed_two_partial, "head", scatter_dimension=0, tiled=True
-        ).astype(F32)
+        )
         down_partial = dot(mixed, down).astype(BF16)
 
         def band(values, place_of):
             return lax.dynamic_slice_in_dim(values, place_of * band_rows, band_rows, 1)
 
         both_terms = terms_of(lambda j: outer_sum(band(normed_two_group, j), both_back))
-        both_passed, both_own = sum_pass(both_terms), sum_own(both_terms)
+        both_passed = sum_pass(both_terms)
         down_terms = terms_of(
             lambda j: outer_sum(lax.dynamic_slice_in_dim(mixed, j * chunk, chunk, 1), upstream_group)
         )
-        normed_two_grad, down_partial, both_terms, both_passed, both_own, down_terms = (
+        normed_two_grad, down_partial, both_terms, both_passed, down_terms = (
             lax.optimization_barrier(
-                (normed_two_grad, down_partial, both_terms, both_passed, both_own, down_terms)
+                (normed_two_grad, down_partial, both_terms, both_passed, down_terms)
             )
         )
 
-    residual_grad = upstream + normalize_back(normed_two, inverse_two, normed_two_grad)
-    residual_low = residual_grad.astype(BF16)
+    residual_grad, residual_low = norm_back(residual, upstream_low, normed_two_grad, (F32, BF16))
 
     def to_shards(summed):
         return lax.all_to_all(
@@ -649,13 +706,12 @@
 
     with jax.named_scope("attention_back"):
         residual_group = lax.all_gather(residual_low, "head", axis=0, tiled=True)
-        both_far = sum_far(both_terms, both_passed)
-        both_far, down_terms = lax.optimization_barrier((both_far, down_terms))
+        both_own, both_far = sum_own(both_terms), sum_far(both_terms, both_passed)
         both_sum = sum_end(both_terms, both_own, both_far).astype(BF16)
+        residual_group, both_sum, down_terms = lax.optimization_barrier(
+            (residual_group, both_sum, down_terms)
+        )
         down_passed, down_own = sum_pass(down_terms), sum_own(down_terms)
-        residual_group, both_sum, down_terms, down_passed, down_own = lax.optimization_barrier(
-            (residual_group, both_sum, down_terms, down_passed, down_own)
-        )
         attended_grad = dot_transposed(residual_group, output).astype(BF16)
         down_act = lax.psum_scatter(
             after(down_partial, residual_group), "head", scatter_dimension=0, tiled=True
@@ -668,8 +724,9 @@
         key_value_grads = [pairs[-1]] + [
             swapped(pairs[order.index(mask)], mask, lambda i, j: j < i) for mask in masks[1:]
         ]
-        down_far = sum_far(down_terms, down_passed)
-        query_grad, both_sum, down_far = lax.optimization_barrier((query_grad, both_sum, down_far))
+        query_grad, both_sum, down_passed, down_own = lax.optimization_barrier(
+            (query_grad, both_sum, down_passed, down_own)
+        )
         hidden_shards = to_shards(both_sum)
         residual_group = after(residual_group, key_value_grads[1])
         output_terms = terms_of(
@@ -680,29 +737,31 @@
         query_grad, key_value_grads, hidden_shards, output_terms = lax.optimization_barrier(
             (query_grad, key_value_grads, hidden_shards, output_terms)
         )
-        down_sum = sum_end(down_terms, down_own, down_far)
         down_act = after(down_act, query_grad)
         layer_output = ((residual + down_act) * valid).astype(BF16)[None]
-        projection_back = unrope(
-            place, query_grad, cosine, sine, key_value_grads, masks,
+        projection_back, normed_one_partial = project_back(
+            place, query_grad, projection, cosine, sine, key_value_grads, masks,
             heads, block_rows,
         )
         normed_one_grad = lax.psum_scatter(
-            dot_transposed(projection_back, projection).astype(BF16),
-            "head",
-            scatter_dimension=0,
-            tiled=True,
-        ).astype(F32)
-        tokens_grad = (
-            residual_grad + normalize_back(normed_one, inverse_one, normed_one_grad)
-        ).astype(BF16)[None]
+            normed_one_partial, "head", scatter_dimension=0, tiled=True
+        )
+        (tokens_grad,) = norm_back(tokens[0], residual_grad, normed_one_grad, (BF16,))
+        tokens_grad = tokens_grad[None]
 
     with jax.named_scope("weight_grads"):
 
         gate_grad, up_grad = spread(hidden_shards, 2, parts, blocks, chunk)
         terms = terms_of(lambda j: outer_sum(band(normed_group, j), projection_back))
-        summed = sum_end(terms, sum_own(terms), sum_far(terms, sum_pass(terms)))
-        summed, output_part = lax.optimization_barrier((summed, sum_to_owner(output_terms)))
+        passed, own = sum_pass(terms), sum_own(terms)
+        passed, own, terms, output_terms, gate_grad, up_grad = lax.optimization_barrier(
+            (passed, own, terms, output_terms, gate_grad, up_grad)
+        )
+        summed = sum_end(terms, own, sum_far(terms, passed))
+        summed, output_part, down_passed = lax.optimization_barrier(
+            (summed, sum_to_owner(output_terms), down_passed)
+        )
+        down_sum = sum_end(down_terms, down_own, sum_far(down_terms, down_passed))
         output_grad = lax.ppermute(
             output_part.astype(BF16),
             ("blk", "head"),

time: 667 us -> 655 us (0.982)
  other arithmetic: 44.8 us -> 24.5 us
  waiting for transfers between devices: 290 us -> 304 us
  starting transfers between devices: 101 us -> 89.5 us
  local copies, waits for them, and re-layouts: 60.6 us -> 68.9 us
  matrix products: 66.6 us -> 58.6 us
  Pallas kernels: 79.2 us -> 86.7 us
    ppermute x43, waiting for transfers between devices: 209 us -> 224 us  [swapped(): return lax.ppermute(value, 'blk', pairs)]
    unnamed x86 -> x142, local copies, waits for them, and re-layouts: 14.8 us -> 27 us
    ppermute x43, starting transfers between devices: 60.3 us -> 48.1 us  [swapped(): return lax.ppermute(value, 'blk', pairs)]
    pallas_call x2 -> x5, Pallas kernels: 9.71 us -> 18.8 us  [the longest x1 8.41 us: project_back(): pl.pallas_call(functools.partial(project_back_kernel, heads=heads, masks=...]
    dot_general x2 -> x1, matrix products: 11.6 us -> 2.74 us  [dot_transposed(): lax.dot_general(left, right, (((1,), (1,)), ((), ())), preferred_element_...]
    dot_general x16, matrix products: 35.8 us -> 42.9 us  [outer_sum(): lax.dot_general(left, right, (((0,), (0,)), ((), ())), preferred_element_...]
    all_to_all x1, waiting for transfers between devices: 9.83 us -> 16.7 us  [local(): lax.all_to_all(after(both, upstream_group, *sent), 'head', split_axis=0,...]
    dot_general x3 -> x2, matrix products: 19.1 us -> 13 us  [dot(): return jnp.dot(left, right, preferred_element_type=F32)]
  transfers between devices with their start and end apart: 57 -> 57, of which waited for: 34 -> 31; matrix products, arithmetic and copies ran while one was open for 22% -> 19% of each run, Pallas kernels for 7% -> 8%
where the time goes in v4:
time: 655 us; the launch traced here: 648 us
  waiting for transfers between devices  304 us (46%)
  starting transfers between devices  89.5 us (14%)
  Pallas kernels  86.7 us (13%)
  local copies, waits for them, and re-layouts  68.9 us (11%)
  matrix products  58.6 us (9%)
  other arithmetic  24.5 us (4%)
  between operations  16.1 us (2%)
    ppermute x43, waiting for transfers between devices, swapped(): return lax.ppermute(value, 'blk', pairs)  224 us
    ppermute x43, starting transfers between devices, swapped(): return lax.ppermute(value, 'blk', pairs)  48.1 us
    dot_general x16, matrix products, outer_sum(): lax.dot_general(left, right, (((0,), (0,)), ((), ())), preferred_element_...  42.9 us
    pallas_call x1, Pallas kernels, feed_forward(): pl.pallas_call(functools.partial(feed_kernel, columns=min(256, hidden)),...  29.3 us
    unnamed x142, local copies, waits for them, and re-layouts  27 us
    pallas_call x1, Pallas kernels, backward_attention(): pl.pallas_call(functools.partial(backward_kernel, masks=masks, started=st...  19.3 us
    dynamic_update_slice x16, local copies, waits for them, and re-layouts, gather_blk(): whole = lax.dynamic_update_slice(whole, piece[None], start)  17.4 us
    all_to_all x2, waiting for transfers between devices, to_shards(): lax.all_to_all(summed.astype(BF16).reshape(parts, shard_rows, summed.shap...  17.3 us
  transfers between devices with their start and end apart: 57, of which 31 were waited for; matrix products, arithmetic and copies ran while one was open for 19% of the time, Pallas kernels for 8%

profile of v4, /device:TPU:5, one launch (start us, length us, event | category | flops | bytes accessed | tf_op | source)
XLA Modules:
  0.0 648.1 jit_solution(3920204408690466086)
XLA Ops:
  11.0 5.5 all-to-all-start
  20.2 16.6 %all-to-all-done = bf16[8,64,768]{2,1,0:T(8,128)(2,1)} async-done(((bf16[8,64,768]{2,1,0:T(8,128)(2,1)}), bf16[8,64,768]{2,1,0:T(8,128)(2,1)}, u32[]{:S(2)}, u32[]{:S(2)}) %all-to-all-start) | async-done | bytes 786464 | tf_op jit(solution)/shard_map/projection_weights/all_to_all | solution.py:614
  40.0 3.4 collective-permute-start.4
  44.9 10.5 %collective-permute-done = bf16[512,768]{1,0:T(8,128)(2,1)} collective-permute-done((bf16[512,768]{1,0:T(8,128)(2,1)}, bf16[512,768]{1,0:T(8,128)(2,1)}, u32[]{:S(2)}, u32[]{:S(2)}) %collective-permute-start) | collective-permute-done | bytes 786464 | tf_op jit(solution)/shard_map/projection_weights/ppermute | solution.py:66
  56.5 4.6 collective-permute-start.2
  71.6 3.3 collective-permute-start.6
  77.5 3.4 collective-permute-start.7
  88.6 6.1 project.1
  103.2 11.6 %collective-permute-done.9.refs_1_.refs_2_ = bf16[1024,512]{1,0:T(8,128)(2,1)S(1)} collective-permute-done((bf16[1024,512]{1,0:T(8,128)(2,1)S(1)}, bf16[1024,512]{1,0:T(8,128)(2,1)S(1)}, u32[]{:S(2)}, u32[]{:S(2)}) %collective-permute-start.9) | collective-permute-done | bytes 1048608 | tf_op jit(solution)/shard_map/attention/ppermute | solution.py:66
  114.8 35.5 %collective-permute-done.10.refs_2_.refs_1_ = bf16[1024,512]{1,0:T(8,128)(2,1)S(1)} collective-permute-done((bf16[1024,512]{1,0:T(8,128)(2,1)S(1)}, bf16[1024,512]{1,0:T(8,128)(2,1)S(1)}, u32[]{:S(2)}, u32[]{:S(2)}) %collective-permute-start.10) | collective-permute-done | bytes 1048608 | tf_op jit(solution)/shard_map/attention/ppermute | solution.py:66
  152.4 12.1 %all-to-all-start.1 = ((bf16[8,64,2048]{2,1,0:T(8,128)(2,1)}), bf16[8,64,2048]{2,1,0:T(8,128)(2,1)}, u32[]{:S(2)}, u32[]{:S(2)}) async-start(bf16[8,64,2048]{2,1,0:T(8,128)(2,1)} %collect.3), calls=%async_computation.1 | async-start | bytes 4194304 | tf_op jit(solution)/shard_map/attention/all_to_all | solution.py:651
  167.1 13.4 %attention_forward.1 = (bf16[1024,256]{1,0:T(8,128)(2,1)S(1)}, f32[2,1,1024]{2,1,0:T(1,128)S(1)}) custom-call(s32[2]{0:T(128)S(1)} %pad_add_fusion.place_ref, bf16[1024,256]{1,0:T(8,128)(2,1)S(1)} %copy-done.20, bf16[1024,512]{1,0:T(8,128)(2,1)S(1)} %copy-done.11, bf16[1024,512]{1,0:T(8,128)(2,1)S(1)} %collective-permute-done.9.refs_1_.refs_2_, ...), custom_call_target="tpu_custom_call" | custom-call | tf_op jit(solution)/shard_map/attention/attention_forward/pallas_call | solution.py:418
  180.5 9.0 %collective-permute-done.12 = bf16[256,2048]{1,0:T(8,128)(2,1)S(1)} collective-permute-done((bf16[256,2048]{1,0:T(8,128)(2,1)}, bf16[256,2048]{1,0:T(8,128)(2,1)S(1)}, u32[]{:S(2)}, u32[]{:S(2)}) %collective-permute-start.12) | collective-permute-done | bytes 1048608 | tf_op jit(solution)/shard_map/attention/ppermute | solution.py:66
  191.5 4.6 convolution_convert_fusion
  196.1 16.7 %all-to-all-done.1 = bf16[8,64,2048]{2,1,0:T(8,128)(2,1)} async-done(((bf16[8,64,2048]{2,1,0:T(8,128)(2,1)}), bf16[8,64,2048]{2,1,0:T(8,128)(2,1)}, u32[]{:S(2)}, u32[]{:S(2)}) %all-to-all-start.1) | async-done | bytes 2097184 | tf_op jit(solution)/shard_map/attention/all_to_all | solution.py:651
  213.0 46.5 %collective-permute-done.14 = bf16[512,2048]{1,0:T(8,128)(2,1)} collective-permute-done((bf16[512,2048]{1,0:T(8,128)(2,1)}, bf16[512,2048]{1,0:T(8,128)(2,1)}, u32[]{:S(2)}, u32[]{:S(2)}) %collective-permute-start.14) | collective-permute-done | bytes 2097184 | tf_op jit(solution)/shard_map/attention/ppermute | solution.py:66
  270.2 4.3 broadcast_in_dim.119
  274.5 3.4 bitcast_dynamic-update-slice_fusion.2
  277.9 8.3 %collective-permute-done.16 = bf16[256,2048]{1,0:T(8,128)(2,1)S(1)} collective-permute-done((bf16[256,2048]{1,0:T(8,128)(2,1)S(1)}, bf16[256,2048]{1,0:T(8,128)(2,1)S(1)}, u32[]{:S(2)}, u32[]{:S(2)}) %collective-permute-start.16) | collective-permute-done | bytes 1048608 | tf_op jit(solution)/shard_map/attention/ppermute | solution.py:66
  290.0 3.1 bitcast_dynamic-update-slice_fusion.1
  293.1 3.1 bitcast_dynamic-update-slice_fusion
  302.8 7.4 %all-gather.9.cloned.1.call-done.normed_ref = bf16[1024,2048]{1,0:T(8,128)(2,1)} async-done(((bf16[128,2048]{1,0:T(8,128)(2,1)}), bf16[1024,2048]{1,0:T(8,128)(2,1)}) %all-gather.9.cloned.1.call-update) | async-done | bytes 4194320 | tf_op jit(solution)/shard_map/feed_forward/all_gather | solution.py:673
  310.2 29.3 %feed_forward.1 = (bf16[1024,1024]{1,0:T(8,128)(2,1)S(1)}, bf16[1024,2048]{1,0:T(8,128)(2,1)}, bf16[1024,2048]{1,0:T(8,128)(2,1)}) custom-call(bf16[1024,2048]{1,0:T(8,128)(2,1)} %all-gather.9.cloned.1.call-done.normed_ref, bf16[1024,2048]{1,0:T(8,128)(2,1)} %all-gather.7.cloned.1.call-done.grad_ref, bf16[2048,2048]{1,0:T(8,128)(2,1)} %bitcast.23.both_ref, ...), custom_call_target="tpu_custom_call" | custom-call | tf_op jit(solution)/shard_map/feed_forward/feed_forward/pallas_call | solution.py:559
  341.1 5.0 convolution_convert_fusion.2
  356.2 4.6 fusion.13
  360.8 3.8 convolution_convert_fusion.4
  364.6 3.8 convolution_convert_fusion.3
  368.4 2.8 convolution_convert_fusion.5
  371.2 8.4 %convolution_convert_fusion.1 = bf16[1024,2048]{1,0:T(8,128)(2,1)} fusion(bf16[1024,1024]{1,0:T(8,128)(2,1)S(1)} %copy-done.39, bf16[1024,2048]{1,0:T(8,128)(2,1)} %bitcast.29.down_ref), kind=kOutput, calls=%fused_computation.1 | convolution fusion | flops 4297064448 | bytes 10485760 | tf_op jit(solution)/shard_map/feed_forward/dot_general | solution.py:52
  379.6 8.4 %reduce-scatter.7.cloned.1.call-done.grad_ref = bf16[128,2048]{1,0:T(8,128)(2,1)} async-done(((bf16[1024,2048]{1,0:T(8,128)(2,1)}), bf16[128,2048]{1,0:T(8,128)(2,1)}) %reduce-scatter.7.cloned.1.call-update) | async-done | bytes 524304 | tf_op jit(solution)/shard_map/feed_forward/reduce_scatter | solution.py:677
  399.9 17.2 %collective-permute-done.23 = bf16[256,2048]{1,0:T(8,128)(2,1)S(1)} collective-permute-done((bf16[256,2048]{1,0:T(8,128)(2,1)S(1)}, bf16[256,2048]{1,0:T(8,128)(2,1)S(1)}, u32[]{:S(2)}, u32[]{:S(2)}) %collective-permute-start.23) | collective-permute-done | bytes 1048608 | tf_op jit(solution)/shard_map/attention_back/ppermute | solution.py:66
  417.2 22.4 %collective-permute-done.25 = bf16[256,2048]{1,0:T(8,128)(2,1)S(1)} collective-permute-done((bf16[256,2048]{1,0:T(8,128)(2,1)S(1)}, bf16[256,2048]{1,0:T(8,128)(2,1)S(1)}, u32[]{:S(2)}, u32[]{:S(2)}) %collective-permute-start.25) | collective-permute-done | bytes 1048608 | tf_op jit(solution)/shard_map/attention_back/ppermute | solution.py:66
  446.9 2.7 convolution_convert_fusion.14.do_ref
  449.7 19.3 %attention_backward.1 = (f32[1024,256]{1,0:T(8,128)S(1)}, bf16[1024,512]{1,0:T(8,128)(2,1)}, bf16[1024,512]{1,0:T(8,128)(2,1)}, bf16[1024,512]{1,0:T(8,128)(2,1)}, bf16[1024,512]{1,0:T(8,128)(2,1)S(1)}) custom-call(s32[2]{0:T(128)S(1)} %pad_add_fusion.place_ref, bf16[1024,256]{1,0:T(8,128)(2,1)S(1)} %copy-done.21, ...), custom_call_target="tpu_custom_call" | custom-call | tf_op jit(solution)/shard_map/attention_back/attention_backward/pallas_call | solution.py:503
  472.6 9.3 %all-to-all-start.2 = ((bf16[8,64,2048]{2,1,0:T(8,128)(2,1)}), bf16[8,64,2048]{2,1,0:T(8,128)(2,1)S(1)}, u32[]{:S(2)}, u32[]{:S(2)}) async-start(bf16[8,64,2048]{2,1,0:T(8,128)(2,1)} %bitcast.88), calls=%async_computation.5 | async-start | bytes 4194304 | tf_op jit(solution)/shard_map/attention_back/all_to_all | solution.py:699
  484.9 3.4 collective-permute-start.32
  488.3 25.2 %collective-permute-done.30.refs_1_ = bf16[1024,512]{1,0:T(8,128)(2,1)} collective-permute-done((bf16[1024,512]{1,0:T(8,128)(2,1)}, bf16[1024,512]{1,0:T(8,128)(2,1)}, u32[]{:S(2)}, u32[]{:S(2)}) %collective-permute-start.30) | collective-permute-done | bytes 1048608 | tf_op jit(solution)/shard_map/attention_back/ppermute | solution.py:66
  513.4 3.1 convolution_convert_fusion.10
  522.7 17.3 %all-to-all-done.2.in_ref = bf16[8,64,2048]{2,1,0:T(8,128)(2,1)S(1)} async-done(((bf16[8,64,2048]{2,1,0:T(8,128)(2,1)}), bf16[8,64,2048]{2,1,0:T(8,128)(2,1)S(1)}, u32[]{:S(2)}, u32[]{:S(2)}) %all-to-all-start.2) | async-done | bytes 2097184 | tf_op jit(solution)/shard_map/attention_back/all_to_all | solution.py:699
  545.7 8.4 %project_back.1 = (bf16[1024,768]{1,0:T(8,128)(2,1)}, bf16[1024,2048]{1,0:T(8,128)(2,1)}) custom-call(s32[2]{0:T(128)S(1)} %pad_add_fusion.place_ref, f32[1024,256]{1,0:T(8,128)S(1)} %copy-done.23, bf16[2048,768]{1,0:T(8,128)(2,1)} %bitcast.85, f32[1024,128]{1,0:T(8,128)S(1)} %copy-done.4, f32[1024,128]{1,0:T(8,128)S(1)} %copy-done.6, ...), custom_call_target="tpu_custom_call" | custom-call | tf_op jit(solution)/shard_map/attention_back/project_back/pallas_call | solution.py:266
  554.2 2.9 convolution_convert_fusion.13
  568.4 7.6 %collective-permute-done.35 = bf16[256,768]{1,0:T(8,128)(2,1)S(1)} collective-permute-done((bf16[256,768]{1,0:T(8,128)(2,1)S(1)}, bf16[256,768]{1,0:T(8,128)(2,1)S(1)}, u32[]{:S(2)}, u32[]{:S(2)}) %collective-permute-start.35) | collective-permute-done | bytes 393248 | tf_op jit(solution)/shard_map/weight_grads/ppermute | solution.py:66
  580.4 3.7 collective-permute-done.41
  584.2 6.3 collective-permute-done.40
  591.2 7.6 %collective-permute-done.37 = bf16[256,768]{1,0:T(8,128)(2,1)S(1)} collective-permute-done((bf16[256,768]{1,0:T(8,128)(2,1)S(1)}, bf16[256,768]{1,0:T(8,128)(2,1)S(1)}, u32[]{:S(2)}, u32[]{:S(2)}) %collective-permute-start.37) | collective-permute-done | bytes 393248 | tf_op jit(solution)/shard_map/weight_grads/ppermute | solution.py:66
  603.7 4.4 all-to-all-start.3
  608.2 6.2 collective-permute-start.42
  624.5 13.4 %collective-permute-done.42 = bf16[64,2048]{1,0:T(8,128)(2,1)} collective-permute-done((bf16[64,2048]{1,0:T(8,128)(2,1)}, bf16[64,2048]{1,0:T(8,128)(2,1)}, u32[]{:S(2)}, u32[]{:S(2)}) %collective-permute-start.42) | collective-permute-done | bytes 262176 | tf_op jit(solution)/shard_map/weight_grads/ppermute | solution.py:765
  (316 shorter events, 153.1 us)
Async XLA Ops:
  11.0 25.8 %all-to-all-start = ((bf16[8,64,768]{2,1,0:T(8,128)(2,1)}), bf16[8,64,768]{2,1,0:T(8,128)(2,1)}, u32[]{:S(2)}, u32[]{:S(2)}) async-start(bf16[8,64,768]{2,1,0:T(8,128)(2,1)} %collect.2), calls=%async_computation | async-start | bytes 1572864 | tf_op jit(solution)/shard_map/projection_weights/all_to_all | solution.py:614
  16.6 69.7 %all-gather.5.cloned.1.call-start = ((), (), s32[]{:S(2)}) async-start(), calls=%async_computation.8 | async-start | bytes 4718592 | tf_op jit(solution)/shard_map/tokens_gather/all_gather | solution.py:623
  36.8 115.5 %all-gather.7.cloned.1.call-start = ((), (), s32[]{:S(2)}) async-start(), calls=%async_computation.9 | async-start | bytes 4718592 | tf_op jit(solution)/shard_map/attention/all_gather | solution.py:648
  36.9 18.6 %collective-permute-start = (bf16[512,768]{1,0:T(8,128)(2,1)}, bf16[512,768]{1,0:T(8,128)(2,1)}, u32[]{:S(2)}, u32[]{:S(2)}) collective-permute-start(bf16[512,768]{1,0:T(8,128)(2,1)} %bitcast.2), channel_id=1, source_target_pairs={{0,8},{8,0},{16,24},{24,16},{1,9},{9,1},{17,25},{25,17},{2,10},{10... | collective-permute-start | bytes 2359304 | tf_op jit(solution)/shard_map/projection_weights/ppermute | solution.py:66
  38.2 22.9 %collective-permute-start.1 = (bf16[512,768]{1,0:T(8,128)(2,1)}, bf16[512,768]{1,0:T(8,128)(2,1)}, u32[]{:S(2)}, u32[]{:S(2)}) collective-permute-start(bf16[512,768]{1,0:T(8,128)(2,1)} %bitcast.2), channel_id=1, source_target_pairs={{0,16},{8,24},{16,0},{24,8},{1,17},{9,25},{17,1},{25,9},{2,18},{10... | collective-permute-start | bytes 2359304 | tf_op jit(solution)/shard_map/projection_weights/ppermute | solution.py:66
  40.0 27.0 %collective-permute-start.4 = (bf16[64,2048]{1,0:T(8,128)(2,1)S(1)}, bf16[64,2048]{1,0:T(8,128)(2,1)S(1)}, u32[]{:S(2)}, u32[]{:S(2)}) collective-permute-start(bf16[64,2048]{1,0:T(8,128)(2,1)S(1)} %copy-done.70), channel_id=1, source_target_pairs={{0,0},{4,1},{8,2},{12,3},{16,4},{20,5},{24,6},{28,7},{1,8},{5,9},{... | collective-permute-start | bytes 786440 | tf_op jit(solution)/shard_map/hidden_weights/ppermute | solution.py:629
  56.5 11.2 %collective-permute-start.2 = (bf16[256,768]{1,0:T(8,128)(2,1)S(1)}, bf16[256,768]{1,0:T(8,128)(2,1)S(1)}, u32[]{:S(2)}, u32[]{:S(2)}) collective-permute-start(bf16[256,768]{1,0:T(8,128)(2,1)S(1)} %slice.128), channel_id=1, source_target_pairs={{0,16},{8,24},{16,0},{24,8},{1,17},{9,25},{17,1},{25,9},{2,18},{10... | collective-permute-start | bytes 1179656 | tf_op jit(solution)/shard_map/projection_weights/ppermute | solution.py:66
  95.5 19.3 %collective-permute-start.9 = (bf16[1024,512]{1,0:T(8,128)(2,1)S(1)}, bf16[1024,512]{1,0:T(8,128)(2,1)S(1)}, u32[]{:S(2)}, u32[]{:S(2)}) collective-permute-start(bf16[1024,512]{1,0:T(8,128)(2,1)S(1)} %get-tuple-element.121.refs_0_.refs_3_), channel_id=1, source_target_pairs={{0,8},{16,24},{1,9},{17,25},{2,10},{18,26},{3,11},{19,27},{4,12},{... | collective-permute-start | bytes 3145736 | tf_op jit(solution)/shard_map/attention/ppermute | solution.py:66
  98.0 52.3 %collective-permute-start.10 = (bf16[1024,512]{1,0:T(8,128)(2,1)S(1)}, bf16[1024,512]{1,0:T(8,128)(2,1)S(1)}, u32[]{:S(2)}, u32[]{:S(2)}) collective-permute-start(bf16[1024,512]{1,0:T(8,128)(2,1)S(1)} %get-tuple-element.121.refs_0_.refs_3_), channel_id=1, source_target_pairs={{0,16},{8,24},{1,17},{9,25},{2,18},{10,26},{3,19},{11,27},{4,20},{... | collective-permute-start | bytes 3145736 | tf_op jit(solution)/shard_map/attention/ppermute | solution.py:66
  99.3 52.1 %collective-permute-start.11 = (bf16[1024,512]{1,0:T(8,128)(2,1)S(1)}, bf16[1024,512]{1,0:T(8,128)(2,1)S(1)}, u32[]{:S(2)}, u32[]{:S(2)}) collective-permute-start(bf16[1024,512]{1,0:T(8,128)(2,1)S(1)} %get-tuple-element.121.refs_0_.refs_3_), channel_id=1, source_target_pairs={{0,24},{8,16},{1,25},{9,17},{2,26},{10,18},{3,27},{11,19},{4,28},{... | collective-permute-start | bytes 3145736 | tf_op jit(solution)/shard_map/attention/ppermute | solution.py:66
  152.4 60.4 %all-to-all-start.1 = ((bf16[8,64,2048]{2,1,0:T(8,128)(2,1)}), bf16[8,64,2048]{2,1,0:T(8,128)(2,1)}, u32[]{:S(2)}, u32[]{:S(2)}) async-start(bf16[8,64,2048]{2,1,0:T(8,128)(2,1)} %collect.3), calls=%async_computation.1 | async-start | bytes 4194304 | tf_op jit(solution)/shard_map/attention/all_to_all | solution.py:651
  164.5 95.1 %reduce-scatter.5.cloned.1.call-start = ((), (), s32[]{:S(2)}) async-start(), calls=%async_computation.10 | async-start | bytes 4718592 | tf_op jit(solution)/shard_map/attention/reduce_scatter | solution.py:663
  164.5 25.0 %collective-permute-start.12 = (bf16[256,2048]{1,0:T(8,128)(2,1)}, bf16[256,2048]{1,0:T(8,128)(2,1)S(1)}, u32[]{:S(2)}, u32[]{:S(2)}) collective-permute-start(bf16[256,2048]{1,0:T(8,128)(2,1)} %param.18), channel_id=1, source_target_pairs={{0,8},{8,0},{16,24},{24,16},{1,9},{9,1},{17,25},{25,17},{2,10},{10... | collective-permute-start | bytes 3145736 | tf_op jit(solution)/shard_map/attention/ppermute | solution.py:66
  164.5 25.0 %collective-permute-start.13 = (bf16[256,2048]{1,0:T(8,128)(2,1)}, bf16[256,2048]{1,0:T(8,128)(2,1)S(1)}, u32[]{:S(2)}, u32[]{:S(2)}) collective-permute-start(bf16[256,2048]{1,0:T(8,128)(2,1)} %param.18), channel_id=1, source_target_pairs={{0,16},{8,24},{16,0},{24,8},{1,17},{9,25},{17,1},{25,9},{2,18},{10... | collective-permute-start | bytes 3145736 | tf_op jit(solution)/shard_map/attention/ppermute | solution.py:66
  212.8 97.4 %all-gather.9.cloned.1.call-start = ((), (), s32[]{:S(2)}) async-start(), calls=%async_computation.11 | async-start | bytes 4718592 | tf_op jit(solution)/shard_map/feed_forward/all_gather | solution.py:673
  212.9 46.7 %collective-permute-start.14 = (bf16[512,2048]{1,0:T(8,128)(2,1)}, bf16[512,2048]{1,0:T(8,128)(2,1)}, u32[]{:S(2)}, u32[]{:S(2)}) collective-permute-start(bf16[512,2048]{1,0:T(8,128)(2,1)} %bitcast.17), channel_id=1, source_target_pairs={{0,8},{8,0},{16,24},{24,16},{1,9},{9,1},{17,25},{25,17},{2,10},{10... | collective-permute-start | bytes 6291464 | tf_op jit(solution)/shard_map/attention/ppermute | solution.py:66
  212.9 46.7 %collective-permute-start.15 = (bf16[512,2048]{1,0:T(8,128)(2,1)}, bf16[512,2048]{1,0:T(8,128)(2,1)}, u32[]{:S(2)}, u32[]{:S(2)}) collective-permute-start(bf16[512,2048]{1,0:T(8,128)(2,1)} %bitcast.17), channel_id=1, source_target_pairs={{0,16},{8,24},{16,0},{24,8},{1,17},{9,25},{17,1},{25,9},{2,18},{10... | collective-permute-start | bytes 6291464 | tf_op jit(solution)/shard_map/attention/ppermute | solution.py:66
  261.9 126.0 %reduce-scatter.7.cloned.1.call-start = ((), (), s32[]{:S(2)}) async-start(), calls=%async_computation.12 | async-start | bytes 4718592 | tf_op jit(solution)/shard_map/feed_forward/reduce_scatter | solution.py:677
  263.6 22.6 %collective-permute-start.16 = (bf16[256,2048]{1,0:T(8,128)(2,1)S(1)}, bf16[256,2048]{1,0:T(8,128)(2,1)S(1)}, u32[]{:S(2)}, u32[]{:S(2)}) collective-permute-start(bf16[256,2048]{1,0:T(8,128)(2,1)S(1)} %slice.100), channel_id=1, source_target_pairs={{0,16},{8,24},{16,0},{24,8},{1,17},{9,25},{17,1},{25,9},{2,18},{10... | collective-permute-start | bytes 3145736 | tf_op jit(solution)/shard_map/attention/ppermute | solution.py:66
  265.3 22.4 %collective-permute-start.17 = (bf16[256,2048]{1,0:T(8,128)(2,1)S(1)}, bf16[256,2048]{1,0:T(8,128)(2,1)S(1)}, u32[]{:S(2)}, u32[]{:S(2)}) collective-permute-start(bf16[256,2048]{1,0:T(8,128)(2,1)S(1)} %slice.101), channel_id=1, source_target_pairs={{0,8},{8,0},{16,24},{24,16},{1,9},{9,1},{17,25},{25,17},{2,10},{10... | collective-permute-start | bytes 3145736 | tf_op jit(solution)/shard_map/attention/ppermute | solution.py:66
  287.8 10.6 %collective-permute-start.18 = (bf16[128,2048]{1,0:T(8,128)(2,1)S(1)}, bf16[128,2048]{1,0:T(8,128)(2,1)S(1)}, u32[]{:S(2)}, u32[]{:S(2)}) collective-permute-start(bf16[128,2048]{1,0:T(8,128)(2,1)S(1)} %slice.102), channel_id=1, source_target_pairs={{0,16},{8,24},{16,0},{24,8},{1,17},{9,25},{17,1},{25,9},{2,18},{10... | collective-permute-start | bytes 1572872 | tf_op jit(solution)/shard_map/attention/ppermute | solution.py:66
  340.8 101.4 %all-gather.11.cloned.1.call-start = ((), (), s32[]{:S(2)}) async-start(), calls=%async_computation.13 | async-start | bytes 4718592 | tf_op jit(solution)/shard_map/attention_back/all_gather | solution.py:708
  347.6 31.9 %collective-permute-start.20 = (bf16[256,2048]{1,0:T(8,128)(2,1)}, bf16[256,2048]{1,0:T(8,128)(2,1)}, u32[]{:S(2)}, u32[]{:S(2)}) collective-permute-start(bf16[256,2048]{1,0:T(8,128)(2,1)} %get-tuple-element.226), channel_id=1, source_target_pairs={{0,8},{8,0},{16,24},{24,16},{1,9},{9,1},{17,25},{25,17},{2,10},{10... | collective-permute-start | bytes 3145736 | tf_op jit(solution)/shard_map/feed_forward/ppermute | solution.py:66
  348.8 30.8 %collective-permute-start.21 = (bf16[256,2048]{1,0:T(8,128)(2,1)}, bf16[256,2048]{1,0:T(8,128)(2,1)}, u32[]{:S(2)}, u32[]{:S(2)}) collective-permute-start(bf16[256,2048]{1,0:T(8,128)(2,1)} %get-tuple-element.225), channel_id=1, source_target_pairs={{0,16},{8,24},{16,0},{24,8},{1,17},{9,25},{17,1},{25,9},{2,18},{10... | collective-permute-start | bytes 3145736 | tf_op jit(solution)/shard_map/feed_forward/ppermute | solution.py:66
  391.5 228.3 %reduce-scatter.9.cloned.1.call-start = ((), (), s32[]{:S(2)}) async-start(), calls=%async_computation.14 | async-start | bytes 4718592 | tf_op jit(solution)/shard_map/attention_back/reduce_scatter | solution.py:716
  395.1 22.0 %collective-permute-start.23 = (bf16[256,2048]{1,0:T(8,128)(2,1)S(1)}, bf16[256,2048]{1,0:T(8,128)(2,1)S(1)}, u32[]{:S(2)}, u32[]{:S(2)}) collective-permute-start(bf16[256,2048]{1,0:T(8,128)(2,1)S(1)} %add_convert_fusion.3), channel_id=1, source_target_pairs={{0,16},{8,24},{16,0},{24,8},{1,17},{9,25},{17,1},{25,9},{2,18},{10... | collective-permute-start | bytes 3145736 | tf_op jit(solution)/shard_map/attention_back/ppermute | solution.py:66
  395.5 21.7 %collective-permute-start.22 = (bf16[256,2048]{1,0:T(8,128)(2,1)S(1)}, bf16[256,2048]{1,0:T(8,128)(2,1)S(1)}, u32[]{:S(2)}, u32[]{:S(2)}) collective-permute-start(bf16[256,2048]{1,0:T(8,128)(2,1)S(1)} %slice.107), channel_id=1, source_target_pairs={{0,8},{8,0},{16,24},{24,16},{1,9},{9,1},{17,25},{25,17},{2,10},{10... | collective-permute-start | bytes 3145736 | tf_op jit(solution)/shard_map/attention_back/ppermute | solution.py:66
  398.4 41.2 %collective-permute-start.25 = (bf16[256,2048]{1,0:T(8,128)(2,1)S(1)}, bf16[256,2048]{1,0:T(8,128)(2,1)S(1)}, u32[]{:S(2)}, u32[]{:S(2)}) collective-permute-start(bf16[256,2048]{1,0:T(8,128)(2,1)S(1)} %add_convert_fusion.1), channel_id=1, source_target_pairs={{0,8},{8,0},{16,24},{24,16},{1,9},{9,1},{17,25},{25,17},{2,10},{10... | collective-permute-start | bytes 3145736 | tf_op jit(solution)/shard_map/attention_back/ppermute | solution.py:66
  398.7 40.9 %collective-permute-start.24 = (bf16[256,2048]{1,0:T(8,128)(2,1)S(1)}, bf16[256,2048]{1,0:T(8,128)(2,1)S(1)}, u32[]{:S(2)}, u32[]{:S(2)}) collective-permute-start(bf16[256,2048]{1,0:T(8,128)(2,1)S(1)} %slice.110), channel_id=1, source_target_pairs={{0,16},{8,24},{16,0},{24,8},{1,17},{9,25},{17,1},{25,9},{2,18},{10... | collective-permute-start | bytes 3145736 | tf_op jit(solution)/shard_map/attention_back/ppermute | solution.py:66
  443.7 27.3 %collective-permute-start.26 = (bf16[128,2048]{1,0:T(8,128)(2,1)S(1)}, bf16[128,2048]{1,0:T(8,128)(2,1)S(1)}, u32[]{:S(2)}, u32[]{:S(2)}) collective-permute-start(bf16[128,2048]{1,0:T(8,128)(2,1)S(1)} %get-tuple-element.230), channel_id=1, source_target_pairs={{0,8},{8,0},{16,24},{24,16},{1,9},{9,1},{17,25},{25,17},{2,10},{10... | collective-permute-start | bytes 1572872 | tf_op jit(solution)/shard_map/attention_back/ppermute | solution.py:66
  444.9 26.1 %collective-permute-start.27 = (bf16[128,2048]{1,0:T(8,128)(2,1)S(1)}, bf16[128,2048]{1,0:T(8,128)(2,1)S(1)}, u32[]{:S(2)}, u32[]{:S(2)}) collective-permute-start(bf16[128,2048]{1,0:T(8,128)(2,1)S(1)} %get-tuple-element.229), channel_id=1, source_target_pairs={{0,16},{8,24},{16,0},{24,8},{1,17},{9,25},{17,1},{25,9},{2,18},{10... | collective-permute-start | bytes 1572872 | tf_op jit(solution)/shard_map/attention_back/ppermute | solution.py:66
  446.2 24.9 %collective-permute-start.28 = (bf16[128,2048]{1,0:T(8,128)(2,1)S(1)}, bf16[128,2048]{1,0:T(8,128)(2,1)S(1)}, u32[]{:S(2)}, u32[]{:S(2)}) collective-permute-start(bf16[128,2048]{1,0:T(8,128)(2,1)S(1)} %slice.114), channel_id=1, source_target_pairs={{0,8},{8,0},{16,24},{24,16},{1,9},{9,1},{17,25},{25,17},{2,10},{10... | collective-permute-start | bytes 1572872 | tf_op jit(solution)/shard_map/attention_back/ppermute | solution.py:66
  446.6 24.4 %collective-permute-start.29 = (bf16[128,2048]{1,0:T(8,128)(2,1)S(1)}, bf16[128,2048]{1,0:T(8,128)(2,1)S(1)}, u32[]{:S(2)}, u32[]{:S(2)}) collective-permute-start(bf16[128,2048]{1,0:T(8,128)(2,1)S(1)} %slice.115), channel_id=1, source_target_pairs={{0,16},{8,24},{16,0},{24,8},{1,17},{9,25},{17,1},{25,9},{2,18},{10... | collective-permute-start | bytes 1572872 | tf_op jit(solution)/shard_map/attention_back/ppermute | solution.py:66
  472.6 67.3 %all-to-all-start.2 = ((bf16[8,64,2048]{2,1,0:T(8,128)(2,1)}), bf16[8,64,2048]{2,1,0:T(8,128)(2,1)S(1)}, u32[]{:S(2)}, u32[]{:S(2)}) async-start(bf16[8,64,2048]{2,1,0:T(8,128)(2,1)} %bitcast.88), calls=%async_computation.5 | async-start | bytes 4194304 | tf_op jit(solution)/shard_map/attention_back/all_to_all | solution.py:699
  481.9 140.0 %reduce-scatter.11.cloned.1.call-start = ((), (), s32[]{:S(2)}) async-start(), calls=%async_computation.15 | async-start | bytes 4718592 | tf_op jit(solution)/shard_map/attention_back/reduce_scatter | solution.py:746
  481.9 31.5 %collective-permute-start.30 = (bf16[1024,512]{1,0:T(8,128)(2,1)}, bf16[1024,512]{1,0:T(8,128)(2,1)}, u32[]{:S(2)}, u32[]{:S(2)}) collective-permute-start(bf16[1024,512]{1,0:T(8,128)(2,1)} %get-tuple-element.172), channel_id=1, source_target_pairs={{8,0},{24,16},{9,1},{25,17},{10,2},{26,18},{11,3},{27,19},{12,4},{... | collective-permute-start | bytes 3145736 | tf_op jit(solution)/shard_map/attention_back/ppermute | solution.py:66
  483.3 38.4 %collective-permute-start.31 = (bf16[1024,512]{1,0:T(8,128)(2,1)}, bf16[1024,512]{1,0:T(8,128)(2,1)S(1)}, u32[]{:S(2)}, u32[]{:S(2)}) collective-permute-start(bf16[1024,512]{1,0:T(8,128)(2,1)} %get-tuple-element.173), channel_id=1, source_target_pairs={{16,0},{24,8},{17,1},{25,9},{18,2},{26,10},{19,3},{27,11},{20,4},{... | collective-permute-start | bytes 3145736 | tf_op jit(solution)/shard_map/attention_back/ppermute | solution.py:66
  484.9 37.8 %collective-permute-start.32 = (bf16[1024,512]{1,0:T(8,128)(2,1)}, bf16[1024,512]{1,0:T(8,128)(2,1)}, u32[]{:S(2)}, u32[]{:S(2)}) collective-permute-start(bf16[1024,512]{1,0:T(8,128)(2,1)} %get-tuple-element.174), channel_id=1, source_target_pairs={{16,8},{24,0},{17,9},{25,1},{18,10},{26,2},{19,11},{27,3},{20,12},... | collective-permute-start | bytes 3145736 | tf_op jit(solution)/shard_map/attention_back/ppermute | solution.py:66
  560.9 15.1 %collective-permute-start.35 = (bf16[256,768]{1,0:T(8,128)(2,1)S(1)}, bf16[256,768]{1,0:T(8,128)(2,1)S(1)}, u32[]{:S(2)}, u32[]{:S(2)}) collective-permute-start(bf16[256,768]{1,0:T(8,128)(2,1)S(1)} %slice.136), channel_id=1, source_target_pairs={{0,8},{8,0},{16,24},{24,16},{1,9},{9,1},{17,25},{25,17},{2,10},{10... | collective-permute-start | bytes 1179656 | tf_op jit(solution)/shard_map/weight_grads/ppermute | solution.py:66
  561.2 15.6 %collective-permute-start.36 = (bf16[256,768]{1,0:T(8,128)(2,1)S(1)}, bf16[256,768]{1,0:T(8,128)(2,1)S(1)}, u32[]{:S(2)}, u32[]{:S(2)}) collective-permute-start(bf16[256,768]{1,0:T(8,128)(2,1)S(1)} %slice.137), channel_id=1, source_target_pairs={{0,16},{8,24},{16,0},{24,8},{1,17},{9,25},{17,1},{25,9},{2,18},{10... | collective-permute-start | bytes 1179656 | tf_op jit(solution)/shard_map/weight_grads/ppermute | solution.py:66
  577.1 13.3 %collective-permute-start.40 = (bf16[64,2048]{1,0:T(8,128)(2,1)S(1)}, bf16[64,2048]{1,0:T(8,128)(2,1)S(1)}, u32[]{:S(2)}, u32[]{:S(2)}) collective-permute-start(bf16[64,2048]{1,0:T(8,128)(2,1)S(1)} %copy-done.66), channel_id=1, source_target_pairs={{0,16},{8,24},{16,0},{24,8},{1,17},{9,25},{17,1},{25,9},{2,18},{10... | collective-permute-start | bytes 786440 | tf_op jit(solution)/shard_map/weight_grads/ppermute | solution.py:66
  578.3 12.1 %collective-permute-start.39 = (bf16[64,2048]{1,0:T(8,128)(2,1)S(1)}, bf16[64,2048]{1,0:T(8,128)(2,1)S(1)}, u32[]{:S(2)}, u32[]{:S(2)}) collective-permute-start(bf16[64,2048]{1,0:T(8,128)(2,1)S(1)} %convolution_convert_fusion.10), channel_id=1, source_target_pairs={{0,8},{8,0},{16,24},{24,16},{1,9},{9,1},{17,25},{25,17},{2,10},{10... | collective-permute-start | bytes 786440 | tf_op jit(solution)/shard_map/weight_grads/ppermute | solution.py:66
  579.6 19.3 %collective-permute-start.37 = (bf16[256,768]{1,0:T(8,128)(2,1)S(1)}, bf16[256,768]{1,0:T(8,128)(2,1)S(1)}, u32[]{:S(2)}, u32[]{:S(2)}) collective-permute-start(bf16[256,768]{1,0:T(8,128)(2,1)S(1)} %add_convert_fusion.7), channel_id=1, source_target_pairs={{0,16},{8,24},{16,0},{24,8},{1,17},{9,25},{17,1},{25,9},{2,18},{10... | collective-permute-start | bytes 1179656 | tf_op jit(solution)/shard_map/weight_grads/ppermute | solution.py:66
  580.0 18.8 %collective-permute-start.38 = (bf16[256,768]{1,0:T(8,128)(2,1)S(1)}, bf16[256,768]{1,0:T(8,128)(2,1)S(1)}, u32[]{:S(2)}, u32[]{:S(2)}) collective-permute-start(bf16[256,768]{1,0:T(8,128)(2,1)S(1)} %add_convert_fusion.6), channel_id=1, source_target_pairs={{0,8},{8,0},{16,24},{24,16},{1,9},{9,1},{17,25},{25,17},{2,10},{10... | collective-permute-start | bytes 1179656 | tf_op jit(solution)/shard_map/weight_grads/ppermute | solution.py:66
  600.9 13.4 %collective-permute-start.43 = (bf16[128,2048]{1,0:T(8,128)(2,1)}, bf16[128,2048]{1,0:T(8,128)(2,1)S(1)}, u32[]{:S(2)}, u32[]{:S(2)}) collective-permute-start(bf16[128,2048]{1,0:T(8,128)(2,1)} %add_convert_fusion.5), channel_id=1, source_target_pairs={{0,16},{8,24},{16,0},{24,8},{1,17},{9,25},{17,1},{25,9},{2,18},{10... | collective-permute-start | bytes 1572872 | tf_op jit(solution)/shard_map/weight_grads/ppermute | solution.py:66
  603.4 12.9 %collective-permute-start.44 = (bf16[128,2048]{1,0:T(8,128)(2,1)}, bf16[128,2048]{1,0:T(8,128)(2,1)S(1)}, u32[]{:S(2)}, u32[]{:S(2)}) collective-permute-start(bf16[128,2048]{1,0:T(8,128)(2,1)} %add_convert_fusion.4), channel_id=1, source_target_pairs={{0,8},{8,0},{16,24},{24,16},{1,9},{9,1},{17,25},{25,17},{2,10},{10... | collective-permute-start | bytes 1572872 | tf_op jit(solution)/shard_map/weight_grads/ppermute | solution.py:66
  603.7 34.2 %all-to-all-start.3 = ((bf16[8,64,768]{2,1,0:T(8,128)(2,1)}), bf16[8,64,768]{2,1,0:T(8,128)(2,1)S(1)}, u32[]{:S(2)}, u32[]{:S(2)}) async-start(bf16[8,64,768]{2,1,0:T(8,128)(2,1)} %bitcast.32), calls=%async_computation.6 | async-start | bytes 1572864 | tf_op jit(solution)/shard_map/weight_grads/all_to_all | solution.py:699
  608.2 29.7 %collective-permute-start.42 = (bf16[64,2048]{1,0:T(8,128)(2,1)}, bf16[64,2048]{1,0:T(8,128)(2,1)}, u32[]{:S(2)}, u32[]{:S(2)}) collective-permute-start(bf16[64,2048]{1,0:T(8,128)(2,1)} %convert_add_fusion.4), channel_id=1, source_target_pairs={{0,0},{1,4},{2,8},{3,12},{4,16},{5,20},{6,24},{7,28},{8,1},{9,5},{... | collective-permute-start | bytes 786440 | tf_op jit(solution)/shard_map/weight_grads/ppermute | solution.py:765
  (80 other events, 1005.7 us)
Sparse Core Ops, SparseCore 0:
  36.9 47.1 all-gather.4
  86.4 59.1 all-gather.6
  212.9 45.9 reduce-scatter.4
  262.0 48.1 all-gather.8
  340.9 46.9 reduce-scatter.6
  391.6 48.0 all-gather.10
  442.3 67.4 reduce-scatter.8
  554.3 46.2 reduce-scatter.10

commit v5 on v4

--- a/solution.py
+++ b/solution.py
@@ -625,7 +625,8 @@
         )
 
     with jax.named_scope("hidden_weights"):
-        both = collect([gate_weight, up_weight], parts, blocks, chunk)
+        gate = collect([gate_weight], parts, blocks, chunk)
+        up = collect([up_weight], parts, blocks, chunk)
         output_rows = lax.ppermute(
             after(output_weight, stacked),
             ("blk", "head"),
@@ -648,17 +649,22 @@
         upstream_group = lax.all_gather(
             after(upstream_low, normed_group), "head", axis=0, tiled=True
         )
-        both = lax.all_to_all(
-            after(both, upstream_group, *sent), "head", split_axis=0, concat_axis=0, tiled=True
-        ).reshape(band_rows, 2 * blocks * chunk)
+        gate = lax.all_to_all(
+            after(gate, query), "head", split_axis=0, concat_axis=0, tiled=True
+        )
+        sent, gate = lax.optimization_barrier((sent, gate))
+        up = lax.all_to_all(
+            after(up, upstream_group, *sent), "head", split_axis=0, concat_axis=0, tiled=True
+        )
         attended, log_total = forward_attention(
             place, query, [key_value] + sent, masks, None, True, heads, block_rows
         )
         down_near = send_near(after(down_weight, sent[0]))
         joined_partial = dot(after(attended, down_near), output).astype(BF16)
-        joined_partial, down_near, both = lax.optimization_barrier(
-            (joined_partial, down_near, both)
-        )
+        joined_partial, down_near, up = lax.optimization_barrier(
+            (joined_partial, down_near, up)
+        )
+        both = jnp.concatenate([gate, up], axis=2).reshape(band_rows, 2 * blocks * chunk)
         near = send_near(both)
         joined = lax.psum_scatter(joined_partial, "head", scatter_dimension=0, tiled=True)
         joined, near = lax.optimization_barrier((joined, near))
@@ -740,8 +746,15 @@
         down_act = after(down_act, query_grad)
         layer_output = ((residual + down_act) * valid).astype(BF16)[None]
         projection_back, normed_one_partial = project_back(
-            place, query_grad, projection, cosine, sine, key_value_grads, masks,
-            heads, block_rows,
+            place,
+            pltpu.with_memory_space_constraint(query_grad, pltpu.HBM),
+            projection,
+            cosine,
+            sine,
+            [pltpu.with_memory_space_constraint(part, pltpu.HBM) for part in key_value_grads],
+            masks,
+            heads,
+            block_rows,
         )
         normed_one_grad = lax.psum_scatter(
             normed_one_partial, "head", scatter_dimension=0, tiled=True

time: 655 us -> 655 us (level)
  waiting for transfers between devices: 304 us -> 281 us
  local copies, waits for them, and re-layouts: 68.9 us -> 87.3 us
  starting transfers between devices: 89.5 us -> 96.6 us
    all_to_all x1 -> x2, waiting for transfers between devices: 16.7 us -> 0.01 us  [the longest x1 0.01 us: local(): lax.all_to_all(after(gate, query), 'head', split_axis=0, concat_axis=0, t...]
    unnamed x142 -> x135, local copies, waits for them, and re-layouts: 27 us -> 39.3 us
    all_to_all x1 -> x2, starting transfers between devices: 12.1 us -> 14.6 us  [the longest x1 10.2 us: local(): lax.all_to_all(after(gate, query), 'head', split_axis=0, concat_axis=0, t...]
  transfers between devices with their start and end apart: 57 -> 58, of which waited for: 31 -> 32; matrix products, arithmetic and copies ran while one was open for 19% -> 20% of each run, Pallas kernels for 8% -> 8%
where the time goes in v5:
time: 655 us; the launch traced here: 647 us
  waiting for transfers between devices  281 us (43%)
  starting transfers between devices  96.6 us (15%)
  local copies, waits for them, and re-layouts  87.3 us (13%)
  Pallas kernels  85 us (13%)
  matrix products  56.6 us (9%)
  other arithmetic  25 us (4%)
  between operations  16.1 us (2%)
    ppermute x43, waiting for transfers between devices, swapped(): return lax.ppermute(value, 'blk', pairs)  219 us
    ppermute x43, starting transfers between devices, swapped(): return lax.ppermute(value, 'blk', pairs)  52.5 us
    dot_general x16, matrix products, outer_sum(): lax.dot_general(left, right, (((0,), (0,)), ((), ())), preferred_element_...  41.1 us
    unnamed x135, local copies, waits for them, and re-layouts  39.3 us
    pallas_call x1, Pallas kernels, feed_forward(): pl.pallas_call(functools.partial(feed_kernel, columns=min(256, hidden)),...  29.2 us
    dynamic_update_slice x16, local copies, waits for them, and re-layouts, gather_blk(): whole = lax.dynamic_update_slice(whole, piece[None], start)  20.2 us
    pallas_call x1, Pallas kernels, backward_attention(): pl.pallas_call(functools.partial(backward_kernel, masks=masks, started=st...  19.3 us
    all_to_all x2, waiting for transfers between devices, to_shards(): lax.all_to_all(summed.astype(BF16).reshape(parts, shard_rows, summed.shap...  17.6 us
  transfers between devices with their start and end apart: 58, of which 32 were waited for; matrix products, arithmetic and copies ran while one was open for 20% of the time, Pallas kernels for 8%

profile of v5, /device:TPU:5, one launch (start us, length us, event | category | flops | bytes accessed | tf_op | source)
XLA Modules:
  0.0 647.2 jit_solution(16540161908318117459)
XLA Ops:
  11.0 5.5 all-to-all-start
  20.2 16.6 %all-to-all-done = bf16[8,64,768]{2,1,0:T(8,128)(2,1)} async-done(((bf16[8,64,768]{2,1,0:T(8,128)(2,1)}), bf16[8,64,768]{2,1,0:T(8,128)(2,1)}, u32[]{:S(2)}, u32[]{:S(2)}) %all-to-all-start) | async-done | bytes 786464 | tf_op jit(solution)/shard_map/projection_weights/all_to_all | solution.py:614
  40.0 3.4 collective-permute-start.4
  44.9 10.5 %collective-permute-done = bf16[512,768]{1,0:T(8,128)(2,1)} collective-permute-done((bf16[512,768]{1,0:T(8,128)(2,1)}, bf16[512,768]{1,0:T(8,128)(2,1)}, u32[]{:S(2)}, u32[]{:S(2)}) %collective-permute-start) | collective-permute-done | bytes 786464 | tf_op jit(solution)/shard_map/projection_weights/ppermute | solution.py:66
  56.5 4.6 collective-permute-start.2
  71.6 3.3 collective-permute-start.6
  77.5 3.4 collective-permute-start.7
  90.0 6.1 project.1
  97.8 10.2 %all-to-all-start.1 = ((bf16[8,64,1024]{2,1,0:T(8,128)(2,1)}), bf16[8,64,1024]{2,1,0:T(8,128)(2,1)}, u32[]{:S(2)}, u32[]{:S(2)}) async-start(bf16[8,64,1024]{2,1,0:T(8,128)(2,1)} %copy-done.24), calls=%async_computation.1 | async-start | bytes 2097152 | tf_op jit(solution)/shard_map/attention/all_to_all | solution.py:652
  108.1 6.8 %collective-permute-start.9 = (bf16[1024,512]{1,0:T(8,128)(2,1)}, bf16[1024,512]{1,0:T(8,128)(2,1)S(1)}, u32[]{:S(2)}, u32[]{:S(2)}) collective-permute-start(bf16[1024,512]{1,0:T(8,128)(2,1)} %copy-done.14), channel_id=1, source_target_pairs={{0,8},{16,24},{1,9},{17,25},{2,10},{18,26},{3,11},{19,27},{4,12},{... | collective-permute-start | bytes 3145736 | tf_op jit(solution)/shard_map/attention/ppermute | solution.py:66
  119.9 17.9 %collective-permute-done.9.refs_1_.refs_2_ = bf16[1024,512]{1,0:T(8,128)(2,1)S(1)} collective-permute-done((bf16[1024,512]{1,0:T(8,128)(2,1)}, bf16[1024,512]{1,0:T(8,128)(2,1)S(1)}, u32[]{:S(2)}, u32[]{:S(2)}) %collective-permute-start.9) | collective-permute-done | bytes 1048608 | tf_op jit(solution)/shard_map/attention/ppermute | solution.py:66
  138.8 25.3 %collective-permute-done.10.refs_2_.refs_1_ = bf16[1024,512]{1,0:T(8,128)(2,1)S(1)} collective-permute-done((bf16[1024,512]{1,0:T(8,128)(2,1)}, bf16[1024,512]{1,0:T(8,128)(2,1)S(1)}, u32[]{:S(2)}, u32[]{:S(2)}) %collective-permute-start.10) | collective-permute-done | bytes 1048608 | tf_op jit(solution)/shard_map/attention/ppermute | solution.py:66
  167.9 4.4 all-to-all-start.2
  179.8 13.4 %attention_forward.1 = (bf16[1024,256]{1,0:T(8,128)(2,1)S(1)}, f32[2,1,1024]{2,1,0:T(1,128)S(1)}) custom-call(s32[2]{0:T(128)S(1)} %pad_add_fusion.place_ref, bf16[1024,256]{1,0:T(8,128)(2,1)S(1)} %copy-done.27, bf16[1024,512]{1,0:T(8,128)(2,1)S(1)} %copy-done.15, bf16[1024,512]{1,0:T(8,128)(2,1)S(1)} %copy-done.17, bf16[1024,512]{1,0:T(8,128)(2,1)S(1)} %copy-done.19, ...), custom_call_target="tpu_custom_call" | custom-call | tf_op jit(solution)/shard_map/attention/attention_forward/pallas_call | solution.py:418
  193.2 3.9 collective-permute-done.12
  198.0 4.5 convolution_convert_fusion
  207.6 44.3 %collective-permute-done.14 = bf16[512,2048]{1,0:T(8,128)(2,1)} collective-permute-done((bf16[512,2048]{1,0:T(8,128)(2,1)S(1)}, bf16[512,2048]{1,0:T(8,128)(2,1)}, u32[]{:S(2)}, u32[]{:S(2)}) %collective-permute-start.14) | collective-permute-done | bytes 2097184 | tf_op jit(solution)/shard_map/attention/ppermute | solution.py:66
  264.5 4.6 broadcast_in_dim.119
  270.5 11.0 %collective-permute-done.16 = bf16[256,2048]{1,0:T(8,128)(2,1)S(1)} collective-permute-done((bf16[256,2048]{1,0:T(8,128)(2,1)S(1)}, bf16[256,2048]{1,0:T(8,128)(2,1)S(1)}, u32[]{:S(2)}, u32[]{:S(2)}) %collective-permute-start.16) | collective-permute-done | bytes 1048608 | tf_op jit(solution)/shard_map/attention/ppermute | solution.py:66
  286.4 3.2 bitcast_dynamic-update-slice_fusion.1
  289.7 3.2 bitcast_dynamic-update-slice_fusion
  302.6 4.4 all-gather.9.cloned.1.call-done.normed_ref
  307.0 29.2 %feed_forward.1 = (bf16[1024,1024]{1,0:T(8,128)(2,1)S(1)}, bf16[1024,2048]{1,0:T(8,128)(2,1)}, bf16[1024,2048]{1,0:T(8,128)(2,1)}) custom-call(bf16[1024,2048]{1,0:T(8,128)(2,1)} %all-gather.9.cloned.1.call-done.normed_ref, bf16[1024,2048]{1,0:T(8,128)(2,1)} %all-gather.7.cloned.1.call-done.grad_ref, bf16[2048,2048]{1,0:T(8,128)(2,1)} %bitcast.23.both_ref, ...), custom_call_target="tpu_custom_call" | custom-call | tf_op jit(solution)/shard_map/feed_forward/feed_forward/pallas_call | solution.py:559
  337.8 5.0 convolution_convert_fusion.2
  345.8 2.7 fusion.19
  353.1 4.5 fusion.13
  357.6 3.8 convolution_convert_fusion.4
  361.5 3.8 convolution_convert_fusion.3
  365.2 2.7 convolution_convert_fusion.5
  367.9 8.3 %convolution_convert_fusion.1 = bf16[1024,2048]{1,0:T(8,128)(2,1)} fusion(bf16[1024,1024]{1,0:T(8,128)(2,1)S(1)} %copy-done.44, bf16[1024,2048]{1,0:T(8,128)(2,1)} %bitcast.29.down_ref), kind=kOutput, calls=%fused_computation.1 | convolution fusion | flops 4297064448 | bytes 10485760 | tf_op jit(solution)/shard_map/feed_forward/dot_general | solution.py:52
  376.2 9.3 %reduce-scatter.7.cloned.1.call-done.grad_ref = bf16[128,2048]{1,0:T(8,128)(2,1)} async-done(((bf16[1024,2048]{1,0:T(8,128)(2,1)}), bf16[128,2048]{1,0:T(8,128)(2,1)}) %reduce-scatter.7.cloned.1.call-update) | async-done | bytes 524304 | tf_op jit(solution)/shard_map/feed_forward/reduce_scatter | solution.py:683
  399.9 17.1 %collective-permute-done.23 = bf16[256,2048]{1,0:T(8,128)(2,1)S(1)} collective-permute-done((bf16[256,2048]{1,0:T(8,128)(2,1)S(1)}, bf16[256,2048]{1,0:T(8,128)(2,1)S(1)}, u32[]{:S(2)}, u32[]{:S(2)}) %collective-permute-start.23) | collective-permute-done | bytes 1048608 | tf_op jit(solution)/shard_map/attention_back/ppermute | solution.py:66
  417.2 22.4 %collective-permute-done.25 = bf16[256,2048]{1,0:T(8,128)(2,1)S(1)} collective-permute-done((bf16[256,2048]{1,0:T(8,128)(2,1)S(1)}, bf16[256,2048]{1,0:T(8,128)(2,1)S(1)}, u32[]{:S(2)}, u32[]{:S(2)}) %collective-permute-start.25) | collective-permute-done | bytes 1048608 | tf_op jit(solution)/shard_map/attention_back/ppermute | solution.py:66
  449.1 2.7 convolution_convert_fusion.14.do_ref
  451.8 19.3 %attention_backward.1 = (f32[1024,256]{1,0:T(8,128)S(1)}, bf16[1024,512]{1,0:T(8,128)(2,1)}, bf16[1024,512]{1,0:T(8,128)(2,1)}, bf16[1024,512]{1,0:T(8,128)(2,1)}, bf16[1024,512]{1,0:T(8,128)(2,1)S(1)}) custom-call(s32[2]{0:T(128)S(1)} %pad_add_fusion.place_ref, bf16[1024,256]{1,0:T(8,128)(2,1)S(1)} %copy-done.28, bf16[1024,256]{1,0:T(8,128)(2,1)S(1)} %copy-done.4, ...), custom_call_target="tpu_custom_call" | custom-call | tf_op jit(solution)/shard_map/attention_back/attention_backward/pallas_call | solution.py:503
  473.1 9.5 %all-to-all-start.3 = ((bf16[8,64,2048]{2,1,0:T(8,128)(2,1)}), bf16[8,64,2048]{2,1,0:T(8,128)(2,1)}, u32[]{:S(2)}, u32[]{:S(2)}) async-start(bf16[8,64,2048]{2,1,0:T(8,128)(2,1)} %bitcast.89), calls=%async_computation.6 | async-start | bytes 4194304 | tf_op jit(solution)/shard_map/attention_back/all_to_all | solution.py:705
  488.9 25.3 %collective-permute-done.30.refs_1_ = bf16[1024,512]{1,0:T(8,128)(2,1)} collective-permute-done((bf16[1024,512]{1,0:T(8,128)(2,1)}, bf16[1024,512]{1,0:T(8,128)(2,1)}, u32[]{:S(2)}, u32[]{:S(2)}) %collective-permute-start.30) | collective-permute-done | bytes 1048608 | tf_op jit(solution)/shard_map/attention_back/ppermute | solution.py:66
  514.2 3.2 convolution_convert_fusion.10
  522.5 17.6 %all-to-all-done.3.in_ref = bf16[8,64,2048]{2,1,0:T(8,128)(2,1)} async-done(((bf16[8,64,2048]{2,1,0:T(8,128)(2,1)}), bf16[8,64,2048]{2,1,0:T(8,128)(2,1)}, u32[]{:S(2)}, u32[]{:S(2)}) %all-to-all-start.3) | async-done | bytes 2097184 | tf_op jit(solution)/shard_map/attention_back/all_to_all | solution.py:705
  542.2 7.9 %project_back.1 = (bf16[1024,768]{1,0:T(8,128)(2,1)S(1)}, bf16[1024,2048]{1,0:T(8,128)(2,1)}) custom-call(s32[2]{0:T(128)S(1)} %pad_add_fusion.place_ref, f32[1024,256]{1,0:T(8,128)} %copy-done.29, bf16[2048,768]{1,0:T(8,128)(2,1)S(1)} %bitcast.86, f32[1024,128]{1,0:T(8,128)S(1)} %copy-done.7, f32[1024,128]{1,0:T(8,128)S(1)} %copy-done.9, ...), custom_call_target="tpu_custom_call" | custom-call | tf_op jit(solution)/shard_map/attention_back/project_back/pallas_call | solution.py:266
  560.6 3.8 spread.2
  566.4 7.6 %collective-permute-done.35 = bf16[256,768]{1,0:T(8,128)(2,1)S(1)} collective-permute-done((bf16[256,768]{1,0:T(8,128)(2,1)S(1)}, bf16[256,768]{1,0:T(8,128)(2,1)S(1)}, u32[]{:S(2)}, u32[]{:S(2)}) %collective-permute-start.35) | collective-permute-done | bytes 393248 | tf_op jit(solution)/shard_map/weight_grads/ppermute | solution.py:66
  578.5 3.7 collective-permute-done.41
  582.2 6.3 collective-permute-done.40
  588.6 8.3 %collective-permute-done.37 = bf16[256,768]{1,0:T(8,128)(2,1)S(1)} collective-permute-done((bf16[256,768]{1,0:T(8,128)(2,1)S(1)}, bf16[256,768]{1,0:T(8,128)(2,1)S(1)}, u32[]{:S(2)}, u32[]{:S(2)}) %collective-permute-start.37) | collective-permute-done | bytes 393248 | tf_op jit(solution)/shard_map/weight_grads/ppermute | solution.py:66
  603.9 4.4 all-to-all-start.4
  608.4 6.2 collective-permute-start.42
  626.0 12.0 %collective-permute-done.42 = bf16[64,2048]{1,0:T(8,128)(2,1)S(1)} collective-permute-done((bf16[64,2048]{1,0:T(8,128)(2,1)S(1)}, bf16[64,2048]{1,0:T(8,128)(2,1)S(1)}, u32[]{:S(2)}, u32[]{:S(2)}) %collective-permute-start.42) | collective-permute-done | bytes 262176 | tf_op jit(solution)/shard_map/weight_grads/ppermute | solution.py:778
  (313 shorter events, 173.8 us)
Async XLA Ops:
  11.0 25.8 %all-to-all-start = ((bf16[8,64,768]{2,1,0:T(8,128)(2,1)}), bf16[8,64,768]{2,1,0:T(8,128)(2,1)}, u32[]{:S(2)}, u32[]{:S(2)}) async-start(bf16[8,64,768]{2,1,0:T(8,128)(2,1)} %collect.3), calls=%async_computation | async-start | bytes 1572864 | tf_op jit(solution)/shard_map/projection_weights/all_to_all | solution.py:614
  16.6 69.7 %all-gather.5.cloned.1.call-start = ((), (), s32[]{:S(2)}) async-start(), calls=%async_computation.9 | async-start | bytes 4718592 | tf_op jit(solution)/shard_map/tokens_gather/all_gather | solution.py:623
  36.8 131.1 %all-gather.7.cloned.1.call-start = ((), (), s32[]{:S(2)}) async-start(), calls=%async_computation.10 | async-start | bytes 4718592 | tf_op jit(solution)/shard_map/attention/all_gather | solution.py:649
  36.9 18.6 %collective-permute-start = (bf16[512,768]{1,0:T(8,128)(2,1)}, bf16[512,768]{1,0:T(8,128)(2,1)}, u32[]{:S(2)}, u32[]{:S(2)}) collective-permute-start(bf16[512,768]{1,0:T(8,128)(2,1)} %bitcast.2), channel_id=1, source_target_pairs={{0,8},{8,0},{16,24},{24,16},{1,9},{9,1},{17,25},{25,17},{2,10},{10... | collective-permute-start | bytes 2359304 | tf_op jit(solution)/shard_map/projection_weights/ppermute | solution.py:66
  38.2 22.9 %collective-permute-start.1 = (bf16[512,768]{1,0:T(8,128)(2,1)}, bf16[512,768]{1,0:T(8,128)(2,1)}, u32[]{:S(2)}, u32[]{:S(2)}) collective-permute-start(bf16[512,768]{1,0:T(8,128)(2,1)} %bitcast.2), channel_id=1, source_target_pairs={{0,16},{8,24},{16,0},{24,8},{1,17},{9,25},{17,1},{25,9},{2,18},{10... | collective-permute-start | bytes 2359304 | tf_op jit(solution)/shard_map/projection_weights/ppermute | solution.py:66
  40.0 27.0 %collective-permute-start.4 = (bf16[64,2048]{1,0:T(8,128)(2,1)S(1)}, bf16[64,2048]{1,0:T(8,128)(2,1)S(1)}, u32[]{:S(2)}, u32[]{:S(2)}) collective-permute-start(bf16[64,2048]{1,0:T(8,128)(2,1)S(1)} %copy-done.66), channel_id=1, source_target_pairs={{0,0},{4,1},{8,2},{12,3},{16,4},{20,5},{24,6},{28,7},{1,8},{5,9},{... | collective-permute-start | bytes 786440 | tf_op jit(solution)/shard_map/hidden_weights/ppermute | solution.py:630
  56.5 11.2 %collective-permute-start.2 = (bf16[256,768]{1,0:T(8,128)(2,1)S(1)}, bf16[256,768]{1,0:T(8,128)(2,1)S(1)}, u32[]{:S(2)}, u32[]{:S(2)}) collective-permute-start(bf16[256,768]{1,0:T(8,128)(2,1)S(1)} %slice.128), channel_id=1, source_target_pairs={{0,16},{8,24},{16,0},{24,8},{1,17},{9,25},{17,1},{25,9},{2,18},{10... | collective-permute-start | bytes 1179656 | tf_op jit(solution)/shard_map/projection_weights/ppermute | solution.py:66
  97.8 68.2 %all-to-all-start.1 = ((bf16[8,64,1024]{2,1,0:T(8,128)(2,1)}), bf16[8,64,1024]{2,1,0:T(8,128)(2,1)}, u32[]{:S(2)}, u32[]{:S(2)}) async-start(bf16[8,64,1024]{2,1,0:T(8,128)(2,1)} %copy-done.24), calls=%async_computation.1 | async-start | bytes 2097152 | tf_op jit(solution)/shard_map/attention/all_to_all | solution.py:652
  108.1 29.7 %collective-permute-start.9 = (bf16[1024,512]{1,0:T(8,128)(2,1)}, bf16[1024,512]{1,0:T(8,128)(2,1)S(1)}, u32[]{:S(2)}, u32[]{:S(2)}) collective-permute-start(bf16[1024,512]{1,0:T(8,128)(2,1)} %copy-done.14), channel_id=1, source_target_pairs={{0,8},{16,24},{1,9},{17,25},{2,10},{18,26},{3,11},{19,27},{4,12},{... | collective-permute-start | bytes 3145736 | tf_op jit(solution)/shard_map/attention/ppermute | solution.py:66
  114.9 49.2 %collective-permute-start.10 = (bf16[1024,512]{1,0:T(8,128)(2,1)}, bf16[1024,512]{1,0:T(8,128)(2,1)S(1)}, u32[]{:S(2)}, u32[]{:S(2)}) collective-permute-start(bf16[1024,512]{1,0:T(8,128)(2,1)} %copy-done.14), channel_id=1, source_target_pairs={{0,16},{8,24},{1,17},{9,25},{2,18},{10,26},{3,19},{11,27},{4,20},{... | collective-permute-start | bytes 3145736 | tf_op jit(solution)/shard_map/attention/ppermute | solution.py:66
  116.2 48.8 %collective-permute-start.11 = (bf16[1024,512]{1,0:T(8,128)(2,1)}, bf16[1024,512]{1,0:T(8,128)(2,1)S(1)}, u32[]{:S(2)}, u32[]{:S(2)}) collective-permute-start(bf16[1024,512]{1,0:T(8,128)(2,1)} %copy-done.14), channel_id=1, source_target_pairs={{0,24},{8,16},{1,25},{9,17},{2,26},{10,18},{3,27},{11,19},{4,28},{... | collective-permute-start | bytes 3145736 | tf_op jit(solution)/shard_map/attention/ppermute | solution.py:66
  167.9 35.4 %all-to-all-start.2 = ((bf16[8,64,1024]{2,1,0:T(8,128)(2,1)}), bf16[8,64,1024]{2,1,0:T(8,128)(2,1)}, u32[]{:S(2)}, u32[]{:S(2)}) async-start(bf16[8,64,1024]{2,1,0:T(8,128)(2,1)} %copy-done.25), calls=%async_computation.2 | async-start | bytes 2097152 | tf_op jit(solution)/shard_map/attention/all_to_all | solution.py:656
  172.3 80.8 %reduce-scatter.5.cloned.1.call-start = ((), (), s32[]{:S(2)}) async-start(), calls=%async_computation.11 | async-start | bytes 4718592 | tf_op jit(solution)/shard_map/attention/reduce_scatter | solution.py:669
  172.3 24.8 %collective-permute-start.12 = (bf16[256,2048]{1,0:T(8,128)(2,1)}, bf16[256,2048]{1,0:T(8,128)(2,1)}, u32[]{:S(2)}, u32[]{:S(2)}) collective-permute-start(bf16[256,2048]{1,0:T(8,128)(2,1)} %param.18), channel_id=1, source_target_pairs={{0,8},{8,0},{16,24},{24,16},{1,9},{9,1},{17,25},{25,17},{2,10},{10... | collective-permute-start | bytes 3145736 | tf_op jit(solution)/shard_map/attention/ppermute | solution.py:66
  173.5 24.5 %collective-permute-start.13 = (bf16[256,2048]{1,0:T(8,128)(2,1)}, bf16[256,2048]{1,0:T(8,128)(2,1)}, u32[]{:S(2)}, u32[]{:S(2)}) collective-permute-start(bf16[256,2048]{1,0:T(8,128)(2,1)} %param.18), channel_id=1, source_target_pairs={{0,16},{8,24},{16,0},{24,8},{1,17},{9,25},{17,1},{25,9},{2,18},{10... | collective-permute-start | bytes 3145736 | tf_op jit(solution)/shard_map/attention/ppermute | solution.py:66
  203.3 103.7 %all-gather.9.cloned.1.call-start = ((), (), s32[]{:S(2)}) async-start(), calls=%async_computation.12 | async-start | bytes 4718592 | tf_op jit(solution)/shard_map/feed_forward/all_gather | solution.py:679
  206.0 45.9 %collective-permute-start.14 = (bf16[512,2048]{1,0:T(8,128)(2,1)S(1)}, bf16[512,2048]{1,0:T(8,128)(2,1)}, u32[]{:S(2)}, u32[]{:S(2)}) collective-permute-start(bf16[512,2048]{1,0:T(8,128)(2,1)S(1)} %bitcast.90), channel_id=1, source_target_pairs={{0,8},{8,0},{16,24},{24,16},{1,9},{9,1},{17,25},{25,17},{2,10},{10... | collective-permute-start | bytes 6291464 | tf_op jit(solution)/shard_map/attention/ppermute | solution.py:66
  207.3 45.9 %collective-permute-start.15 = (bf16[512,2048]{1,0:T(8,128)(2,1)S(1)}, bf16[512,2048]{1,0:T(8,128)(2,1)}, u32[]{:S(2)}, u32[]{:S(2)}) collective-permute-start(bf16[512,2048]{1,0:T(8,128)(2,1)S(1)} %bitcast.91), channel_id=1, source_target_pairs={{0,16},{8,24},{16,0},{24,8},{1,17},{9,25},{17,1},{25,9},{2,18},{10... | collective-permute-start | bytes 6291464 | tf_op jit(solution)/shard_map/attention/ppermute | solution.py:66
  257.6 127.9 %reduce-scatter.7.cloned.1.call-start = ((), (), s32[]{:S(2)}) async-start(), calls=%async_computation.13 | async-start | bytes 4718592 | tf_op jit(solution)/shard_map/feed_forward/reduce_scatter | solution.py:683
  259.0 22.5 %collective-permute-start.16 = (bf16[256,2048]{1,0:T(8,128)(2,1)S(1)}, bf16[256,2048]{1,0:T(8,128)(2,1)S(1)}, u32[]{:S(2)}, u32[]{:S(2)}) collective-permute-start(bf16[256,2048]{1,0:T(8,128)(2,1)S(1)} %slice.100), channel_id=1, source_target_pairs={{0,16},{8,24},{16,0},{24,8},{1,17},{9,25},{17,1},{25,9},{2,18},{10... | collective-permute-start | bytes 3145736 | tf_op jit(solution)/shard_map/attention/ppermute | solution.py:66
  260.7 22.2 %collective-permute-start.17 = (bf16[256,2048]{1,0:T(8,128)(2,1)S(1)}, bf16[256,2048]{1,0:T(8,128)(2,1)S(1)}, u32[]{:S(2)}, u32[]{:S(2)}) collective-permute-start(bf16[256,2048]{1,0:T(8,128)(2,1)S(1)} %slice.101), channel_id=1, source_target_pairs={{0,8},{8,0},{16,24},{24,16},{1,9},{9,1},{17,25},{25,17},{2,10},{10... | collective-permute-start | bytes 3145736 | tf_op jit(solution)/shard_map/attention/ppermute | solution.py:66
  337.5 104.7 %all-gather.11.cloned.1.call-start = ((), (), s32[]{:S(2)}) async-start(), calls=%async_computation.14 | async-start | bytes 4718592 | tf_op jit(solution)/shard_map/attention_back/all_gather | solution.py:714
  344.3 31.9 %collective-permute-start.20 = (bf16[256,2048]{1,0:T(8,128)(2,1)}, bf16[256,2048]{1,0:T(8,128)(2,1)}, u32[]{:S(2)}, u32[]{:S(2)}) collective-permute-start(bf16[256,2048]{1,0:T(8,128)(2,1)} %get-tuple-element.236), channel_id=1, source_target_pairs={{0,8},{8,0},{16,24},{24,16},{1,9},{9,1},{17,25},{25,17},{2,10},{10... | collective-permute-start | bytes 3145736 | tf_op jit(solution)/shard_map/feed_forward/ppermute | solution.py:66
  345.5 30.7 %collective-permute-start.21 = (bf16[256,2048]{1,0:T(8,128)(2,1)}, bf16[256,2048]{1,0:T(8,128)(2,1)}, u32[]{:S(2)}, u32[]{:S(2)}) collective-permute-start(bf16[256,2048]{1,0:T(8,128)(2,1)} %get-tuple-element.235), channel_id=1, source_target_pairs={{0,16},{8,24},{16,0},{24,8},{1,17},{9,25},{17,1},{25,9},{2,18},{10... | collective-permute-start | bytes 3145736 | tf_op jit(solution)/shard_map/feed_forward/ppermute | solution.py:66
  391.4 228.7 %reduce-scatter.9.cloned.1.call-start = ((), (), s32[]{:S(2)}) async-start(), calls=%async_computation.15 | async-start | bytes 4718592 | tf_op jit(solution)/shard_map/attention_back/reduce_scatter | solution.py:722
  395.1 22.0 %collective-permute-start.23 = (bf16[256,2048]{1,0:T(8,128)(2,1)S(1)}, bf16[256,2048]{1,0:T(8,128)(2,1)S(1)}, u32[]{:S(2)}, u32[]{:S(2)}) collective-permute-start(bf16[256,2048]{1,0:T(8,128)(2,1)S(1)} %add_convert_fusion.3), channel_id=1, source_target_pairs={{0,16},{8,24},{16,0},{24,8},{1,17},{9,25},{17,1},{25,9},{2,18},{10... | collective-permute-start | bytes 3145736 | tf_op jit(solution)/shard_map/attention_back/ppermute | solution.py:66
  395.5 21.7 %collective-permute-start.22 = (bf16[256,2048]{1,0:T(8,128)(2,1)S(1)}, bf16[256,2048]{1,0:T(8,128)(2,1)S(1)}, u32[]{:S(2)}, u32[]{:S(2)}) collective-permute-start(bf16[256,2048]{1,0:T(8,128)(2,1)S(1)} %slice.107), channel_id=1, source_target_pairs={{0,8},{8,0},{16,24},{24,16},{1,9},{9,1},{17,25},{25,17},{2,10},{10... | collective-permute-start | bytes 3145736 | tf_op jit(solution)/shard_map/attention_back/ppermute | solution.py:66
  398.4 41.2 %collective-permute-start.25 = (bf16[256,2048]{1,0:T(8,128)(2,1)S(1)}, bf16[256,2048]{1,0:T(8,128)(2,1)S(1)}, u32[]{:S(2)}, u32[]{:S(2)}) collective-permute-start(bf16[256,2048]{1,0:T(8,128)(2,1)S(1)} %add_convert_fusion.1), channel_id=1, source_target_pairs={{0,8},{8,0},{16,24},{24,16},{1,9},{9,1},{17,25},{25,17},{2,10},{10... | collective-permute-start | bytes 3145736 | tf_op jit(solution)/shard_map/attention_back/ppermute | solution.py:66
  398.7 40.9 %collective-permute-start.24 = (bf16[256,2048]{1,0:T(8,128)(2,1)S(1)}, bf16[256,2048]{1,0:T(8,128)(2,1)S(1)}, u32[]{:S(2)}, u32[]{:S(2)}) collective-permute-start(bf16[256,2048]{1,0:T(8,128)(2,1)S(1)} %slice.110), channel_id=1, source_target_pairs={{0,16},{8,24},{16,0},{24,8},{1,17},{9,25},{17,1},{25,9},{2,18},{10... | collective-permute-start | bytes 3145736 | tf_op jit(solution)/shard_map/attention_back/ppermute | solution.py:66
  443.7 29.4 %collective-permute-start.26 = (bf16[128,2048]{1,0:T(8,128)(2,1)S(1)}, bf16[128,2048]{1,0:T(8,128)(2,1)}, u32[]{:S(2)}, u32[]{:S(2)}) collective-permute-start(bf16[128,2048]{1,0:T(8,128)(2,1)S(1)} %get-tuple-element.240), channel_id=1, source_target_pairs={{0,8},{8,0},{16,24},{24,16},{1,9},{9,1},{17,25},{25,17},{2,10},{10... | collective-permute-start | bytes 1572872 | tf_op jit(solution)/shard_map/attention_back/ppermute | solution.py:66
  445.0 28.2 %collective-permute-start.27 = (bf16[128,2048]{1,0:T(8,128)(2,1)S(1)}, bf16[128,2048]{1,0:T(8,128)(2,1)}, u32[]{:S(2)}, u32[]{:S(2)}) collective-permute-start(bf16[128,2048]{1,0:T(8,128)(2,1)S(1)} %get-tuple-element.239), channel_id=1, source_target_pairs={{0,16},{8,24},{16,0},{24,8},{1,17},{9,25},{17,1},{25,9},{2,18},{10... | collective-permute-start | bytes 1572872 | tf_op jit(solution)/shard_map/attention_back/ppermute | solution.py:66
  447.2 25.9 %collective-permute-start.28 = (bf16[128,2048]{1,0:T(8,128)(2,1)S(1)}, bf16[128,2048]{1,0:T(8,128)(2,1)}, u32[]{:S(2)}, u32[]{:S(2)}) collective-permute-start(bf16[128,2048]{1,0:T(8,128)(2,1)S(1)} %slice.114), channel_id=1, source_target_pairs={{0,8},{8,0},{16,24},{24,16},{1,9},{9,1},{17,25},{25,17},{2,10},{10... | collective-permute-start | bytes 1572872 | tf_op jit(solution)/shard_map/attention_back/ppermute | solution.py:66
  448.7 24.4 %collective-permute-start.29 = (bf16[128,2048]{1,0:T(8,128)(2,1)S(1)}, bf16[128,2048]{1,0:T(8,128)(2,1)}, u32[]{:S(2)}, u32[]{:S(2)}) collective-permute-start(bf16[128,2048]{1,0:T(8,128)(2,1)S(1)} %slice.115), channel_id=1, source_target_pairs={{0,16},{8,24},{16,0},{24,8},{1,17},{9,25},{17,1},{25,9},{2,18},{10... | collective-permute-start | bytes 1572872 | tf_op jit(solution)/shard_map/attention_back/ppermute | solution.py:66
  473.1 66.9 %all-to-all-start.3 = ((bf16[8,64,2048]{2,1,0:T(8,128)(2,1)}), bf16[8,64,2048]{2,1,0:T(8,128)(2,1)}, u32[]{:S(2)}, u32[]{:S(2)}) async-start(bf16[8,64,2048]{2,1,0:T(8,128)(2,1)} %bitcast.89), calls=%async_computation.6 | async-start | bytes 4194304 | tf_op jit(solution)/shard_map/attention_back/all_to_all | solution.py:705
  482.7 139.5 %reduce-scatter.11.cloned.1.call-start = ((), (), s32[]{:S(2)}) async-start(), calls=%async_computation.16 | async-start | bytes 4718592 | tf_op jit(solution)/shard_map/attention_back/reduce_scatter | solution.py:759
  482.7 31.5 %collective-permute-start.30 = (bf16[1024,512]{1,0:T(8,128)(2,1)}, bf16[1024,512]{1,0:T(8,128)(2,1)}, u32[]{:S(2)}, u32[]{:S(2)}) collective-permute-start(bf16[1024,512]{1,0:T(8,128)(2,1)} %get-tuple-element.182), channel_id=1, source_target_pairs={{8,0},{24,16},{9,1},{25,17},{10,2},{26,18},{11,3},{27,19},{12,4},{... | collective-permute-start | bytes 3145736 | tf_op jit(solution)/shard_map/attention_back/ppermute | solution.py:66
  484.0 38.5 %collective-permute-start.31 = (bf16[1024,512]{1,0:T(8,128)(2,1)}, bf16[1024,512]{1,0:T(8,128)(2,1)}, u32[]{:S(2)}, u32[]{:S(2)}) collective-permute-start(bf16[1024,512]{1,0:T(8,128)(2,1)} %get-tuple-element.183), channel_id=1, source_target_pairs={{16,0},{24,8},{17,1},{25,9},{18,2},{26,10},{19,3},{27,11},{20,4},{... | collective-permute-start | bytes 3145736 | tf_op jit(solution)/shard_map/attention_back/ppermute | solution.py:66
  486.6 35.9 %collective-permute-start.32 = (bf16[1024,512]{1,0:T(8,128)(2,1)}, bf16[1024,512]{1,0:T(8,128)(2,1)}, u32[]{:S(2)}, u32[]{:S(2)}) collective-permute-start(bf16[1024,512]{1,0:T(8,128)(2,1)} %get-tuple-element.184), channel_id=1, source_target_pairs={{16,8},{24,0},{17,9},{25,1},{18,10},{26,2},{19,11},{27,3},{20,12},... | collective-permute-start | bytes 3145736 | tf_op jit(solution)/shard_map/attention_back/ppermute | solution.py:66
  558.9 15.1 %collective-permute-start.35 = (bf16[256,768]{1,0:T(8,128)(2,1)S(1)}, bf16[256,768]{1,0:T(8,128)(2,1)S(1)}, u32[]{:S(2)}, u32[]{:S(2)}) collective-permute-start(bf16[256,768]{1,0:T(8,128)(2,1)S(1)} %slice.136), channel_id=1, source_target_pairs={{0,8},{8,0},{16,24},{24,16},{1,9},{9,1},{17,25},{25,17},{2,10},{10... | collective-permute-start | bytes 1179656 | tf_op jit(solution)/shard_map/weight_grads/ppermute | solution.py:66
  559.3 15.6 %collective-permute-start.36 = (bf16[256,768]{1,0:T(8,128)(2,1)S(1)}, bf16[256,768]{1,0:T(8,128)(2,1)S(1)}, u32[]{:S(2)}, u32[]{:S(2)}) collective-permute-start(bf16[256,768]{1,0:T(8,128)(2,1)S(1)} %slice.137), channel_id=1, source_target_pairs={{0,16},{8,24},{16,0},{24,8},{1,17},{9,25},{17,1},{25,9},{2,18},{10... | collective-permute-start | bytes 1179656 | tf_op jit(solution)/shard_map/weight_grads/ppermute | solution.py:66
  575.2 13.3 %collective-permute-start.40 = (bf16[64,2048]{1,0:T(8,128)(2,1)S(1)}, bf16[64,2048]{1,0:T(8,128)(2,1)S(1)}, u32[]{:S(2)}, u32[]{:S(2)}) collective-permute-start(bf16[64,2048]{1,0:T(8,128)(2,1)S(1)} %copy-done.63), channel_id=1, source_target_pairs={{0,16},{8,24},{16,0},{24,8},{1,17},{9,25},{17,1},{25,9},{2,18},{10... | collective-permute-start | bytes 786440 | tf_op jit(solution)/shard_map/weight_grads/ppermute | solution.py:66
  576.4 12.1 %collective-permute-start.39 = (bf16[64,2048]{1,0:T(8,128)(2,1)S(1)}, bf16[64,2048]{1,0:T(8,128)(2,1)S(1)}, u32[]{:S(2)}, u32[]{:S(2)}) collective-permute-start(bf16[64,2048]{1,0:T(8,128)(2,1)S(1)} %convolution_convert_fusion.10), channel_id=1, source_target_pairs={{0,8},{8,0},{16,24},{24,16},{1,9},{9,1},{17,25},{25,17},{2,10},{10... | collective-permute-start | bytes 786440 | tf_op jit(solution)/shard_map/weight_grads/ppermute | solution.py:66
  577.6 19.3 %collective-permute-start.37 = (bf16[256,768]{1,0:T(8,128)(2,1)S(1)}, bf16[256,768]{1,0:T(8,128)(2,1)S(1)}, u32[]{:S(2)}, u32[]{:S(2)}) collective-permute-start(bf16[256,768]{1,0:T(8,128)(2,1)S(1)} %add_convert_fusion.7), channel_id=1, source_target_pairs={{0,16},{8,24},{16,0},{24,8},{1,17},{9,25},{17,1},{25,9},{2,18},{10... | collective-permute-start | bytes 1179656 | tf_op jit(solution)/shard_map/weight_grads/ppermute | solution.py:66
  578.1 18.8 %collective-permute-start.38 = (bf16[256,768]{1,0:T(8,128)(2,1)S(1)}, bf16[256,768]{1,0:T(8,128)(2,1)S(1)}, u32[]{:S(2)}, u32[]{:S(2)}) collective-permute-start(bf16[256,768]{1,0:T(8,128)(2,1)S(1)} %add_convert_fusion.6), channel_id=1, source_target_pairs={{0,8},{8,0},{16,24},{24,16},{1,9},{9,1},{17,25},{25,17},{2,10},{10... | collective-permute-start | bytes 1179656 | tf_op jit(solution)/shard_map/weight_grads/ppermute | solution.py:66
  600.1 14.5 %collective-permute-start.43 = (bf16[128,2048]{1,0:T(8,128)(2,1)}, bf16[128,2048]{1,0:T(8,128)(2,1)}, u32[]{:S(2)}, u32[]{:S(2)}) collective-permute-start(bf16[128,2048]{1,0:T(8,128)(2,1)} %add_convert_fusion.5), channel_id=1, source_target_pairs={{0,16},{8,24},{16,0},{24,8},{1,17},{9,25},{17,1},{25,9},{2,18},{10... | collective-permute-start | bytes 1572872 | tf_op jit(solution)/shard_map/weight_grads/ppermute | solution.py:66
  603.6 13.1 %collective-permute-start.44 = (bf16[128,2048]{1,0:T(8,128)(2,1)}, bf16[128,2048]{1,0:T(8,128)(2,1)}, u32[]{:S(2)}, u32[]{:S(2)}) collective-permute-start(bf16[128,2048]{1,0:T(8,128)(2,1)} %add_convert_fusion.4), channel_id=1, source_target_pairs={{0,8},{8,0},{16,24},{24,16},{1,9},{9,1},{17,25},{25,17},{2,10},{10... | collective-permute-start | bytes 1572872 | tf_op jit(solution)/shard_map/weight_grads/ppermute | solution.py:66
  603.9 34.0 %all-to-all-start.4 = ((bf16[8,64,768]{2,1,0:T(8,128)(2,1)}), bf16[8,64,768]{2,1,0:T(8,128)(2,1)S(1)}, u32[]{:S(2)}, u32[]{:S(2)}) async-start(bf16[8,64,768]{2,1,0:T(8,128)(2,1)} %bitcast.32), calls=%async_computation.7 | async-start | bytes 1572864 | tf_op jit(solution)/shard_map/weight_grads/all_to_all | solution.py:705
  608.4 29.6 %collective-permute-start.42 = (bf16[64,2048]{1,0:T(8,128)(2,1)S(1)}, bf16[64,2048]{1,0:T(8,128)(2,1)S(1)}, u32[]{:S(2)}, u32[]{:S(2)}) collective-permute-start(bf16[64,2048]{1,0:T(8,128)(2,1)S(1)} %convert_add_fusion.4), channel_id=1, source_target_pairs={{0,0},{1,4},{2,8},{3,12},{4,16},{5,20},{6,24},{7,28},{8,1},{9,5},{... | collective-permute-start | bytes 786440 | tf_op jit(solution)/shard_map/weight_grads/ppermute | solution.py:778
  (77 other events, 520.7 us)
Sparse Core Ops, SparseCore 0:
  36.9 47.1 all-gather.4
  86.4 81.4 all-gather.6
  203.4 48.7 reduce-scatter.4
  257.7 49.2 all-gather.8
  337.6 47.7 reduce-scatter.6
  391.6 48.0 all-gather.10
  442.4 65.9 reduce-scatter.8
  551.3 46.2 reduce-scatter.10

commit v6 on v5

--- a/solution.py
+++ b/solution.py
@@ -120,11 +120,19 @@
     return [swapped(terms[near][rows], near) for rows, near, _ in near_halves(terms)]
 
 
-def sum_far(terms, passed):
+def sum_passing(terms, passed):
     return [
-        swapped((terms[far][rows].astype(F32) + part.astype(F32)).astype(BF16), far)
+        (terms[far][rows].astype(F32) + part.astype(F32)).astype(BF16)
         for part, (rows, _, far) in zip(passed, near_halves(terms))
     ]
+
+
+def send_passing(passing):
+    return [swapped(part, far) for part, far in zip(passing, (2, 1))]
+
+
+def sum_far(terms, passed):
+    return send_passing(sum_passing(terms, passed))
 
 
 def sum_end(terms, own, far):
@@ -740,8 +748,11 @@
                 lax.dynamic_slice_in_dim(attended, j * shard_rows, shard_rows, 1), residual_group
             )
         )
-        query_grad, key_value_grads, hidden_shards, output_terms = lax.optimization_barrier(
-            (query_grad, key_value_grads, hidden_shards, output_terms)
+        down_passing = sum_passing(down_terms, down_passed)
+        query_grad, key_value_grads, hidden_shards, output_terms, down_passing = (
+            lax.optimization_barrier(
+                (query_grad, key_value_grads, hidden_shards, output_terms, down_passing)
+            )
         )
         down_act = after(down_act, query_grad)
         layer_output = ((residual + down_act) * valid).astype(BF16)[None]
@@ -771,10 +782,10 @@
             (passed, own, terms, output_terms, gate_grad, up_grad)
         )
         summed = sum_end(terms, own, sum_far(terms, passed))
-        summed, output_part, down_passed = lax.optimization_barrier(
-            (summed, sum_to_owner(output_terms), down_passed)
-        )
-        down_sum = sum_end(down_terms, down_own, sum_far(down_terms, down_passed))
+        summed, output_part, down_passing = lax.optimization_barrier(
+            (summed, sum_to_owner(output_terms), down_passing)
+        )
+        down_sum = sum_end(down_terms, down_own, send_passing(down_passing))
         output_grad = lax.ppermute(
             output_part.astype(BF16),
             ("blk", "head"),

time: 655 us -> 651 us (level)
    unnamed x135 -> x131, local copies, waits for them, and re-layouts: 39.3 us -> 39.3 us
  transfers between devices with their start and end apart: 58 -> 58, of which waited for: 32 -> 33; matrix products, arithmetic and copies ran while one was open for 20% -> 20% of each run, Pallas kernels for 8% -> 8%
where the time goes in v6:
time: 651 us; the launch traced here: 643 us
  waiting for transfers between devices  277 us (43%)
  starting transfers between devices  96.6 us (15%)
  local copies, waits for them, and re-layouts  87.2 us (13%)
  Pallas kernels  85 us (13%)
  matrix products  56.5 us (9%)
  other arithmetic  25.3 us (4%)
  between operations  16.1 us (2%)
    ppermute x43, waiting for transfers between devices, swapped(): return lax.ppermute(value, 'blk', pairs)  215 us
    ppermute x43, starting transfers between devices, swapped(): return lax.ppermute(value, 'blk', pairs)  52.4 us
    dot_general x16, matrix products, outer_sum(): lax.dot_general(left, right, (((0,), (0,)), ((), ())), preferred_element_...  41.1 us
    unnamed x131, local copies, waits for them, and re-layouts  39.3 us
    pallas_call x1, Pallas kernels, feed_forward(): pl.pallas_call(functools.partial(feed_kernel, columns=min(256, hidden)),...  29.1 us
    dynamic_update_slice x16, local copies, waits for them, and re-layouts, gather_blk(): whole = lax.dynamic_update_slice(whole, piece[None], start)  20.1 us
    pallas_call x1, Pallas kernels, backward_attention(): pl.pallas_call(functools.partial(backward_kernel, masks=masks, started=st...  19.4 us
    all_to_all x2, waiting for transfers between devices, to_shards(): lax.all_to_all(summed.astype(BF16).reshape(parts, shard_rows, summed.shap...  17.6 us
  transfers between devices with their start and end apart: 58, of which 33 were waited for; matrix products, arithmetic and copies ran while one was open for 20% of the time, Pallas kernels for 8%

profile of v6, /device:TPU:5, one launch (start us, length us, event | category | flops | bytes accessed | tf_op | source)
XLA Modules:
  0.0 643.3 jit_solution(16639630192579305797)
XLA Ops:
  11.0 5.5 all-to-all-start
  20.2 16.6 %all-to-all-done = bf16[8,64,768]{2,1,0:T(8,128)(2,1)} async-done(((bf16[8,64,768]{2,1,0:T(8,128)(2,1)}), bf16[8,64,768]{2,1,0:T(8,128)(2,1)}, u32[]{:S(2)}, u32[]{:S(2)}) %all-to-all-start) | async-done | bytes 786464 | tf_op jit(solution)/shard_map/projection_weights/all_to_all | solution.py:622
  40.0 3.4 collective-permute-start.4
  44.9 10.5 %collective-permute-done = bf16[512,768]{1,0:T(8,128)(2,1)} collective-permute-done((bf16[512,768]{1,0:T(8,128)(2,1)}, bf16[512,768]{1,0:T(8,128)(2,1)}, u32[]{:S(2)}, u32[]{:S(2)}) %collective-permute-start) | collective-permute-done | bytes 786464 | tf_op jit(solution)/shard_map/projection_weights/ppermute | solution.py:66
  56.5 4.6 collective-permute-start.2
  71.6 3.3 collective-permute-start.6
  77.5 3.4 collective-permute-start.7
  90.0 6.1 project.1
  97.8 10.2 %all-to-all-start.1 = ((bf16[8,64,1024]{2,1,0:T(8,128)(2,1)}), bf16[8,64,1024]{2,1,0:T(8,128)(2,1)}, u32[]{:S(2)}, u32[]{:S(2)}) async-start(bf16[8,64,1024]{2,1,0:T(8,128)(2,1)} %copy-done.24), calls=%async_computation.1 | async-start | bytes 2097152 | tf_op jit(solution)/shard_map/attention/all_to_all | solution.py:660
  108.1 6.9 %collective-permute-start.9 = (bf16[1024,512]{1,0:T(8,128)(2,1)}, bf16[1024,512]{1,0:T(8,128)(2,1)S(1)}, u32[]{:S(2)}, u32[]{:S(2)}) collective-permute-start(bf16[1024,512]{1,0:T(8,128)(2,1)} %copy-done.14), channel_id=1, source_target_pairs={{0,8},{16,24},{1,9},{17,25},{2,10},{18,26},{3,11},{19,27},{4,12},{... | collective-permute-start | bytes 3145736 | tf_op jit(solution)/shard_map/attention/ppermute | solution.py:66
  119.9 17.9 %collective-permute-done.9.refs_1_.refs_2_ = bf16[1024,512]{1,0:T(8,128)(2,1)S(1)} collective-permute-done((bf16[1024,512]{1,0:T(8,128)(2,1)}, bf16[1024,512]{1,0:T(8,128)(2,1)S(1)}, u32[]{:S(2)}, u32[]{:S(2)}) %collective-permute-start.9) | collective-permute-done | bytes 1048608 | tf_op jit(solution)/shard_map/attention/ppermute | solution.py:66
  138.8 25.3 %collective-permute-done.10.refs_2_.refs_1_ = bf16[1024,512]{1,0:T(8,128)(2,1)S(1)} collective-permute-done((bf16[1024,512]{1,0:T(8,128)(2,1)}, bf16[1024,512]{1,0:T(8,128)(2,1)S(1)}, u32[]{:S(2)}, u32[]{:S(2)}) %collective-permute-start.10) | collective-permute-done | bytes 1048608 | tf_op jit(solution)/shard_map/attention/ppermute | solution.py:66
  167.9 4.4 all-to-all-start.2
  179.8 13.4 %attention_forward.1 = (bf16[1024,256]{1,0:T(8,128)(2,1)S(1)}, f32[2,1,1024]{2,1,0:T(1,128)S(1)}) custom-call(s32[2]{0:T(128)S(1)} %pad_add_fusion.place_ref, bf16[1024,256]{1,0:T(8,128)(2,1)S(1)} %copy-done.27, bf16[1024,512]{1,0:T(8,128)(2,1)S(1)} %copy-done.15, bf16[1024,512]{1,0:T(8,128)(2,1)S(1)} %copy-done.17, bf16[1024,512]{1,0:T(8,128)(2,1)S(1)} %copy-done.19, ...), custom_call_target="tpu_custom_call" | custom-call | tf_op jit(solution)/shard_map/attention/attention_forward/pallas_call | solution.py:426
  193.2 3.9 collective-permute-done.12
  198.0 4.5 convolution_convert_fusion
  207.6 44.3 %collective-permute-done.14 = bf16[512,2048]{1,0:T(8,128)(2,1)} collective-permute-done((bf16[512,2048]{1,0:T(8,128)(2,1)S(1)}, bf16[512,2048]{1,0:T(8,128)(2,1)}, u32[]{:S(2)}, u32[]{:S(2)}) %collective-permute-start.14) | collective-permute-done | bytes 2097184 | tf_op jit(solution)/shard_map/attention/ppermute | solution.py:66
  264.6 4.5 broadcast_in_dim.119
  270.6 11.0 %collective-permute-done.16 = bf16[256,2048]{1,0:T(8,128)(2,1)S(1)} collective-permute-done((bf16[256,2048]{1,0:T(8,128)(2,1)S(1)}, bf16[256,2048]{1,0:T(8,128)(2,1)S(1)}, u32[]{:S(2)}, u32[]{:S(2)}) %collective-permute-start.16) | collective-permute-done | bytes 1048608 | tf_op jit(solution)/shard_map/attention/ppermute | solution.py:66
  286.4 3.1 bitcast_dynamic-update-slice_fusion.1
  289.5 3.1 bitcast_dynamic-update-slice_fusion
  302.5 4.5 all-gather.9.cloned.1.call-done.normed_ref
  307.0 29.1 %feed_forward.1 = (bf16[1024,1024]{1,0:T(8,128)(2,1)S(1)}, bf16[1024,2048]{1,0:T(8,128)(2,1)}, bf16[1024,2048]{1,0:T(8,128)(2,1)}) custom-call(bf16[1024,2048]{1,0:T(8,128)(2,1)} %all-gather.9.cloned.1.call-done.normed_ref, bf16[1024,2048]{1,0:T(8,128)(2,1)} %all-gather.7.cloned.1.call-done.grad_ref, bf16[2048,2048]{1,0:T(8,128)(2,1)} %bitcast.23.both_ref, ...), custom_call_target="tpu_custom_call" | custom-call | tf_op jit(solution)/shard_map/feed_forward/feed_forward/pallas_call | solution.py:567
  337.8 5.0 convolution_convert_fusion.2
  345.7 2.7 fusion.19
  353.0 4.5 fusion.13
  357.5 3.8 convolution_convert_fusion.4
  361.3 3.8 convolution_convert_fusion.3
  365.1 2.7 convolution_convert_fusion.5
  367.8 8.3 %convolution_convert_fusion.1 = bf16[1024,2048]{1,0:T(8,128)(2,1)} fusion(bf16[1024,1024]{1,0:T(8,128)(2,1)S(1)} %copy-done.44, bf16[1024,2048]{1,0:T(8,128)(2,1)} %bitcast.29.down_ref), kind=kOutput, calls=%fused_computation.1 | convolution fusion | flops 4297064448 | bytes 10485760 | tf_op jit(solution)/shard_map/feed_forward/dot_general | solution.py:52
  376.1 9.4 %reduce-scatter.7.cloned.1.call-done.grad_ref = bf16[128,2048]{1,0:T(8,128)(2,1)} async-done(((bf16[1024,2048]{1,0:T(8,128)(2,1)}), bf16[128,2048]{1,0:T(8,128)(2,1)}) %reduce-scatter.7.cloned.1.call-update) | async-done | bytes 524304 | tf_op jit(solution)/shard_map/feed_forward/reduce_scatter | solution.py:691
  399.9 17.1 %collective-permute-done.23 = bf16[256,2048]{1,0:T(8,128)(2,1)S(1)} collective-permute-done((bf16[256,2048]{1,0:T(8,128)(2,1)S(1)}, bf16[256,2048]{1,0:T(8,128)(2,1)S(1)}, u32[]{:S(2)}, u32[]{:S(2)}) %collective-permute-start.23) | collective-permute-done | bytes 1048608 | tf_op jit(solution)/shard_map/attention_back/ppermute | solution.py:66
  417.2 22.4 %collective-permute-done.25 = bf16[256,2048]{1,0:T(8,128)(2,1)S(1)} collective-permute-done((bf16[256,2048]{1,0:T(8,128)(2,1)S(1)}, bf16[256,2048]{1,0:T(8,128)(2,1)S(1)}, u32[]{:S(2)}, u32[]{:S(2)}) %collective-permute-start.25) | collective-permute-done | bytes 1048608 | tf_op jit(solution)/shard_map/attention_back/ppermute | solution.py:66
  449.1 2.7 convolution_convert_fusion.14.do_ref
  451.8 19.4 %attention_backward.1 = (f32[1024,256]{1,0:T(8,128)S(1)}, bf16[1024,512]{1,0:T(8,128)(2,1)}, bf16[1024,512]{1,0:T(8,128)(2,1)}, bf16[1024,512]{1,0:T(8,128)(2,1)}, bf16[1024,512]{1,0:T(8,128)(2,1)S(1)}) custom-call(s32[2]{0:T(128)S(1)} %pad_add_fusion.place_ref, bf16[1024,256]{1,0:T(8,128)(2,1)S(1)} %copy-done.28, bf16[1024,256]{1,0:T(8,128)(2,1)S(1)} %copy-done.4, ...), custom_call_target="tpu_custom_call" | custom-call | tf_op jit(solution)/shard_map/attention_back/attention_backward/pallas_call | solution.py:511
  473.1 9.5 %all-to-all-start.3 = ((bf16[8,64,2048]{2,1,0:T(8,128)(2,1)}), bf16[8,64,2048]{2,1,0:T(8,128)(2,1)}, u32[]{:S(2)}, u32[]{:S(2)}) async-start(bf16[8,64,2048]{2,1,0:T(8,128)(2,1)} %bitcast.89), calls=%async_computation.6 | async-start | bytes 4194304 | tf_op jit(solution)/shard_map/attention_back/all_to_all | solution.py:713
  493.1 21.1 %collective-permute-done.30.refs_1_ = bf16[1024,512]{1,0:T(8,128)(2,1)} collective-permute-done((bf16[1024,512]{1,0:T(8,128)(2,1)}, bf16[1024,512]{1,0:T(8,128)(2,1)}, u32[]{:S(2)}, u32[]{:S(2)}) %collective-permute-start.30) | collective-permute-done | bytes 1048608 | tf_op jit(solution)/shard_map/attention_back/ppermute | solution.py:66
  514.2 3.2 convolution_convert_fusion.10
  522.5 17.6 %all-to-all-done.3.in_ref = bf16[8,64,2048]{2,1,0:T(8,128)(2,1)} async-done(((bf16[8,64,2048]{2,1,0:T(8,128)(2,1)}), bf16[8,64,2048]{2,1,0:T(8,128)(2,1)}, u32[]{:S(2)}, u32[]{:S(2)}) %all-to-all-start.3) | async-done | bytes 2097184 | tf_op jit(solution)/shard_map/attention_back/all_to_all | solution.py:713
  542.2 7.9 %project_back.1 = (bf16[1024,768]{1,0:T(8,128)(2,1)S(1)}, bf16[1024,2048]{1,0:T(8,128)(2,1)}) custom-call(s32[2]{0:T(128)S(1)} %pad_add_fusion.place_ref, f32[1024,256]{1,0:T(8,128)} %copy-done.29, bf16[2048,768]{1,0:T(8,128)(2,1)S(1)} %bitcast.86, f32[1024,128]{1,0:T(8,128)S(1)} %copy-done.7, f32[1024,128]{1,0:T(8,128)S(1)} %copy-done.9, ...), custom_call_target="tpu_custom_call" | custom-call | tf_op jit(solution)/shard_map/attention_back/project_back/pallas_call | solution.py:274
  560.6 3.8 spread.2
  566.4 7.5 %collective-permute-done.35 = bf16[256,768]{1,0:T(8,128)(2,1)S(1)} collective-permute-done((bf16[256,768]{1,0:T(8,128)(2,1)S(1)}, bf16[256,768]{1,0:T(8,128)(2,1)S(1)}, u32[]{:S(2)}, u32[]{:S(2)}) %collective-permute-start.35) | collective-permute-done | bytes 393248 | tf_op jit(solution)/shard_map/weight_grads/ppermute | solution.py:66
  578.4 3.8 collective-permute-done.41
  582.2 6.2 collective-permute-done.40
  588.6 8.3 %collective-permute-done.37 = bf16[256,768]{1,0:T(8,128)(2,1)S(1)} collective-permute-done((bf16[256,768]{1,0:T(8,128)(2,1)S(1)}, bf16[256,768]{1,0:T(8,128)(2,1)S(1)}, u32[]{:S(2)}, u32[]{:S(2)}) %collective-permute-start.37) | collective-permute-done | bytes 393248 | tf_op jit(solution)/shard_map/weight_grads/ppermute | solution.py:66
  600.0 4.5 all-to-all-start.4
  604.4 6.2 collective-permute-start.42
  622.0 12.0 %collective-permute-done.42 = bf16[64,2048]{1,0:T(8,128)(2,1)S(1)} collective-permute-done((bf16[64,2048]{1,0:T(8,128)(2,1)S(1)}, bf16[64,2048]{1,0:T(8,128)(2,1)S(1)}, u32[]{:S(2)}, u32[]{:S(2)}) %collective-permute-start.42) | collective-permute-done | bytes 262176 | tf_op jit(solution)/shard_map/weight_grads/ppermute | solution.py:789
  (309 shorter events, 174.2 us)
Async XLA Ops:
  11.0 25.8 %all-to-all-start = ((bf16[8,64,768]{2,1,0:T(8,128)(2,1)}), bf16[8,64,768]{2,1,0:T(8,128)(2,1)}, u32[]{:S(2)}, u32[]{:S(2)}) async-start(bf16[8,64,768]{2,1,0:T(8,128)(2,1)} %collect.3), calls=%async_computation | async-start | bytes 1572864 | tf_op jit(solution)/shard_map/projection_weights/all_to_all | solution.py:622
  16.6 69.7 %all-gather.5.cloned.1.call-start = ((), (), s32[]{:S(2)}) async-start(), calls=%async_computation.9 | async-start | bytes 4718592 | tf_op jit(solution)/shard_map/tokens_gather/all_gather | solution.py:631
  36.8 131.1 %all-gather.7.cloned.1.call-start = ((), (), s32[]{:S(2)}) async-start(), calls=%async_computation.10 | async-start | bytes 4718592 | tf_op jit(solution)/shard_map/attention/all_gather | solution.py:657
  36.9 18.6 %collective-permute-start = (bf16[512,768]{1,0:T(8,128)(2,1)}, bf16[512,768]{1,0:T(8,128)(2,1)}, u32[]{:S(2)}, u32[]{:S(2)}) collective-permute-start(bf16[512,768]{1,0:T(8,128)(2,1)} %bitcast.2), channel_id=1, source_target_pairs={{0,8},{8,0},{16,24},{24,16},{1,9},{9,1},{17,25},{25,17},{2,10},{10... | collective-permute-start | bytes 2359304 | tf_op jit(solution)/shard_map/projection_weights/ppermute | solution.py:66
  38.2 22.9 %collective-permute-start.1 = (bf16[512,768]{1,0:T(8,128)(2,1)}, bf16[512,768]{1,0:T(8,128)(2,1)}, u32[]{:S(2)}, u32[]{:S(2)}) collective-permute-start(bf16[512,768]{1,0:T(8,128)(2,1)} %bitcast.2), channel_id=1, source_target_pairs={{0,16},{8,24},{16,0},{24,8},{1,17},{9,25},{17,1},{25,9},{2,18},{10... | collective-permute-start | bytes 2359304 | tf_op jit(solution)/shard_map/projection_weights/ppermute | solution.py:66
  40.0 27.0 %collective-permute-start.4 = (bf16[64,2048]{1,0:T(8,128)(2,1)S(1)}, bf16[64,2048]{1,0:T(8,128)(2,1)S(1)}, u32[]{:S(2)}, u32[]{:S(2)}) collective-permute-start(bf16[64,2048]{1,0:T(8,128)(2,1)S(1)} %copy-done.64), channel_id=1, source_target_pairs={{0,0},{4,1},{8,2},{12,3},{16,4},{20,5},{24,6},{28,7},{1,8},{5,9},{... | collective-permute-start | bytes 786440 | tf_op jit(solution)/shard_map/hidden_weights/ppermute | solution.py:638
  56.5 11.2 %collective-permute-start.2 = (bf16[256,768]{1,0:T(8,128)(2,1)S(1)}, bf16[256,768]{1,0:T(8,128)(2,1)S(1)}, u32[]{:S(2)}, u32[]{:S(2)}) collective-permute-start(bf16[256,768]{1,0:T(8,128)(2,1)S(1)} %slice.128), channel_id=1, source_target_pairs={{0,16},{8,24},{16,0},{24,8},{1,17},{9,25},{17,1},{25,9},{2,18},{10... | collective-permute-start | bytes 1179656 | tf_op jit(solution)/shard_map/projection_weights/ppermute | solution.py:66
  97.8 68.2 %all-to-all-start.1 = ((bf16[8,64,1024]{2,1,0:T(8,128)(2,1)}), bf16[8,64,1024]{2,1,0:T(8,128)(2,1)}, u32[]{:S(2)}, u32[]{:S(2)}) async-start(bf16[8,64,1024]{2,1,0:T(8,128)(2,1)} %copy-done.24), calls=%async_computation.1 | async-start | bytes 2097152 | tf_op jit(solution)/shard_map/attention/all_to_all | solution.py:660
  108.1 29.7 %collective-permute-start.9 = (bf16[1024,512]{1,0:T(8,128)(2,1)}, bf16[1024,512]{1,0:T(8,128)(2,1)S(1)}, u32[]{:S(2)}, u32[]{:S(2)}) collective-permute-start(bf16[1024,512]{1,0:T(8,128)(2,1)} %copy-done.14), channel_id=1, source_target_pairs={{0,8},{16,24},{1,9},{17,25},{2,10},{18,26},{3,11},{19,27},{4,12},{... | collective-permute-start | bytes 3145736 | tf_op jit(solution)/shard_map/attention/ppermute | solution.py:66
  114.9 49.2 %collective-permute-start.10 = (bf16[1024,512]{1,0:T(8,128)(2,1)}, bf16[1024,512]{1,0:T(8,128)(2,1)S(1)}, u32[]{:S(2)}, u32[]{:S(2)}) collective-permute-start(bf16[1024,512]{1,0:T(8,128)(2,1)} %copy-done.14), channel_id=1, source_target_pairs={{0,16},{8,24},{1,17},{9,25},{2,18},{10,26},{3,19},{11,27},{4,20},{... | collective-permute-start | bytes 3145736 | tf_op jit(solution)/shard_map/attention/ppermute | solution.py:66
  116.2 48.8 %collective-permute-start.11 = (bf16[1024,512]{1,0:T(8,128)(2,1)}, bf16[1024,512]{1,0:T(8,128)(2,1)S(1)}, u32[]{:S(2)}, u32[]{:S(2)}) collective-permute-start(bf16[1024,512]{1,0:T(8,128)(2,1)} %copy-done.14), channel_id=1, source_target_pairs={{0,24},{8,16},{1,25},{9,17},{2,26},{10,18},{3,27},{11,19},{4,28},{... | collective-permute-start | bytes 3145736 | tf_op jit(solution)/shard_map/attention/ppermute | solution.py:66
  167.9 35.4 %all-to-all-start.2 = ((bf16[8,64,1024]{2,1,0:T(8,128)(2,1)}), bf16[8,64,1024]{2,1,0:T(8,128)(2,1)}, u32[]{:S(2)}, u32[]{:S(2)}) async-start(bf16[8,64,1024]{2,1,0:T(8,128)(2,1)} %copy-done.25), calls=%async_computation.2 | async-start | bytes 2097152 | tf_op jit(solution)/shard_map/attention/all_to_all | solution.py:664
  172.3 80.8 %reduce-scatter.5.cloned.1.call-start = ((), (), s32[]{:S(2)}) async-start(), calls=%async_computation.11 | async-start | bytes 4718592 | tf_op jit(solution)/shard_map/attention/reduce_scatter | solution.py:677
  172.3 24.8 %collective-permute-start.12 = (bf16[256,2048]{1,0:T(8,128)(2,1)}, bf16[256,2048]{1,0:T(8,128)(2,1)}, u32[]{:S(2)}, u32[]{:S(2)}) collective-permute-start(bf16[256,2048]{1,0:T(8,128)(2,1)} %param.18), channel_id=1, source_target_pairs={{0,8},{8,0},{16,24},{24,16},{1,9},{9,1},{17,25},{25,17},{2,10},{10... | collective-permute-start | bytes 3145736 | tf_op jit(solution)/shard_map/attention/ppermute | solution.py:66
  173.5 24.5 %collective-permute-start.13 = (bf16[256,2048]{1,0:T(8,128)(2,1)}, bf16[256,2048]{1,0:T(8,128)(2,1)}, u32[]{:S(2)}, u32[]{:S(2)}) collective-permute-start(bf16[256,2048]{1,0:T(8,128)(2,1)} %param.18), channel_id=1, source_target_pairs={{0,16},{8,24},{16,0},{24,8},{1,17},{9,25},{17,1},{25,9},{2,18},{10... | collective-permute-start | bytes 3145736 | tf_op jit(solution)/shard_map/attention/ppermute | solution.py:66
  203.3 103.7 %all-gather.9.cloned.1.call-start = ((), (), s32[]{:S(2)}) async-start(), calls=%async_computation.12 | async-start | bytes 4718592 | tf_op jit(solution)/shard_map/feed_forward/all_gather | solution.py:687
  206.0 45.9 %collective-permute-start.14 = (bf16[512,2048]{1,0:T(8,128)(2,1)S(1)}, bf16[512,2048]{1,0:T(8,128)(2,1)}, u32[]{:S(2)}, u32[]{:S(2)}) collective-permute-start(bf16[512,2048]{1,0:T(8,128)(2,1)S(1)} %bitcast.90), channel_id=1, source_target_pairs={{0,8},{8,0},{16,24},{24,16},{1,9},{9,1},{17,25},{25,17},{2,10},{10... | collective-permute-start | bytes 6291464 | tf_op jit(solution)/shard_map/attention/ppermute | solution.py:66
  207.3 45.8 %collective-permute-start.15 = (bf16[512,2048]{1,0:T(8,128)(2,1)S(1)}, bf16[512,2048]{1,0:T(8,128)(2,1)}, u32[]{:S(2)}, u32[]{:S(2)}) collective-permute-start(bf16[512,2048]{1,0:T(8,128)(2,1)S(1)} %bitcast.91), channel_id=1, source_target_pairs={{0,16},{8,24},{16,0},{24,8},{1,17},{9,25},{17,1},{25,9},{2,18},{10... | collective-permute-start | bytes 6291464 | tf_op jit(solution)/shard_map/attention/ppermute | solution.py:66
  257.6 127.9 %reduce-scatter.7.cloned.1.call-start = ((), (), s32[]{:S(2)}) async-start(), calls=%async_computation.13 | async-start | bytes 4718592 | tf_op jit(solution)/shard_map/feed_forward/reduce_scatter | solution.py:691
  259.0 22.5 %collective-permute-start.16 = (bf16[256,2048]{1,0:T(8,128)(2,1)S(1)}, bf16[256,2048]{1,0:T(8,128)(2,1)S(1)}, u32[]{:S(2)}, u32[]{:S(2)}) collective-permute-start(bf16[256,2048]{1,0:T(8,128)(2,1)S(1)} %slice.100), channel_id=1, source_target_pairs={{0,16},{8,24},{16,0},{24,8},{1,17},{9,25},{17,1},{25,9},{2,18},{10... | collective-permute-start | bytes 3145736 | tf_op jit(solution)/shard_map/attention/ppermute | solution.py:66
  260.7 22.2 %collective-permute-start.17 = (bf16[256,2048]{1,0:T(8,128)(2,1)S(1)}, bf16[256,2048]{1,0:T(8,128)(2,1)S(1)}, u32[]{:S(2)}, u32[]{:S(2)}) collective-permute-start(bf16[256,2048]{1,0:T(8,128)(2,1)S(1)} %slice.101), channel_id=1, source_target_pairs={{0,8},{8,0},{16,24},{24,16},{1,9},{9,1},{17,25},{25,17},{2,10},{10... | collective-permute-start | bytes 3145736 | tf_op jit(solution)/shard_map/attention/ppermute | solution.py:66
  337.5 104.7 %all-gather.11.cloned.1.call-start = ((), (), s32[]{:S(2)}) async-start(), calls=%async_computation.14 | async-start | bytes 4718592 | tf_op jit(solution)/shard_map/attention_back/all_gather | solution.py:722
  344.3 31.8 %collective-permute-start.20 = (bf16[256,2048]{1,0:T(8,128)(2,1)}, bf16[256,2048]{1,0:T(8,128)(2,1)}, u32[]{:S(2)}, u32[]{:S(2)}) collective-permute-start(bf16[256,2048]{1,0:T(8,128)(2,1)} %get-tuple-element.240), channel_id=1, source_target_pairs={{0,8},{8,0},{16,24},{24,16},{1,9},{9,1},{17,25},{25,17},{2,10},{10... | collective-permute-start | bytes 3145736 | tf_op jit(solution)/shard_map/feed_forward/ppermute | solution.py:66
  345.5 30.7 %collective-permute-start.21 = (bf16[256,2048]{1,0:T(8,128)(2,1)}, bf16[256,2048]{1,0:T(8,128)(2,1)}, u32[]{:S(2)}, u32[]{:S(2)}) collective-permute-start(bf16[256,2048]{1,0:T(8,128)(2,1)} %get-tuple-element.239), channel_id=1, source_target_pairs={{0,16},{8,24},{16,0},{24,8},{1,17},{9,25},{17,1},{25,9},{2,18},{10... | collective-permute-start | bytes 3145736 | tf_op jit(solution)/shard_map/feed_forward/ppermute | solution.py:66
  391.4 224.7 %reduce-scatter.9.cloned.1.call-start = ((), (), s32[]{:S(2)}) async-start(), calls=%async_computation.15 | async-start | bytes 4718592 | tf_op jit(solution)/shard_map/attention_back/reduce_scatter | solution.py:730
  395.0 22.0 %collective-permute-start.23 = (bf16[256,2048]{1,0:T(8,128)(2,1)S(1)}, bf16[256,2048]{1,0:T(8,128)(2,1)S(1)}, u32[]{:S(2)}, u32[]{:S(2)}) collective-permute-start(bf16[256,2048]{1,0:T(8,128)(2,1)S(1)} %add_convert_fusion.3), channel_id=1, source_target_pairs={{0,16},{8,24},{16,0},{24,8},{1,17},{9,25},{17,1},{25,9},{2,18},{10... | collective-permute-start | bytes 3145736 | tf_op jit(solution)/shard_map/attention_back/ppermute | solution.py:66
  395.5 21.7 %collective-permute-start.22 = (bf16[256,2048]{1,0:T(8,128)(2,1)S(1)}, bf16[256,2048]{1,0:T(8,128)(2,1)S(1)}, u32[]{:S(2)}, u32[]{:S(2)}) collective-permute-start(bf16[256,2048]{1,0:T(8,128)(2,1)S(1)} %slice.107), channel_id=1, source_target_pairs={{0,8},{8,0},{16,24},{24,16},{1,9},{9,1},{17,25},{25,17},{2,10},{10... | collective-permute-start | bytes 3145736 | tf_op jit(solution)/shard_map/attention_back/ppermute | solution.py:66
  398.4 41.2 %collective-permute-start.25 = (bf16[256,2048]{1,0:T(8,128)(2,1)S(1)}, bf16[256,2048]{1,0:T(8,128)(2,1)S(1)}, u32[]{:S(2)}, u32[]{:S(2)}) collective-permute-start(bf16[256,2048]{1,0:T(8,128)(2,1)S(1)} %add_convert_fusion.1), channel_id=1, source_target_pairs={{0,8},{8,0},{16,24},{24,16},{1,9},{9,1},{17,25},{25,17},{2,10},{10... | collective-permute-start | bytes 3145736 | tf_op jit(solution)/shard_map/attention_back/ppermute | solution.py:66
  398.7 40.9 %collective-permute-start.24 = (bf16[256,2048]{1,0:T(8,128)(2,1)S(1)}, bf16[256,2048]{1,0:T(8,128)(2,1)S(1)}, u32[]{:S(2)}, u32[]{:S(2)}) collective-permute-start(bf16[256,2048]{1,0:T(8,128)(2,1)S(1)} %slice.110), channel_id=1, source_target_pairs={{0,16},{8,24},{16,0},{24,8},{1,17},{9,25},{17,1},{25,9},{2,18},{10... | collective-permute-start | bytes 3145736 | tf_op jit(solution)/shard_map/attention_back/ppermute | solution.py:66
  443.7 29.4 %collective-permute-start.26 = (bf16[128,2048]{1,0:T(8,128)(2,1)S(1)}, bf16[128,2048]{1,0:T(8,128)(2,1)}, u32[]{:S(2)}, u32[]{:S(2)}) collective-permute-start(bf16[128,2048]{1,0:T(8,128)(2,1)S(1)} %get-tuple-element.244), channel_id=1, source_target_pairs={{0,8},{8,0},{16,24},{24,16},{1,9},{9,1},{17,25},{25,17},{2,10},{10... | collective-permute-start | bytes 1572872 | tf_op jit(solution)/shard_map/attention_back/ppermute | solution.py:66
  444.9 28.2 %collective-permute-start.27 = (bf16[128,2048]{1,0:T(8,128)(2,1)S(1)}, bf16[128,2048]{1,0:T(8,128)(2,1)}, u32[]{:S(2)}, u32[]{:S(2)}) collective-permute-start(bf16[128,2048]{1,0:T(8,128)(2,1)S(1)} %get-tuple-element.243), channel_id=1, source_target_pairs={{0,16},{8,24},{16,0},{24,8},{1,17},{9,25},{17,1},{25,9},{2,18},{10... | collective-permute-start | bytes 1572872 | tf_op jit(solution)/shard_map/attention_back/ppermute | solution.py:66
  447.2 25.9 %collective-permute-start.28 = (bf16[128,2048]{1,0:T(8,128)(2,1)S(1)}, bf16[128,2048]{1,0:T(8,128)(2,1)}, u32[]{:S(2)}, u32[]{:S(2)}) collective-permute-start(bf16[128,2048]{1,0:T(8,128)(2,1)S(1)} %slice.114), channel_id=1, source_target_pairs={{0,8},{8,0},{16,24},{24,16},{1,9},{9,1},{17,25},{25,17},{2,10},{10... | collective-permute-start | bytes 1572872 | tf_op jit(solution)/shard_map/attention_back/ppermute | solution.py:66
  448.7 24.4 %collective-permute-start.29 = (bf16[128,2048]{1,0:T(8,128)(2,1)S(1)}, bf16[128,2048]{1,0:T(8,128)(2,1)}, u32[]{:S(2)}, u32[]{:S(2)}) collective-permute-start(bf16[128,2048]{1,0:T(8,128)(2,1)S(1)} %slice.115), channel_id=1, source_target_pairs={{0,16},{8,24},{16,0},{24,8},{1,17},{9,25},{17,1},{25,9},{2,18},{10... | collective-permute-start | bytes 1572872 | tf_op jit(solution)/shard_map/attention_back/ppermute | solution.py:66
  473.1 66.9 %all-to-all-start.3 = ((bf16[8,64,2048]{2,1,0:T(8,128)(2,1)}), bf16[8,64,2048]{2,1,0:T(8,128)(2,1)}, u32[]{:S(2)}, u32[]{:S(2)}) async-start(bf16[8,64,2048]{2,1,0:T(8,128)(2,1)} %bitcast.89), calls=%async_computation.6 | async-start | bytes 4194304 | tf_op jit(solution)/shard_map/attention_back/all_to_all | solution.py:713
  482.7 135.6 %reduce-scatter.11.cloned.1.call-start = ((), (), s32[]{:S(2)}) async-start(), calls=%async_computation.16 | async-start | bytes 4718592 | tf_op jit(solution)/shard_map/attention_back/reduce_scatter | solution.py:770
  482.7 31.5 %collective-permute-start.30 = (bf16[1024,512]{1,0:T(8,128)(2,1)}, bf16[1024,512]{1,0:T(8,128)(2,1)}, u32[]{:S(2)}, u32[]{:S(2)}) collective-permute-start(bf16[1024,512]{1,0:T(8,128)(2,1)} %get-tuple-element.184), channel_id=1, source_target_pairs={{8,0},{24,16},{9,1},{25,17},{10,2},{26,18},{11,3},{27,19},{12,4},{... | collective-permute-start | bytes 3145736 | tf_op jit(solution)/shard_map/attention_back/ppermute | solution.py:66
  484.0 38.5 %collective-permute-start.31 = (bf16[1024,512]{1,0:T(8,128)(2,1)}, bf16[1024,512]{1,0:T(8,128)(2,1)}, u32[]{:S(2)}, u32[]{:S(2)}) collective-permute-start(bf16[1024,512]{1,0:T(8,128)(2,1)} %get-tuple-element.185), channel_id=1, source_target_pairs={{16,0},{24,8},{17,1},{25,9},{18,2},{26,10},{19,3},{27,11},{20,4},{... | collective-permute-start | bytes 3145736 | tf_op jit(solution)/shard_map/attention_back/ppermute | solution.py:66
  486.5 35.9 %collective-permute-start.32 = (bf16[1024,512]{1,0:T(8,128)(2,1)}, bf16[1024,512]{1,0:T(8,128)(2,1)}, u32[]{:S(2)}, u32[]{:S(2)}) collective-permute-start(bf16[1024,512]{1,0:T(8,128)(2,1)} %get-tuple-element.186), channel_id=1, source_target_pairs={{16,8},{24,0},{17,9},{25,1},{18,10},{26,2},{19,11},{27,3},{20,12},... | collective-permute-start | bytes 3145736 | tf_op jit(solution)/shard_map/attention_back/ppermute | solution.py:66
  558.9 15.1 %collective-permute-start.35 = (bf16[256,768]{1,0:T(8,128)(2,1)S(1)}, bf16[256,768]{1,0:T(8,128)(2,1)S(1)}, u32[]{:S(2)}, u32[]{:S(2)}) collective-permute-start(bf16[256,768]{1,0:T(8,128)(2,1)S(1)} %slice.136), channel_id=1, source_target_pairs={{0,8},{8,0},{16,24},{24,16},{1,9},{9,1},{17,25},{25,17},{2,10},{10... | collective-permute-start | bytes 1179656 | tf_op jit(solution)/shard_map/weight_grads/ppermute | solution.py:66
  559.3 15.6 %collective-permute-start.36 = (bf16[256,768]{1,0:T(8,128)(2,1)S(1)}, bf16[256,768]{1,0:T(8,128)(2,1)S(1)}, u32[]{:S(2)}, u32[]{:S(2)}) collective-permute-start(bf16[256,768]{1,0:T(8,128)(2,1)S(1)} %slice.137), channel_id=1, source_target_pairs={{0,16},{8,24},{16,0},{24,8},{1,17},{9,25},{17,1},{25,9},{2,18},{10... | collective-permute-start | bytes 1179656 | tf_op jit(solution)/shard_map/weight_grads/ppermute | solution.py:66
  575.2 13.3 %collective-permute-start.40 = (bf16[64,2048]{1,0:T(8,128)(2,1)S(1)}, bf16[64,2048]{1,0:T(8,128)(2,1)S(1)}, u32[]{:S(2)}, u32[]{:S(2)}) collective-permute-start(bf16[64,2048]{1,0:T(8,128)(2,1)S(1)} %copy-done.61), channel_id=1, source_target_pairs={{0,16},{8,24},{16,0},{24,8},{1,17},{9,25},{17,1},{25,9},{2,18},{10... | collective-permute-start | bytes 786440 | tf_op jit(solution)/shard_map/weight_grads/ppermute | solution.py:66
  576.4 12.1 %collective-permute-start.39 = (bf16[64,2048]{1,0:T(8,128)(2,1)S(1)}, bf16[64,2048]{1,0:T(8,128)(2,1)S(1)}, u32[]{:S(2)}, u32[]{:S(2)}) collective-permute-start(bf16[64,2048]{1,0:T(8,128)(2,1)S(1)} %convolution_convert_fusion.10), channel_id=1, source_target_pairs={{0,8},{8,0},{16,24},{24,16},{1,9},{9,1},{17,25},{25,17},{2,10},{10... | collective-permute-start | bytes 786440 | tf_op jit(solution)/shard_map/weight_grads/ppermute | solution.py:66
  577.6 19.3 %collective-permute-start.37 = (bf16[256,768]{1,0:T(8,128)(2,1)S(1)}, bf16[256,768]{1,0:T(8,128)(2,1)S(1)}, u32[]{:S(2)}, u32[]{:S(2)}) collective-permute-start(bf16[256,768]{1,0:T(8,128)(2,1)S(1)} %add_convert_fusion.7), channel_id=1, source_target_pairs={{0,16},{8,24},{16,0},{24,8},{1,17},{9,25},{17,1},{25,9},{2,18},{10... | collective-permute-start | bytes 1179656 | tf_op jit(solution)/shard_map/weight_grads/ppermute | solution.py:66
  578.1 18.8 %collective-permute-start.38 = (bf16[256,768]{1,0:T(8,128)(2,1)S(1)}, bf16[256,768]{1,0:T(8,128)(2,1)S(1)}, u32[]{:S(2)}, u32[]{:S(2)}) collective-permute-start(bf16[256,768]{1,0:T(8,128)(2,1)S(1)} %add_convert_fusion.6), channel_id=1, source_target_pairs={{0,8},{8,0},{16,24},{24,16},{1,9},{9,1},{17,25},{25,17},{2,10},{10... | collective-permute-start | bytes 1179656 | tf_op jit(solution)/shard_map/weight_grads/ppermute | solution.py:66
  598.1 12.8 %collective-permute-start.43 = (bf16[128,2048]{1,0:T(8,128)(2,1)}, bf16[128,2048]{1,0:T(8,128)(2,1)}, u32[]{:S(2)}, u32[]{:S(2)}) collective-permute-start(bf16[128,2048]{1,0:T(8,128)(2,1)} %add_convert_fusion.5), channel_id=1, source_target_pairs={{0,16},{8,24},{16,0},{24,8},{1,17},{9,25},{17,1},{25,9},{2,18},{10... | collective-permute-start | bytes 1572872 | tf_op jit(solution)/shard_map/weight_grads/ppermute | solution.py:66
  599.7 13.0 %collective-permute-start.44 = (bf16[128,2048]{1,0:T(8,128)(2,1)}, bf16[128,2048]{1,0:T(8,128)(2,1)}, u32[]{:S(2)}, u32[]{:S(2)}) collective-permute-start(bf16[128,2048]{1,0:T(8,128)(2,1)} %add_convert_fusion.4), channel_id=1, source_target_pairs={{0,8},{8,0},{16,24},{24,16},{1,9},{9,1},{17,25},{25,17},{2,10},{10... | collective-permute-start | bytes 1572872 | tf_op jit(solution)/shard_map/weight_grads/ppermute | solution.py:66
  600.0 34.1 %all-to-all-start.4 = ((bf16[8,64,768]{2,1,0:T(8,128)(2,1)}), bf16[8,64,768]{2,1,0:T(8,128)(2,1)S(1)}, u32[]{:S(2)}, u32[]{:S(2)}) async-start(bf16[8,64,768]{2,1,0:T(8,128)(2,1)} %bitcast.32), calls=%async_computation.7 | async-start | bytes 1572864 | tf_op jit(solution)/shard_map/weight_grads/all_to_all | solution.py:713
  604.4 29.6 %collective-permute-start.42 = (bf16[64,2048]{1,0:T(8,128)(2,1)S(1)}, bf16[64,2048]{1,0:T(8,128)(2,1)S(1)}, u32[]{:S(2)}, u32[]{:S(2)}) collective-permute-start(bf16[64,2048]{1,0:T(8,128)(2,1)S(1)} %convert_add_fusion.4), channel_id=1, source_target_pairs={{0,0},{1,4},{2,8},{3,12},{4,16},{5,20},{6,24},{7,28},{8,1},{9,5},{... | collective-permute-start | bytes 786440 | tf_op jit(solution)/shard_map/weight_grads/ppermute | solution.py:789
  (75 other events, 483.0 us)
Sparse Core Ops, SparseCore 0:
  36.9 47.1 all-gather.4
  86.4 81.4 all-gather.6
  203.4 48.7 reduce-scatter.4
  257.7 49.2 all-gather.8
  337.6 47.8 reduce-scatter.6
  391.6 48.0 all-gather.10
  442.4 65.9 reduce-scatter.8
  551.3 46.2 reduce-scatter.10
